TPU v7x, 128 devices: a whole 4x4x4 slice. The times are simulated.
128 devices in a mesh: front: 4 (over y), hss: 32 (over x, z, core).
Axes of the slice: x: 4, y: 4, z: 4, core: 2. Of those that a mesh axis runs over, the one named last changes fastest.
Arguments:
- front_rows: bfloat16 [4, 19456, 19456], P('front', 'hss'), may hold values from -0.0390625 to 0.0390625
- samples: bfloat16 [4, 19456, 256], P('front', 'hss'), may hold values from -6 to 6
- child_rows: bfloat16 [4, 16384, 256], P('front', 'hss'), may hold values from -6 to 6
- child_owner: int32 [4, 16384, 1], P('front'), may hold values from 0 to 31; in each aligned block of 512 rows (0 to 511, 512 to 1023, ..., all dimensions but the last counted through in order) at most 64 rows name the same one
- child_local: int32 [4, 16384], P('front'), may hold values from 0 to 607
- leaf_skeleton: int32 [4, 32, 128], P('front'), may hold values from 0 to 607, as said below
- merge_select: int32 [4, 31, 128], P('front'), may hold values from 0 to 255, as said below
Outputs:
- parent_sample: bfloat16 [4, 19456, 256], P('front', 'hss')
- pair_sample: float32 [4, 4096, 256], P('front', 'hss')
- root_sample: float32 [4, 128, 256], P('front')
Inputs may be any that keep to these rules, and one draw needn't show every extreme that they name: `child_owner`: in the rows of one device (aligned blocks of 512 rows) no owner is named more than 64 times, a bound that some block reaches. `leaf_skeleton`: the 128 entries of one leaf are distinct. `merge_select`: the 128 entries of one node are distinct.
All inputs are finite; a program needn't handle non-finite values.
Results may differ from a plain program's by a relative error of at most 0.0013.
Values may be sent and summed in bfloat16 or wider, within the bound.
No kernel may reach another device: no remote copies, remote signals or barrier semaphores. Data moves between devices by JAX's collectives and lax.ppermute only.
A program may use at most 192 MiB of HBM per device.

v0:
```python
import jax
import jax.numpy as jnp
from jax import lax
from jax.sharding import PartitionSpec as P

ROWS = 608
SAMPLES = 256
RANK = 128
CHILD = 512
CAP = 64
BF = jnp.bfloat16
F32 = jnp.float32


def pick_index(table, position):
    return lax.dynamic_index_in_dim(table, position, 0, keepdims=False)


def iota(n):
    return jnp.arange(n, dtype=jnp.int32)


def shifted(x, axis, move):
    return lax.ppermute(x, axis, [(i, move(i)) for i in range(lax.axis_size(axis))])


def fates(selections, leaf_total, depth):
    survived = jnp.zeros((1, RANK), jnp.int32)
    root_slot = iota(RANK)[None] + 1
    for height in reversed(range(depth)):
        offset = leaf_total - (leaf_total >> height)
        node_total = leaf_total >> (height + 1)
        chosen = selections[offset : offset + node_total]
        hit = chosen[:, :, None] == iota(2 * RANK)[None, None, :]
        survived = jnp.sum(jnp.where(hit, survived[:, :, None] + 1, 0), axis=1).reshape(-1, RANK)
        root_slot = jnp.sum(jnp.where(hit, root_slot[:, :, None], 0), axis=1).reshape(-1, RANK)
    return survived, root_slot


def total_over_hss(x, side):
    core = lambda i: i ^ 1
    along_z = lambda s: lambda i: i // 8 * 8 + (i // 2 + s) % 4 * 2 + i % 2
    along_x = lambda s: lambda i: (i + 8 * s) % 32
    half = x.shape[0] // 2
    low, high = x[:half], x[half:]
    mine = jnp.where(side == 0, low, high)
    yours = jnp.where(side == 0, high, low)
    mine = mine + shifted(yours, "hss", core)
    for along in (along_z, along_x):
        mine = mine + sum([shifted(mine, "hss", along(s)) for s in (2, 1, 3)])
    other = shifted(mine, "hss", core)
    return jnp.concatenate([jnp.where(side == 0, mine, other), jnp.where(side == 0, other, mine)], axis=0)


def body(front_rows, samples, child_rows, child_owner, child_local, leaf_skeleton, merge_select):
    leaf_total = lax.axis_size("hss")
    depth = leaf_total.bit_length() - 1
    myself = lax.axis_index("hss")
    side = jnp.bitwise_and(myself, 1)
    front = front_rows[0]
    gathered = lax.all_gather(samples[0], "hss", axis=0, tiled=True)

    owners = child_owner[0, :, 0].reshape(leaf_total, CHILD)
    targets = child_local[0].reshape(leaf_total, CHILD)
    mine = pick_index(owners, myself)
    earlier = iota(CHILD)[:, None] < iota(CHILD)[None, :]
    my_slots = jnp.sum(((mine[:, None] == mine[None, :]) & earlier).astype(jnp.int32), axis=0)
    destination = mine * CAP + my_slots
    send_select = (iota(leaf_total * CAP)[:, None] == destination[None, :]).astype(BF)
    outgoing = jnp.dot(send_select, child_rows[0], preferred_element_type=F32).astype(BF)
    incoming = lax.all_to_all(
        outgoing.reshape(leaf_total, CAP, SAMPLES), "hss", split_axis=0, concat_axis=0, tiled=True
    ).reshape(leaf_total * CAP, SAMPLES)

    hits = owners == myself
    order = jnp.dot(hits.astype(BF), earlier.astype(BF), preferred_element_type=F32).astype(jnp.int32)
    placed = jnp.where(hits, order, CAP)
    slot_hits = placed[:, :, None] == iota(CAP)[None, None, :]
    slot_rows = (jnp.sum(jnp.where(slot_hits, targets[:, :, None] + 1, 0), axis=1) - 1).reshape(-1)
    selector = (iota(ROWS)[:, None] == slot_rows[None, :]).astype(BF)

    skeletons = leaf_skeleton[0]
    survived, root_slot = fates(merge_select[0], leaf_total, depth)
    my_skeleton = pick_index(skeletons, myself)
    my_root_slot = pick_index(root_slot, myself)
    root_rows = jnp.sum(jnp.where(my_root_slot[:, None] == iota(RANK)[None, :] + 1, my_skeleton[:, None] + 1, 0), axis=0) - 1
    pair_choice = pick_index(merge_select[0], jnp.right_shift(myself, 1)) - side * RANK
    pair_rows = jnp.sum(jnp.where(iota(RANK)[:, None] == pair_choice[None, :], my_skeleton[:, None] + 1, 0), axis=0) - 1
    root_pick = (root_rows[:, None] == iota(ROWS)[None, :]).astype(BF)
    pair_pick = (pair_rows[:, None] == iota(ROWS)[None, :]).astype(BF)

    marks = jnp.sum(
        jnp.where(skeletons[:, :, None] == iota(ROWS)[None, None, :], survived[:, :, None] + 1, 0), axis=1
    )
    apart = jnp.bitwise_xor(iota(leaf_total), myself)
    level = sum([(apart >= (2 << h)).astype(jnp.int32) for h in range(depth - 1)])
    root_keep = (apart != 0)[:, None] & (marks <= level[:, None])
    pair_keep = (apart != 0)[:, None] & ((apart != 1)[:, None] | (marks == 0))
    root_front = jnp.dot(root_pick, front, preferred_element_type=F32).astype(BF)
    root_front = jnp.where(root_keep.reshape(1, -1), root_front, 0)
    pair_front = jnp.dot(pair_pick, front, preferred_element_type=F32).astype(BF)
    pair_front = jnp.where(pair_keep.reshape(1, -1), pair_front, 0)
    root_arrivals = jnp.dot(
        jnp.dot(root_pick, selector, preferred_element_type=F32).astype(BF), incoming, preferred_element_type=F32
    )
    pair_arrivals = jnp.dot(
        jnp.dot(pair_pick, selector, preferred_element_type=F32).astype(BF), incoming, preferred_element_type=F32
    )
    arrivals = jnp.dot(selector, incoming, preferred_element_type=F32)
    front, gathered, root_front, pair_front, root_arrivals, pair_arrivals, arrivals = lax.optimization_barrier(
        (front, gathered, root_front, pair_front, root_arrivals, pair_arrivals, arrivals)
    )

    root = jnp.dot(root_front, gathered, preferred_element_type=F32) + root_arrivals
    root, gathered = lax.optimization_barrier((root, gathered))
    root = total_over_hss(root, side)
    parent = (jnp.dot(front, gathered, preferred_element_type=F32) + arrivals).astype(BF)
    pair = jnp.dot(pair_front, gathered, preferred_element_type=F32) + pair_arrivals
    pair = pair + shifted(pair, "hss", lambda i: i ^ 1)
    return (parent[None], pair[None], root[None])


def solution(mesh):
    in_specs = (
        P("front", "hss", None),
        P("front", "hss", None),
        P("front", "hss", None),
        P("front", None, None),
        P("front", None),
        P("front", None, None),
        P("front", None, None),
    )
    out_specs = (P("front", "hss", None), P("front", "hss", None), P("front", None, None))
    return jax.shard_map(body, mesh=mesh, in_specs=in_specs, out_specs=out_specs, check_vma=False)
```

profile of v0, /device:TPU:1, one launch (start us, length us, event | category | flops | bytes accessed | tf_op | source)
XLA Modules:
  0.0 118.5 jit_solution(18386641065360428931)
XLA Ops:
  7.2 0.0 copy-start
  7.2 0.0 copy-start.3
  7.2 0.0 slice-start.2
  7.2 0.0 slice-start.3
  7.2 0.0 slice-start.4
  7.2 0.0 slice-start.5
  7.2 0.0 copy-start.4
  7.2 0.0 copy-start.2
  7.3 0.0 all-gather.3.cloned.1.call-start
  7.3 0.7 all-gather.3.cloned.1.call-update
  8.0 0.5 broadcast.240
  8.5 1.6 %reduce.9 = s32[16384]{0:T(1024)S(1)} reduce(s32[1,16384,1]{1,2,0:T(1,128)} %param.10, s32[]{:T(128)} %broadcast.240), dimensions={0,2}, to_apply=%param.10.reduce_sub_computation.3 | reduce | bytes 131076 | tf_op args[3]
  10.2 0.2 convert_reduce_fusion
  10.4 0.0 copy-done
  10.4 1.8 %fusion.6 = bf16[2048,256]{1,0:T(8,128)(2,1)} fusion(s32[512]{0:T(512)S(1)} %bitcast.63, bf16[1,512,256]{2,1,0:T(8,128)(2,1)S(1)} %copy-done), kind=kOutput, calls=%fused_computation.14 | convolution fusion | flops 538443776 | bytes 1312768 | tf_op jit(solution)/shard_map/dot_general | solution.py:70
  12.2 9.4 %all-to-all-start = ((bf16[32,64,256]{2,1,0:T(8,128)(2,1)}), bf16[32,64,256]{2,1,0:T(8,128)(2,1)S(1)}, u32[]{:S(2)}, u32[]{:S(2)}) async-start(bf16[32,64,256]{2,1,0:T(8,128)(2,1)} %bitcast.17), calls=%async_computation | async-start | bytes 2097152 | tf_op jit(solution)/shard_map/all_to_all | solution.py:71
  21.7 0.0 copy-done.3
  21.7 0.1 select_reduce_fusion.10
  21.8 0.2 select_reduce_fusion.8
  22.1 0.3 select_reduce_fusion.6
  22.4 0.0 slice-done.4
  22.4 0.6 select_reduce_fusion.4
  23.0 0.0 slice-done.5
  23.0 1.3 %select_reduce_fusion.2 = (s32[16,256]{1,0:T(8,128)S(1)}, s32[16,256]{1,0:T(8,128)S(1)}) fusion(s32[16,128]{1,0:T(8,128)S(1)} %broadcast_in_dim.225, s32[16,128]{1,0:T(8,128)S(1)} %bitcast.58, s32[16,128]{1,0:T(8,128)S(1)} %add.208), kind=kLoop, calls=%fused_computation.21 | loop fusion | flops 2613248 | bytes 57344 | tf_op jit(solution)/shard_map/reduce_sum | solution.py:36
  24.5 2.8 %select_reduce_fusion = s32[32,608]{1,0:T(8,128)S(1)} fusion(s32[32,128]{1,0:T(8,128)S(1)} %add.211, s32[32,128]{1,0:T(8,128)S(1)} %bitcast.60), kind=kLoop, calls=%fused_computation.4 | loop fusion | flops 7451648 | bytes 110592 | tf_op jit(solution)/shard_map/reduce_sum | solution.py:92
  27.2 0.1 or_and_fusion
  27.3 0.1 and.39
  27.5 0.1 and.37
  27.6 0.2 add_reduce_fusion
  27.8 0.2 fusion.17
  28.0 0.6 select_reduce_fusion.1
  28.7 0.1 sub.31
  28.7 0.1 select_reduce_fusion.12
  28.9 14.1 %fusion = bf16[128,19456]{1,0:T(8,128)(2,1)} fusion(pred[19456]{0:T(1024)(128)(4,1)S(1)} %and.37, s32[128]{0:T(128)S(1)} %get-tuple-element.42, bf16[1,608,19456]{2,1,0:T(8,128)(2,1)} %param.7), kind=kOutput, calls=%fused_computation.2 | convolution fusion | flops 3033346048 | bytes 28659200 | tf_op jit(solution)/shard_map/dot_general | solution.py:99
  43.0 14.1 %fusion.1 = bf16[128,19456]{1,0:T(8,128)(2,1)} fusion(pred[19456]{0:T(1024)(128)(4,1)S(1)} %and.39, s32[128]{0:T(128)S(1)} %get-tuple-element.41, bf16[1,608,19456]{2,1,0:T(8,128)(2,1)} %param.7), kind=kOutput, calls=%fused_computation.3 | convolution fusion | flops 3033346048 | bytes 28659200 | tf_op jit(solution)/shard_map/dot_general | solution.py:101
  57.1 0.0 all-to-all-done
  57.1 1.5 %fusion.13 = f32[128,256]{1,0:T(8,128)S(1)} fusion(bf16[2048,256]{1,0:T(8,128)(2,1)S(1)} %bitcast.52, s32[2048]{0:T(1024)S(1)} %sub.31, s32[128]{0:T(128)S(1)} %get-tuple-element.41), kind=kOutput, calls=%fused_computation.25 | convolution fusion | flops 454569984 | bytes 1188352 | tf_op jit(solution)/shard_map/dot_general | solution.py:106
  58.7 1.3 %fusion.14 = f32[128,256]{1,0:T(8,128)S(1)} fusion(bf16[2048,256]{1,0:T(8,128)(2,1)S(1)} %bitcast.53, s32[2048]{0:T(1024)S(1)} %sub.31, s32[128]{0:T(128)S(1)} %get-tuple-element.42), kind=kOutput, calls=%fused_computation.26 | convolution fusion | flops 454569984 | bytes 1188352 | tf_op jit(solution)/shard_map/dot_general | solution.py:103
  60.0 0.0 slice-start
  60.0 0.9 fusion.2
  60.9 15.8 %all-gather.3.cloned.1.call-done = bf16[1,19456,256]{2,1,0:T(8,128)(2,1)} async-done(((bf16[1,608,256]{2,1,0:T(8,128)(2,1)}), bf16[1,19456,256]{2,1,0:T(8,128)(2,1)}) %all-gather.3.cloned.1.call-update) | async-done | bytes 9961488 | tf_op jit(solution)/shard_map/all_gather | solution.py:61
  76.7 6.9 %convolution_add_fusion.2 = f32[128,256]{1,0:T(8,128)S(1)} fusion(f32[128,256]{1,0:T(8,128)S(1)} %fusion.14, bf16[128,19456]{1,0:T(8,128)(2,1)} %fusion, bf16[19456,256]{1,0:T(8,128)(2,1)} %bitcast.47), kind=kOutput, calls=%fused_computation.30 | convolution fusion | flops 1275101184 | bytes 15204352 | tf_op jit(solution)/shard_map/dot_general | solution.py:114
  83.7 0.3 collective-permute-start.1
  84.0 1.0 collective-permute-done.1
  85.0 2.3 %collective-permute-start.4 = (f32[64,256]{1,0:T(8,128)S(1)}, f32[64,256]{1,0:T(8,128)S(1)}, u32[]{:S(2)}, u32[]{:S(2)}) collective-permute-start(f32[64,256]{1,0:T(8,128)S(1)} %select_add_fusion), channel_id=1, source_target_pairs={{0,6},{1,7},{2,0},{3,1},{4,2},{5,3},{6,4},{7,5},{8,14},{9,15},{10,... | collective-permute-start | bytes 196616 | tf_op jit(solution)/shard_map/ppermute | solution.py:24
  87.3 0.0 collective-permute-start.3
  87.3 1.7 %collective-permute-start.2 = (f32[64,256]{1,0:T(8,128)S(1)}, f32[64,256]{1,0:T(8,128)S(1)}, u32[]{:S(2)}, u32[]{:S(2)}) collective-permute-start(f32[64,256]{1,0:T(8,128)S(1)} %select_add_fusion), channel_id=1, source_target_pairs={{0,4},{1,5},{2,6},{3,7},{4,0},{5,1},{6,2},{7,3},{8,12},{9,13},{10,... | collective-permute-start | bytes 196616 | tf_op jit(solution)/shard_map/ppermute | solution.py:24
  89.0 1.5 %convolution_add_fusion.1 = f32[128,256]{1,0:T(8,128)S(1)} fusion(f32[128,256]{1,0:T(8,128)S(1)} %fusion.13, bf16[128,19456]{1,0:T(8,128)(2,1)S(1)} %bitcast.51, bf16[19456,256]{1,0:T(8,128)(2,1)S(1)} %bitcast.48), kind=kOutput, calls=%fused_computation.29 | convolution fusion | flops 1275101184 | bytes 15204352 | tf_op jit(solution)/shard_map/dot_general | solution.py:118
  90.5 1.2 collective-permute-start
  91.6 0.0 collective-permute-done.4
  91.6 0.8 collective-permute-done.3
  92.4 0.3 collective-permute-done.2
  92.7 1.1 collective-permute-start.7
  93.8 0.5 collective-permute-start.6
  94.3 1.3 %collective-permute-start.5 = (f32[64,256]{1,0:T(8,128)S(1)}, f32[64,256]{1,0:T(8,128)S(1)}, u32[]{:S(2)}, u32[]{:S(2)}) collective-permute-start(f32[64,256]{1,0:T(8,128)S(1)} %add_add_fusion.1), channel_id=1, source_target_pairs={{0,16},{1,17},{2,18},{3,19},{4,20},{5,21},{6,22},{7,23},{8,24},{9,... | collective-permute-start | bytes 196616 | tf_op jit(solution)/shard_map/ppermute | solution.py:24
  95.5 11.8 %fusion.16 = bf16[1,608,256]{2,1,0:T(8,128)(2,1)} fusion(f32[608,256]{1,0:T(8,128)S(1)} %fusion.2, bf16[608,19456]{1,0:T(8,128)(2,1)} %bitcast.46, bf16[19456,256]{1,0:T(8,128)(2,1)S(1)} %bitcast.49), kind=kOutput, calls=%fused_computation.28 | convolution fusion | flops 6056886272 | bytes 34553856 | tf_op jit(solution)/shard_map/dot_general | solution.py:117
  107.3 0.0 collective-permute-done.7
  107.3 0.0 collective-permute-done.6
  107.3 0.0 collective-permute-done.5
  107.3 2.8 %collective-permute-start.8 = (f32[64,256]{1,0:T(8,128)S(1)}, f32[64,256]{1,0:T(8,128)S(1)}, u32[]{:S(2)}, u32[]{:S(2)}) collective-permute-start(f32[64,256]{1,0:T(8,128)S(1)} %add_add_fusion), channel_id=1, source_target_pairs={{0,1},{1,0},{2,3},{3,2},{4,5},{5,4},{6,7},{7,6},{8,9},{9,8},{10,11... | collective-permute-start | bytes 196616 | tf_op jit(solution)/shard_map/ppermute | solution.py:24
  110.1 0.0 collective-permute-done
  110.1 0.7 add_bitcast_fusion
  110.8 0.2 collective-permute-done.8
  111.0 0.7 maximum_bitcast_fusion
  (40 shorter events, 0.3 us)
Async XLA Ops:
  7.2 3.2 %copy-start = (bf16[1,512,256]{2,1,0:T(8,128)(2,1)S(1)}, bf16[1,512,256]{2,1,0:T(8,128)(2,1)}, u32[]{:S(2)}) copy-start(bf16[1,512,256]{2,1,0:T(8,128)(2,1)} %param.9) | copy-start | bytes 786436
  7.2 14.5 %copy-start.3 = (s32[1,31,128]{2,0,1:T(1,128)S(1)}, s32[1,31,128]{2,0,1:T(1,128)}, u32[]{:S(2)}) copy-start(s32[1,31,128]{2,0,1:T(1,128)} %param.13) | copy-start | bytes 47620
  7.2 14.6 %slice-start.2 = ((s32[1,31,128]{2,0,1:T(1,128)}), s32[1,2,128]{2,0,1:T(1,128)S(1)}, s32[]{:S(2)}) async-start(s32[1,31,128]{2,0,1:T(1,128)} %param.13), calls=%async_computation.4 | async-start | bytes 2048 | tf_op jit(solution)/shard_map/slice | solution.py:33
  7.2 14.8 %slice-start.3 = ((s32[1,31,128]{2,0,1:T(1,128)}), s32[1,4,128]{2,0,1:T(1,128)S(1)}, s32[]{:S(2)}) async-start(s32[1,31,128]{2,0,1:T(1,128)} %param.13), calls=%async_computation.5 | async-start | bytes 4096 | tf_op jit(solution)/shard_map/slice | solution.py:33
  7.2 15.2 %slice-start.4 = ((s32[1,31,128]{2,0,1:T(1,128)}), s32[1,8,128]{2,0,1:T(1,128)S(1)}, s32[]{:S(2)}) async-start(s32[1,31,128]{2,0,1:T(1,128)} %param.13), calls=%async_computation.6 | async-start | bytes 8192 | tf_op jit(solution)/shard_map/slice | solution.py:33
  7.2 15.8 %slice-start.5 = ((s32[1,31,128]{2,0,1:T(1,128)}), s32[1,16,128]{2,0,1:T(1,128)S(1)}, s32[]{:S(2)}) async-start(s32[1,31,128]{2,0,1:T(1,128)} %param.13), calls=%async_computation.7 | async-start | bytes 16384 | tf_op jit(solution)/shard_map/slice | solution.py:33
  7.2 17.2 %copy-start.4 = (s32[1,32,128]{2,1,0:T(8,128)S(1)}, s32[1,32,128]{2,1,0:T(8,128)}, u32[]{:S(2)}) copy-start(s32[1,32,128]{2,1,0:T(8,128)} %param.12) | copy-start | bytes 49156
  7.2 20.4 %copy-start.2 = (s32[1,16384]{1,0:T(1,128)S(1)}, s32[1,16384]{1,0:T(1,128)}, u32[]{:S(2)}) copy-start(s32[1,16384]{1,0:T(1,128)} %param.11) | copy-start | bytes 196612
  7.3 69.5 %all-gather.3.cloned.1.call-start = ((), (), s32[]{:S(2)}) async-start(), calls=%async_computation.1 | async-start | bytes 10272768 | tf_op jit(solution)/shard_map/all_gather | solution.py:61
  12.2 44.9 %all-to-all-start = ((bf16[32,64,256]{2,1,0:T(8,128)(2,1)}), bf16[32,64,256]{2,1,0:T(8,128)(2,1)S(1)}, u32[]{:S(2)}, u32[]{:S(2)}) async-start(bf16[32,64,256]{2,1,0:T(8,128)(2,1)} %bitcast.17), calls=%async_computation | async-start | bytes 2097152 | tf_op jit(solution)/shard_map/all_to_all | solution.py:71
  60.0 29.0 %slice-start = ((s8[4980736]{0:T(1024)(128)(4,1)}), s8[786432]{0:T(1024)(128)(4,1)S(1)}, s32[]{:S(2)}) async-start(s8[4980736]{0:T(1024)(128)(4,1)} %bitcast.50), calls=%async_computation.2 | async-start | bytes 1572864
  76.7 12.3 %copy-start.1 = (bf16[1,19456,256]{2,1,0:T(8,128)(2,1)S(1)}, bf16[1,19456,256]{2,1,0:T(8,128)(2,1)}, u32[]{:S(2)}) copy-start(bf16[1,19456,256]{2,1,0:T(8,128)(2,1)} %all-gather.3.cloned.1.call-done) | copy-start | bytes 29884420
  76.7 12.3 %slice-start.1 = ((s8[4980736]{0:T(1024)(128)(4,1)}), s8[4194304]{0:T(1024)(128)(4,1)S(1)}, s32[]{:S(2)}) async-start(s8[4980736]{0:T(1024)(128)(4,1)} %bitcast.50), calls=%async_computation.3 | async-start | bytes 8388608
  83.7 1.3 %collective-permute-start.1 = (f32[64,256]{1,0:T(8,128)S(1)}, f32[64,256]{1,0:T(8,128)S(1)}, u32[]{:S(2)}, u32[]{:S(2)}) collective-permute-start(f32[64,256]{1,0:T(8,128)S(1)} %slice_select_fusion), channel_id=1, source_target_pairs={{0,1},{1,0},{2,3},{3,2},{4,5},{5,4},{6,7},{7,6},{8,9},{9,8},{10,11... | collective-permute-start | bytes 196616 | tf_op jit(solution)/shard_map/ppermute | solution.py:24
  85.0 6.6 %collective-permute-start.4 = (f32[64,256]{1,0:T(8,128)S(1)}, f32[64,256]{1,0:T(8,128)S(1)}, u32[]{:S(2)}, u32[]{:S(2)}) collective-permute-start(f32[64,256]{1,0:T(8,128)S(1)} %select_add_fusion), channel_id=1, source_target_pairs={{0,6},{1,7},{2,0},{3,1},{4,2},{5,3},{6,4},{7,5},{8,14},{9,15},{10,... | collective-permute-start | bytes 196616 | tf_op jit(solution)/shard_map/ppermute | solution.py:24
  87.3 5.1 %collective-permute-start.3 = (f32[64,256]{1,0:T(8,128)S(1)}, f32[64,256]{1,0:T(8,128)S(1)}, u32[]{:S(2)}, u32[]{:S(2)}) collective-permute-start(f32[64,256]{1,0:T(8,128)S(1)} %select_add_fusion), channel_id=1, source_target_pairs={{0,2},{1,3},{2,4},{3,5},{4,6},{5,7},{6,0},{7,1},{8,10},{9,11},{10,... | collective-permute-start | bytes 196616 | tf_op jit(solution)/shard_map/ppermute | solution.py:24
  87.3 5.4 %collective-permute-start.2 = (f32[64,256]{1,0:T(8,128)S(1)}, f32[64,256]{1,0:T(8,128)S(1)}, u32[]{:S(2)}, u32[]{:S(2)}) collective-permute-start(f32[64,256]{1,0:T(8,128)S(1)} %select_add_fusion), channel_id=1, source_target_pairs={{0,4},{1,5},{2,6},{3,7},{4,0},{5,1},{6,2},{7,3},{8,12},{9,13},{10,... | collective-permute-start | bytes 196616 | tf_op jit(solution)/shard_map/ppermute | solution.py:24
  90.5 19.7 %collective-permute-start = (f32[128,256]{1,0:T(8,128)S(1)}, f32[128,256]{1,0:T(8,128)S(1)}, u32[]{:S(2)}, u32[]{:S(2)}) collective-permute-start(f32[128,256]{1,0:T(8,128)S(1)} %convolution_add_fusion.1), channel_id=1, source_target_pairs={{0,1},{1,0},{2,3},{3,2},{4,5},{5,4},{6,7},{7,6},{8,9},{9,8},{10,11... | collective-permute-start | bytes 393224 | tf_op jit(solution)/shard_map/ppermute | solution.py:24
  92.7 14.6 %collective-permute-start.7 = (f32[64,256]{1,0:T(8,128)S(1)}, f32[64,256]{1,0:T(8,128)S(1)}, u32[]{:S(2)}, u32[]{:S(2)}) collective-permute-start(f32[64,256]{1,0:T(8,128)S(1)} %add_add_fusion.1), channel_id=1, source_target_pairs={{0,24},{1,25},{2,26},{3,27},{4,28},{5,29},{6,30},{7,31},{8,0},{9,1... | collective-permute-start | bytes 196616 | tf_op jit(solution)/shard_map/ppermute | solution.py:24
  93.8 13.5 %collective-permute-start.6 = (f32[64,256]{1,0:T(8,128)S(1)}, f32[64,256]{1,0:T(8,128)S(1)}, u32[]{:S(2)}, u32[]{:S(2)}) collective-permute-start(f32[64,256]{1,0:T(8,128)S(1)} %add_add_fusion.1), channel_id=1, source_target_pairs={{0,8},{1,9},{2,10},{3,11},{4,12},{5,13},{6,14},{7,15},{8,16},{9,17... | collective-permute-start | bytes 196616 | tf_op jit(solution)/shard_map/ppermute | solution.py:24
  94.3 13.0 %collective-permute-start.5 = (f32[64,256]{1,0:T(8,128)S(1)}, f32[64,256]{1,0:T(8,128)S(1)}, u32[]{:S(2)}, u32[]{:S(2)}) collective-permute-start(f32[64,256]{1,0:T(8,128)S(1)} %add_add_fusion.1), channel_id=1, source_target_pairs={{0,16},{1,17},{2,18},{3,19},{4,20},{5,21},{6,22},{7,23},{8,24},{9,... | collective-permute-start | bytes 196616 | tf_op jit(solution)/shard_map/ppermute | solution.py:24
  107.3 3.7 %collective-permute-start.8 = (f32[64,256]{1,0:T(8,128)S(1)}, f32[64,256]{1,0:T(8,128)S(1)}, u32[]{:S(2)}, u32[]{:S(2)}) collective-permute-start(f32[64,256]{1,0:T(8,128)S(1)} %add_add_fusion), channel_id=1, source_target_pairs={{0,1},{1,0},{2,3},{3,2},{4,5},{5,4},{6,7},{7,6},{8,9},{9,8},{10,11... | collective-permute-start | bytes 196616 | tf_op jit(solution)/shard_map/ppermute | solution.py:24
Sparse Core Ops, SparseCore 0:
  10.3 66.3 all-gather.2
where the time goes:
time: 119 us
  matrix products  54.1 us (45%)
  starting transfers between devices  20.5 us (17%)
  waiting for transfers between devices  18.8 us (16%)
  between operations  14.5 us (12%)
  other arithmetic  9.62 us (8%)
    all_gather x1, waiting for transfers between devices, body(): gathered = lax.all_gather(samples[0], 'hss', axis=0, tiled=True)  15.8 us
    dot_general x1, matrix products, body(): jnp.dot(root_pick, front, preferred_element_type=F32).astype(BF)  14.1 us
    dot_general x1, matrix products, body(): jnp.dot(pair_pick, front, preferred_element_type=F32).astype(BF)  14.1 us
    dot_general x1, matrix products, body(): jnp.dot(front, gathered, preferred_element_type=F32) + arrivals  11.8 us
    ppermute x9, starting transfers between devices, shifted(): lax.ppermute(x, axis, [(i, move(i)) for i in range(lax.axis_size(axis))])  11 us
    all_to_all x1, starting transfers between devices, body(): lax.all_to_all(outgoing.reshape(leaf_total, CAP, SAMPLES), 'hss', split_a...  9.43 us
    dot_general x1, matrix products, body(): jnp.dot(root_front, gathered, preferred_element_type=F32) + root_arrivals  6.92 us
    reduce_sum x1, other arithmetic, body(): jnp.sum(jnp.where(skeletons[:, :, None] == iota(ROWS)[None, None, :], sur...  2.78 us
  transfers between devices with their start and end apart: 11, of which 5 were waited for; matrix products, arithmetic and copies ran while one was open for 48% of the time, Pallas kernels for 0%

commit v1 on v0

v1 whole, which is shorter than its diff:
```python
import functools

import jax
import jax.numpy as jnp
from jax import lax
from jax.experimental import pallas as pl
from jax.experimental.pallas import tpu as pltpu
from jax.sharding import PartitionSpec as P

ROWS = 608
SAMPLES = 256
RANK = 128
CHILD = 512
CAP = 64
BF = jnp.bfloat16
F32 = jnp.float32
LANES = 128
SUBLANES = 16
WINDOW = 768
PLACES = (0, 96, 64, 160)
RING = 4
TURNS = (0, 1, 3, 2)
AHEAD = 2
VMEM = 42 << 20


def pick_index(table, position):
    return lax.dynamic_index_in_dim(table, position, 0, keepdims=False)


def iota(n):
    return jnp.arange(n, dtype=jnp.int32)


def shifted(x, move):
    return lax.ppermute(x, "hss", [(i, move(i)) for i in range(lax.axis_size("hss"))])


def cores(i):
    return i ^ 1


def along_z(turn):
    return lambda i: i ^ 2 * TURNS[turn]


def along_x(turn):
    return lambda i: i ^ 8 * TURNS[turn]


def first(turn):
    return lambda i: along_x(turn)(i) if i % 2 else along_z(turn)(i)


def second(turn):
    return lambda i: along_z(turn)(i) if i % 2 else along_x(turn)(i)


def total_over_ring(x, along):
    near, far, opposite = [shifted(x, along(turn)) for turn in (1, 2, 3)]
    return (x + near) + (far + opposite)


def fate_kernel(me_ref, select_ref, skeleton_ref, slots_ref, keep_ref):
    me = me_ref[0]
    row = lax.broadcasted_iota(jnp.int32, (SUBLANES, RANK), 0)
    once = jnp.where(row == 0, 1.0, 0.0)
    carried = [jnp.where(row == 1, lax.broadcasted_iota(jnp.int32, (SUBLANES, RANK), 1) + 1, 0).astype(F32)]
    place = lax.broadcasted_iota(jnp.int32, (2 * RANK, RANK), 0)
    at = select_ref.shape[0]
    while at > 0:
        at -= len(carried)
        below = []
        for node, values in enumerate(carried):
            hit = jnp.where(place == select_ref[at + node : at + node + 1, :], 1.0, 0.0).astype(BF)
            spread = lax.dot_general((values + once).astype(BF), hit, (((1,), (1,)), ((), ())), preferred_element_type=F32)
            below += [spread[:, :RANK], spread[:, RANK:]]
        carried = below
    gone = []
    for leaf, values in enumerate(carried):
        slots_ref[leaf : leaf + 1, :] = values[1:2, :].astype(jnp.int32)
        apart = jnp.bitwise_xor(me, leaf)
        level = sum([jnp.where(apart >= (2 << h), 1, 0) for h in range(4)])
        names = skeleton_ref[leaf : leaf + 1, :]
        gone.append(jnp.where(values[0:1, :].astype(jnp.int32) >= level, names, -WINDOW))
    gone = jnp.concatenate(gone + [gone[0]] * (RANK - len(gone)), axis=0).T
    lane = lax.broadcasted_iota(jnp.int32, (RANK, WINDOW), 1)
    for leaf in range(len(carried)):
        named = jnp.where(lane - PLACES[leaf % 4] == gone[:, leaf : leaf + 1], 1.0, 0.0)
        keep = 1.0 - jnp.max(named, axis=0, keepdims=True)
        keep_ref[leaf : leaf + 1, :] = keep * jnp.where(me == leaf, 0.0, 1.0)


def fates(me, selections, skeletons):
    leaves = skeletons.shape[0]
    return pl.pallas_call(
        fate_kernel,
        in_specs=[pl.BlockSpec(memory_space=pltpu.SMEM), pl.BlockSpec(), pl.BlockSpec()],
        out_shape=[jax.ShapeDtypeStruct((leaves, RANK), jnp.int32), jax.ShapeDtypeStruct((leaves, WINDOW), F32)],
        compiler_params=pltpu.CompilerParams(vmem_limit_bytes=VMEM),
        cost_estimate=pl.CostEstimate(flops=leaves << 20, bytes_accessed=leaves << 12, transcendentals=0),
    )(me[None], selections, skeletons)


def window_tile(leaf):
    return 19 * leaf // 4 - jnp.where(leaf % 4 == 3, 1, 0)


def window_place(leaf):
    kind = leaf % 4
    return jnp.where(kind == 0, PLACES[0], jnp.where(kind == 1, PLACES[1], jnp.where(kind == 2, PLACES[2], PLACES[3])))


def leaf_of(me, whose, step, j):
    by_first = 2 * TURNS[j] + 8 * TURNS[step]
    by_second = 8 * TURNS[j] + 2 * TURNS[step]
    side = jnp.bitwise_and(me, 1)
    moved = jnp.where(side == whose, by_first, by_second)
    return jnp.bitwise_xor(jnp.bitwise_xor(me, whose), moved)


def product_kernel(units, plain, masked, added, me_ref, front, keep_ref, *refs):
    blocks, refs = refs[: units[-1][0] + 1], refs[units[-1][0] + 1 :]
    out_ref, left_buf, right_buf, sems = refs[-4:]
    leaves = [leaf_of(me_ref[0], *unit[2:]) for unit in units]

    def copies(u):
        block, row = units[u][:2]
        slot, half = u // 2, u % 2
        columns = pl.ds(pl.multiple_of(window_tile(leaves[u]) * LANES, LANES), WINDOW)
        rows = pl.ds(pl.multiple_of(half * WINDOW + window_place(leaves[u]), 32), ROWS)
        return (
            pltpu.make_async_copy(
                front.at[:, columns], left_buf.at[slot, :, pl.ds(half * WINDOW, WINDOW)], sems.at[u, 0]
            ),
            pltpu.make_async_copy(blocks[block].at[row], right_buf.at[slot, rows, :], sems.at[u, 1]),
        )

    def begin(slot):
        for u in (2 * slot, 2 * slot + 1):
            edge = (u % 2) * WINDOW
            right_buf[slot, edge : edge + PLACES[-1], :] = jnp.zeros((PLACES[-1], SAMPLES), BF)
            right_buf[slot, edge + ROWS : edge + WINDOW, :] = jnp.zeros((WINDOW - ROWS, SAMPLES), BF)
            for copy in copies(u):
                copy.start()

    slots = len(units) // 2
    for slot in range(min(AHEAD, slots)):
        begin(slot)
    for slot in range(slots):
        for u in (2 * slot, 2 * slot + 1):
            for copy in copies(u):
                copy.wait()
        if slot + AHEAD < slots:
            begin(slot + AHEAD)
        at = 0
        for kind in [0] * plain + [1] * masked:
            left = left_buf[slot]
            if kind:
                keep = [keep_ref[pl.ds(leaves[2 * slot + half], 1), :].astype(BF) for half in range(2)]
                left = left * jnp.concatenate(keep, axis=1)
            value = jnp.dot(left, right_buf[slot], preferred_element_type=F32)
            rows = pl.ds(at, ROWS)
            if slot:
                out_ref[rows, :] += value
            elif added:
                out_ref[rows, :] = refs[0][rows, :] + value
            else:
                out_ref[rows, :] = value
            at += ROWS


def products(front, me, keep, parts, start=None, plain=True, masked=True):
    blocks = [part[0] for part in parts]
    units = [(i, row, part[1], part[2], part[3] + row) for i, part in enumerate(parts) for row in range(2)]
    out = jax.ShapeDtypeStruct(((plain + masked) * ROWS, SAMPLES), F32)
    anywhere = pl.BlockSpec(memory_space=pl.ANY)
    whole = lambda array: pl.BlockSpec(array.shape, lambda i, s: (0, 0))
    return pl.pallas_call(
        functools.partial(product_kernel, units, plain, masked, start is not None),
        grid_spec=pltpu.PrefetchScalarGridSpec(
            num_scalar_prefetch=1,
            grid=(1,),
            in_specs=[anywhere, whole(keep)] + [anywhere] * len(blocks) + ([] if start is None else [whole(start)]),
            out_specs=whole(out),
            scratch_shapes=[
                pltpu.VMEM((len(units) // 2, ROWS, 2 * WINDOW), BF),
                pltpu.VMEM((len(units) // 2, 2 * WINDOW, SAMPLES), BF),
                pltpu.SemaphoreType.DMA((len(units), 2)),
            ],
        ),
        out_shape=out,
        input_output_aliases={} if start is None else {3 + len(blocks): 0},
        compiler_params=pltpu.CompilerParams(vmem_limit_bytes=VMEM),
        cost_estimate=pl.CostEstimate(
            flops=2 * len(units) * out.shape[0] * WINDOW * SAMPLES,
            bytes_accessed=2 * len(units) * ROWS * WINDOW,
            transcendentals=0,
        ),
    )(me[None], front, keep, *blocks, *([] if start is None else [start]))


def pair_kernel(me_ref, front, mine_ref, yours_ref, names_ref, out_ref, left_buf, right_buf, sems):
    leaves = (me_ref[0], jnp.bitwise_xor(me_ref[0], 1))
    copies = [
        pltpu.make_async_copy(
            front.at[:, pl.ds(pl.multiple_of(window_tile(leaf) * LANES, LANES), WINDOW)],
            left_buf.at[:, pl.ds(half * WINDOW, WINDOW)],
            sems.at[half],
        )
        for half, leaf in enumerate(leaves)
    ]
    for copy in copies:
        copy.start()
    named = jnp.where(lax.broadcasted_iota(jnp.int32, (ROWS, RANK), 0) == names_ref[...], 1.0, 0.0).astype(BF)
    count = jnp.dot(named, jnp.ones((RANK, SAMPLES), BF), preferred_element_type=F32).astype(BF)
    right_buf[...] = jnp.zeros_like(right_buf)
    for half, leaf in enumerate(leaves):
        at = pl.ds(pl.multiple_of(half * WINDOW + window_place(leaf), 32), ROWS)
        right_buf[at, :] = yours_ref[...] * count if half else mine_ref[...]
    for copy in copies:
        copy.wait()
    out_ref[...] = jnp.dot(left_buf[...], right_buf[...], preferred_element_type=F32)


def pair_terms(front, me, mine, yours, names):
    whole = lambda array: pl.BlockSpec(array.shape, lambda i, s: (0, 0))
    return pl.pallas_call(
        pair_kernel,
        grid_spec=pltpu.PrefetchScalarGridSpec(
            num_scalar_prefetch=1,
            grid=(1,),
            in_specs=[pl.BlockSpec(memory_space=pl.ANY), whole(mine), whole(yours), whole(names)],
            out_specs=pl.BlockSpec((ROWS, SAMPLES), lambda i, s: (0, 0)),
            scratch_shapes=[
                pltpu.VMEM((ROWS, 2 * WINDOW), BF),
                pltpu.VMEM((2 * WINDOW, SAMPLES), BF),
                pltpu.SemaphoreType.DMA((2,)),
            ],
        ),
        out_shape=jax.ShapeDtypeStruct((ROWS, SAMPLES), F32),
        compiler_params=pltpu.CompilerParams(vmem_limit_bytes=VMEM),
        cost_estimate=pl.CostEstimate(flops=4 * ROWS * WINDOW * SAMPLES, bytes_accessed=4 * ROWS * WINDOW, transcendentals=0),
    )(me[None], front, mine, yours, names)


def body(front_rows, samples, child_rows, child_owner, child_local, leaf_skeleton, merge_select):
    leaf_total = lax.axis_size("hss")
    myself = lax.axis_index("hss")
    side = jnp.bitwise_and(myself, 1)
    front = front_rows[0]
    skeletons = leaf_skeleton[0]

    own = samples[0]
    turned = [own] + [shifted(own, first(turn)) for turn in (1, 2, 3)]
    lines = [jnp.stack(turned[:2]), jnp.stack(turned[2:])]

    root_slot, keep = fates(myself, merge_select[0], skeletons)

    groups = CHILD // LANES
    owners = lax.reshape(child_owner, (leaf_total * groups, LANES))
    targets = lax.reshape(child_local, (leaf_total * groups, LANES))
    my_owners = lax.dynamic_slice_in_dim(owners, myself * groups, groups, 0).reshape(-1)
    my_targets = my_owners * ROWS + lax.dynamic_slice_in_dim(targets, myself * groups, groups, 0).reshape(-1)
    earlier = iota(CHILD)[:, None] < iota(CHILD)[None, :]
    my_slots = jnp.sum(((my_owners[:, None] == my_owners[None, :]) & earlier).astype(jnp.int32), axis=0)
    destination = my_owners * CAP + my_slots
    send_select = (iota(leaf_total * CAP)[:, None] == destination[None, :]).astype(BF)
    outgoing = jnp.dot(send_select, child_rows[0], preferred_element_type=F32).astype(BF)
    all_rows = iota(leaf_total)[:, None] * ROWS + skeletons + 1
    root_ids = jnp.sum(
        jnp.where(root_slot[:, :, None] == iota(RANK)[None, None, :] + 1, all_rows[:, :, None], 0), axis=(0, 1)
    ) - 1
    root_hits = (root_ids[:, None] == my_targets[None, :]).astype(BF)
    root_arrivals = jnp.dot(root_hits, child_rows[0], preferred_element_type=F32)

    lines, outgoing = lax.optimization_barrier((lines, outgoing))
    far_a = shifted(lines[0], second(2))
    near_b = shifted(lines[1], second(1))
    near_a = shifted(lines[0], second(1))
    far_b = shifted(lines[1], second(2))

    def both(block, step, turn):
        return [(block, 0, step, turn), (shifted(block, cores), 1, step, turn)]

    parts = both(lines[0], 0, 0) + both(lines[1], 0, 2)
    total = products(front, myself, keep, parts)
    yours = parts[1][0][0]
    far_a, near_b, outgoing, total = lax.optimization_barrier((far_a, near_b, outgoing, total))
    incoming = lax.all_to_all(
        outgoing.reshape(leaf_total, CAP, SAMPLES), "hss", split_axis=0, concat_axis=0, tiled=True
    ).reshape(leaf_total * CAP, SAMPLES)
    opposite = [shifted(far_a, second(1)), shifted(near_b, second(2))]
    parts = both(far_a, 2, 0) + both(near_b, 1, 2) + both(near_a, 1, 0) + both(far_b, 2, 2)
    total = products(front, myself, keep, parts, total)
    opposite, total = lax.optimization_barrier((opposite, total))
    full, root = total[:ROWS], total[ROWS:]
    parts = both(opposite[0], 3, 0) + both(opposite[1], 3, 2)
    root = products(front, myself, keep, parts, root, plain=False)
    my_root_slot = pick_index(root_slot, myself)
    my_skeleton = pick_index(skeletons, myself)
    root_rows = jnp.sum(jnp.where(my_root_slot[:, None] == iota(RANK)[None, :] + 1, my_skeleton[:, None] + 1, 0), axis=0) - 1
    root_pick = (root_rows[:, None] == iota(ROWS)[None, :]).astype(F32)
    root = jnp.dot(root_pick, root, precision=lax.Precision.HIGHEST) + root_arrivals

    half = RANK // 2
    kept = jnp.where(side == 0, root[:half], root[half:])
    kept = kept + shifted(jnp.where(side == 0, root[half:], root[:half]), cores)
    kept, full = lax.optimization_barrier((kept, full))
    full = products(front, myself, keep, parts[:2], full, masked=False)
    kept = total_over_ring(kept, along_z)
    kept, full = lax.optimization_barrier((kept, full))
    full = products(front, myself, keep, parts[2:], full, masked=False)
    kept = total_over_ring(kept, along_x)
    other = shifted(kept, cores)
    root = jnp.concatenate([jnp.where(side == 0, kept, other), jnp.where(side == 0, other, kept)], axis=0)

    hits = (owners == myself).astype(BF)
    before = (iota(LANES)[:, None] < iota(LANES)[None, :]).astype(BF)
    row = iota(leaf_total * groups)
    above = ((row[:, None] // groups == row[None, :] // groups) & (row[:, None] > row[None, :])).astype(BF)
    counts = jnp.dot(hits, jnp.ones((LANES, LANES), BF), preferred_element_type=F32).astype(BF)
    order = jnp.dot(hits, before, preferred_element_type=F32) + jnp.dot(above, counts, preferred_element_type=F32)
    placed = jnp.where(owners == myself, order.astype(jnp.int32), CAP).reshape(leaf_total, groups, LANES)
    slot_hits = placed[:, :, :, None] == iota(CAP)
    slot_rows = jnp.sum(jnp.where(slot_hits, targets.reshape(leaf_total, groups, LANES)[:, :, :, None] + 1, 0), axis=(1, 2)) - 1
    selector = (iota(ROWS)[:, None] == slot_rows.reshape(-1)[None, :]).astype(BF)
    full = full + jnp.dot(selector, incoming, preferred_element_type=F32)
    parent = full.astype(BF)

    pair_choice = pick_index(merge_select[0], jnp.right_shift(myself, 1)) - side * RANK
    pair_rows = jnp.sum(jnp.where(iota(RANK)[:, None] == pair_choice[None, :], my_skeleton[:, None] + 1, 0), axis=0) - 1
    pair_pick = (pair_rows[:, None] == iota(ROWS)[None, :]).astype(F32)
    pair_gone = pair_terms(front, myself, own, yours, pick_index(skeletons, cores(myself))[None])
    pair = jnp.dot(pair_pick, full - pair_gone, precision=lax.Precision.HIGHEST)
    pair = pair + shifted(pair, cores)
    return (parent[None], pair[None], root[None])


def solution(mesh):
    in_specs = (
        P("front", "hss", None),
        P("front", "hss", None),
        P("front", "hss", None),
        P("front", None, None),
        P("front", None),
        P("front", None, None),
        P("front", None, None),
    )
    out_specs = (P("front", "hss", None), P("front", "hss", None), P("front", None, None))
    return jax.shard_map(body, mesh=mesh, in_specs=in_specs, out_specs=out_specs, check_vma=False)
```

time: 119 us -> 102 us (0.86)
  matrix products: 54.1 us -> 6.77 us
  Pallas kernels: 0 us -> 36.4 us
  between operations: 14.5 us -> 1.09 us
  starting transfers between devices: 20.5 us -> 32.3 us
  waiting for transfers between devices: 18.8 us -> 10.1 us
  local copies, waits for them, and re-layouts: 0.99 us -> 5.37 us
    dot_general x9 -> x6, matrix products: 52.3 us -> 4.97 us  [the longest x1 2.12 us: body(): full = full + jnp.dot(selector, incoming, preferred_element_type=F32)]
    pallas_call x0 -> x7, Pallas kernels: none -> 36.4 us  [the longest x5 31.2 us: products(): pl.pallas_call(functools.partial(product_kernel, units, plain, masked, st...]
    all_gather x1 -> x0, waiting for transfers between devices: 15.8 us -> none  [body(): gathered = lax.all_gather(samples[0], 'hss', axis=0, tiled=True)]
    ppermute x9 -> x26, starting transfers between devices: 11 us -> 26.8 us  [shifted(): lax.ppermute(x, 'hss', [(i, move(i)) for i in range(lax.axis_size('hss'))])]
    all_to_all x1, waiting for transfers between devices: 0.01 us -> 5.42 us  [body(): lax.all_to_all(outgoing.reshape(leaf_total, CAP, SAMPLES), 'hss', split_a...]
    unnamed x15 -> x29, local copies, waits for them, and re-layouts: 0.55 us -> 5.19 us
    reduce_sum x8 -> x3, other arithmetic: 6.1 us -> 2.18 us  [the longest x1 1.39 us: body(): jnp.sum(jnp.where(root_slot[:, :, None] == iota(RANK)[None, None, :] + 1,...]
    all_to_all x1, starting transfers between devices: 9.43 us -> 5.53 us  [body(): lax.all_to_all(outgoing.reshape(leaf_total, CAP, SAMPLES), 'hss', split_a...]
  transfers between devices with their start and end apart: 11 -> 27, of which waited for: 5 -> 4; matrix products, arithmetic and copies ran while one was open for 48% -> 16% of each run, Pallas kernels for 0% -> 36%
where the time goes in v1:
time: 102 us; the launch traced here: 101 us
  Pallas kernels  36.4 us (36%)
  starting transfers between devices  32.3 us (32%)
  waiting for transfers between devices  10.1 us (10%)
  other arithmetic  8.99 us (9%)
  matrix products  6.77 us (7%)
  local copies, waits for them, and re-layouts  5.37 us (5%)
  between operations  1.09 us (1%)
    pallas_call x5, Pallas kernels, products(): pl.pallas_call(functools.partial(product_kernel, units, plain, masked, st...  31.2 us
    ppermute x26, starting transfers between devices, shifted(): lax.ppermute(x, 'hss', [(i, move(i)) for i in range(lax.axis_size('hss'))])  26.8 us
    all_to_all x1, starting transfers between devices, body(): lax.all_to_all(outgoing.reshape(leaf_total, CAP, SAMPLES), 'hss', split_a...  5.53 us
    all_to_all x1, waiting for transfers between devices, body(): lax.all_to_all(outgoing.reshape(leaf_total, CAP, SAMPLES), 'hss', split_a...  5.42 us
    unnamed x29, local copies, waits for them, and re-layouts  5.19 us
    ppermute x26, waiting for transfers between devices, shifted(): lax.ppermute(x, 'hss', [(i, move(i)) for i in range(lax.axis_size('hss'))])  4.66 us
    pallas_call x1, Pallas kernels, fates(): pl.pallas_call(fate_kernel, in_specs=[pl.BlockSpec(memory_space=pltpu.SME...  2.65 us
    pallas_call x1, Pallas kernels, pair_terms(): pl.pallas_call(pair_kernel, grid_spec=pltpu.PrefetchScalarGridSpec(num_sc...  2.55 us
  transfers between devices with their start and end apart: 27, of which 4 were waited for; matrix products, arithmetic and copies ran while one was open for 16% of the time, Pallas kernels for 36%

profile of v1, /device:TPU:1, one launch (start us, length us, event | category | flops | bytes accessed | tf_op | source)
XLA Modules:
  0.0 101.0 jit_solution(16167755339681177186)
XLA Ops:
  0.7 3.4 %collective-permute-start.1 = (bf16[608,256]{1,0:T(8,128)(2,1)}, bf16[608,256]{1,0:T(8,128)(2,1)S(1)}, u32[]{:S(2)}, u32[]{:S(2)}) collective-permute-start(bf16[608,256]{1,0:T(8,128)(2,1)} %bitcast.47), channel_id=1, source_target_pairs={{0,6},{1,25},{2,4},{3,27},{4,2},{5,29},{6,0},{7,31},{8,14},{9,17},... | collective-permute-start | bytes 933896 | tf_op jit(solution)/shard_map/ppermute | solution.py:36
  4.0 0.5 collective-permute-start.2
  4.6 0.2 collective-permute-start
  4.7 0.9 broadcast_add_fusion
  5.6 0.7 bitcast_add_fusion
  6.3 0.2 convert_reduce_fusion
  6.5 0.7 copy.16
  7.2 0.8 fusion.30
  8.0 0.7 copy-done.9
  8.7 2.6 %shard_map.94 = (s32[32,128]{1,0:T(8,128)S(1)}, f32[32,768]{1,0:T(8,128)S(1)}) custom-call(s32[1]{0:T(128)} %bitcast.me_ref, s32[31,128]{1,0:T(8,128)S(1)} %bitcast.52, s32[32,128]{1,0:T(8,128)S(1)} %bitcast.51), custom_call_target="tpu_custom_call" | custom-call | flops 33554432 | bytes 131072 | tf_op jit(solution)/shard_map/pallas_call | solution.py:96
  11.4 0.8 add_add_fusion.2
  12.2 1.8 %fusion.2 = bf16[2048,256]{1,0:T(8,128)(2,1)} fusion(s32[512]{0:T(512)S(1)} %multiply_add_fusion, bf16[1,512,256]{2,1,0:T(8,128)(2,1)S(1)} %copy-done), kind=kOutput, calls=%fused_computation.6 | convolution fusion | flops 538443776 | bytes 1312768 | tf_op jit(solution)/shard_map/dot_general | solution.py:269
  14.0 0.7 fusion.32
  14.7 0.6 select_reduce_fusion.2
  15.3 0.1 pad_maximum_fusion.refs_0_
  15.4 0.1 pad_maximum_fusion.1.refs_2_
  15.5 2.6 %collective-permute-start.5 = (bf16[2,608,256]{2,1,0:T(8,128)(2,1)S(1)}, bf16[2,608,256]{2,1,0:T(8,128)(2,1)S(1)}, u32[]{:S(2)}, u32[]{:S(2)}) collective-permute-start(bf16[2,608,256]{2,1,0:T(8,128)(2,1)S(1)} %pad_maximum_fusion.refs_0_), channel_id=1, source_target_pairs={{0,1},{1,0},{2,3},{3,2},{4,5},{5,4},{6,7},{7,6},{8,9},{9,8},{10,11... | collective-permute-start | bytes 1867784 | tf_op jit(solution)/shard_map/ppermute | solution.py:36
  18.0 1.4 %select_reduce_fusion.1 = s32[128]{0:T(128)S(1)} fusion(s32[32,128]{1,0:T(8,128)S(1)} %add_add_fusion.2, s32[128]{0:T(128)S(1)} %iota_add_fusion, s32[32,128]{1,0:T(8,128)S(1)} %get-tuple-element.27), kind=kLoop, calls=%fused_computation.8 | loop fusion | flops 1572736 | bytes 33792 | tf_op jit(solution)/shard_map/reduce_sum | solution.py:271
  19.5 0.1 collective-permute-start.6
  19.6 0.1 fusion.19
  19.7 2.9 %collective-permute-start.3 = (bf16[2,608,256]{2,1,0:T(8,128)(2,1)S(1)}, bf16[2,608,256]{2,1,0:T(8,128)(2,1)}, u32[]{:S(2)}, u32[]{:S(2)}) collective-permute-start(bf16[2,608,256]{2,1,0:T(8,128)(2,1)S(1)} %pad_maximum_fusion.refs_0_), channel_id=1, source_target_pairs={{0,24},{1,7},{2,26},{3,5},{4,28},{5,3},{6,30},{7,1},{8,16},{9,15},... | collective-permute-start | bytes 1867784 | tf_op jit(solution)/shard_map/ppermute | solution.py:36
  22.6 1.5 %collective-permute-start.11 = (bf16[2,608,256]{2,1,0:T(8,128)(2,1)S(1)}, bf16[2,608,256]{2,1,0:T(8,128)(2,1)}, u32[]{:S(2)}, u32[]{:S(2)}) collective-permute-start(bf16[2,608,256]{2,1,0:T(8,128)(2,1)S(1)} %pad_maximum_fusion.refs_0_), channel_id=1, source_target_pairs={{0,8},{1,3},{2,10},{3,1},{4,12},{5,7},{6,14},{7,5},{8,0},{9,11},{1... | collective-permute-start | bytes 1867784 | tf_op jit(solution)/shard_map/ppermute | solution.py:36
  24.1 0.1 collective-permute-start.13
  24.2 0.9 fusion.6
  25.1 0.8 copy-done.7
  26.0 1.1 %copy-done.8 = bf16[2,608,256]{2,1,0:T(8,128)(2,1)S(1)} copy-done((bf16[2,608,256]{2,1,0:T(8,128)(2,1)S(1)}, bf16[2,608,256]{2,1,0:T(8,128)(2,1)}, u32[]{:S(2)}) %copy-start.8) | copy-done | bytes 622616
  27.0 6.3 %shard_map.95.refs_8_ = f32[1216,256]{1,0:T(8,128)S(1)} custom-call(s32[1]{0:T(128)} %bitcast.me_ref, bf16[608,19456]{1,0:T(8,128)(2,1)} %bitcast.53, f32[32,768]{1,0:T(8,128)S(1)} %get-tuple-element.19.keep_ref, bf16[2,608,256]{2,1,0:T(8,128)(2,1)S(1)} %pad_maximum_fusion.refs_0_, bf16[2,608,256]{2,1,0:T(8,128)(2,1)S(1)} %collective-permute-done.5.refs_1_, ...), custom_call_target="tpu_custom_call" | custom-call | flops 3825205248 | bytes 7471104 | tf_op jit(solution)/shard_map/pallas_call | solution.py:179
  33.3 1.4 %collective-permute-start.10 = (bf16[2,608,256]{2,1,0:T(8,128)(2,1)}, bf16[2,608,256]{2,1,0:T(8,128)(2,1)S(1)}, u32[]{:S(2)}, u32[]{:S(2)}) collective-permute-start(bf16[2,608,256]{2,1,0:T(8,128)(2,1)} %collective-permute-done.4.refs_2_), channel_id=1, source_target_pairs={{0,1},{1,0},{2,3},{3,2},{4,5},{5,4},{6,7},{7,6},{8,9},{9,8},{10,11... | collective-permute-start | bytes 1867784 | tf_op jit(solution)/shard_map/ppermute | solution.py:36
  34.7 0.1 collective-permute-start.9
  34.8 4.0 %collective-permute-done.11.refs_4_ = bf16[2,608,256]{2,1,0:T(8,128)(2,1)} collective-permute-done((bf16[2,608,256]{2,1,0:T(8,128)(2,1)S(1)}, bf16[2,608,256]{2,1,0:T(8,128)(2,1)}, u32[]{:S(2)}, u32[]{:S(2)}) %collective-permute-start.11) | collective-permute-done | bytes 622624 | tf_op jit(solution)/shard_map/ppermute | solution.py:36
  38.8 1.2 %collective-permute-start.12 = (bf16[2,608,256]{2,1,0:T(8,128)(2,1)}, bf16[2,608,256]{2,1,0:T(8,128)(2,1)S(1)}, u32[]{:S(2)}, u32[]{:S(2)}) collective-permute-start(bf16[2,608,256]{2,1,0:T(8,128)(2,1)} %collective-permute-done.11.refs_4_), channel_id=1, source_target_pairs={{0,1},{1,0},{2,3},{3,2},{4,5},{5,4},{6,7},{7,6},{8,9},{9,8},{10,11... | collective-permute-start | bytes 1867784 | tf_op jit(solution)/shard_map/ppermute | solution.py:36
  40.0 0.6 select_reduce_fusion
  40.7 0.9 fusion.11
  41.6 0.8 collective-permute-start.7
  42.4 2.3 %collective-permute-start.8 = (bf16[2,608,256]{2,1,0:T(8,128)(2,1)}, bf16[2,608,256]{2,1,0:T(8,128)(2,1)S(1)}, u32[]{:S(2)}, u32[]{:S(2)}) collective-permute-start(bf16[2,608,256]{2,1,0:T(8,128)(2,1)} %collective-permute-done.4.refs_2_), channel_id=1, source_target_pairs={{0,24},{1,7},{2,26},{3,5},{4,28},{5,3},{6,30},{7,1},{8,16},{9,15},... | collective-permute-start | bytes 1867784 | tf_op jit(solution)/shard_map/ppermute | solution.py:36
  44.7 11.1 %shard_map.96 = f32[1216,256]{1,0:T(8,128)S(1)} custom-call(s32[1]{0:T(128)} %bitcast.me_ref, bf16[608,19456]{1,0:T(8,128)(2,1)} %bitcast.54, f32[32,768]{1,0:T(8,128)S(1)} %get-tuple-element.19.keep_ref, bf16[2,608,256]{2,1,0:T(8,128)(2,1)} %collective-permute-done.3.refs_0_, ...), custom_call_target="tpu_custom_call", output_to_operand_aliasing={{}: (11, {})} | custom-call | flops 7650410496 | bytes 14942208 | tf_op jit(solution)/shard_map/pallas_call | solution.py:179
  55.9 0.1 collective-permute-start.15
  55.9 0.5 collective-permute-start.16
  56.4 0.1 sub.45
  56.5 5.5 %all-to-all-start = ((bf16[32,64,256]{2,1,0:T(8,128)(2,1)}), bf16[32,64,256]{2,1,0:T(8,128)(2,1)}, u32[]{:S(2)}, u32[]{:S(2)}) async-start(bf16[32,64,256]{2,1,0:T(8,128)(2,1)} %bitcast.59), calls=%async_computation | async-start | bytes 2097152 | tf_op jit(solution)/shard_map/all_to_all | solution.py:290
  62.1 1.0 copy-done.6
  63.1 2.5 %shard_map.100 = f32[608,256]{1,0:T(8,128)S(1)} custom-call(s32[1]{0:T(128)} %bitcast.me_ref, bf16[608,19456]{1,0:T(8,128)(2,1)} %bitcast.55, bf16[608,256]{1,0:T(8,128)(2,1)S(1)} %bitcast.50, bf16[608,256]{1,0:T(8,128)(2,1)S(1)} %slice_bitcast_fusion.yours_ref, s32[1,128]{1,0:T(1,128)S(1)} %get-tuple-element.43.names_ref), custom_call_target="tpu_custom_call" | custom-call | flops 478150656 | bytes 1867776 | tf_op jit(solution)/shard_map/pallas_call | solution.py:228
  65.6 0.8 copy-done.1
  66.5 0.1 fusion.35
  66.6 6.2 %shard_map.97 = f32[608,256]{1,0:T(8,128)S(1)} custom-call(s32[1]{0:T(128)} %bitcast.me_ref, bf16[608,19456]{1,0:T(8,128)(2,1)} %bitcast.56, f32[32,768]{1,0:T(8,128)S(1)} %get-tuple-element.19.keep_ref, bf16[2,608,256]{2,1,0:T(8,128)(2,1)S(1)} %collective-permute-done.7.refs_0_, ...), custom_call_target="tpu_custom_call", output_to_operand_aliasing={{}: (7, {})} | custom-call | flops 1912602624 | bytes 7471104 | tf_op jit(solution)/shard_map/pallas_call | solution.py:179
  72.8 0.4 convolution_add_fusion
  73.2 0.4 collective-permute-start.17
  73.6 5.4 %all-to-all-done = bf16[32,64,256]{2,1,0:T(8,128)(2,1)} async-done(((bf16[32,64,256]{2,1,0:T(8,128)(2,1)}), bf16[32,64,256]{2,1,0:T(8,128)(2,1)}, u32[]{:S(2)}, u32[]{:S(2)}) %all-to-all-start) | async-done | bytes 1048608 | tf_op jit(solution)/shard_map/all_to_all | solution.py:290
  79.0 2.1 %fusion = f32[608,256]{1,0:T(8,128)S(1)} fusion(bf16[2048,256]{1,0:T(8,128)(2,1)} %bitcast.17, s32[2048]{0:T(1024)S(1)} %sub.45), kind=kOutput, calls=%fused_computation.1 | convolution fusion | flops 638779392 | bytes 1679360 | tf_op jit(solution)/shard_map/dot_general | solution.py:328
  81.2 0.1 collective-permute-start.18
  81.3 1.3 %collective-permute-start.19 = (f32[64,256]{1,0:T(8,128)S(1)}, f32[64,256]{1,0:T(8,128)S(1)}, u32[]{:S(2)}, u32[]{:S(2)}) collective-permute-start(f32[64,256]{1,0:T(8,128)S(1)} %select_add_fusion), channel_id=1, source_target_pairs={{0,6},{1,7},{2,4},{3,5},{4,2},{5,3},{6,0},{7,1},{8,14},{9,15},{10,... | collective-permute-start | bytes 196616 | tf_op jit(solution)/shard_map/ppermute | solution.py:36
  82.6 2.0 %collective-permute-start.20 = (f32[64,256]{1,0:T(8,128)S(1)}, f32[64,256]{1,0:T(8,128)S(1)}, u32[]{:S(2)}, u32[]{:S(2)}) collective-permute-start(f32[64,256]{1,0:T(8,128)S(1)} %select_add_fusion), channel_id=1, source_target_pairs={{0,4},{1,5},{2,6},{3,7},{4,0},{5,1},{6,2},{7,3},{8,12},{9,13},{10,... | collective-permute-start | bytes 196616 | tf_op jit(solution)/shard_map/ppermute | solution.py:36
  84.5 3.8 %shard_map.98.refs_2_ = f32[608,256]{1,0:T(8,128)S(1)} custom-call(s32[1]{0:T(128)} %bitcast.me_ref, bf16[608,19456]{1,0:T(8,128)(2,1)} %bitcast.57, f32[32,768]{1,0:T(8,128)S(1)} %get-tuple-element.19.keep_ref, bf16[2,608,256]{2,1,0:T(8,128)(2,1)S(1)} %collective-permute-done.7.refs_0_, ...), custom_call_target="tpu_custom_call", output_to_operand_aliasing={{}: (5, {})} | custom-call | flops 956301312 | bytes 3735552 | tf_op jit(solution)/shard_map/pallas_call | solution.py:179
  88.4 0.1 collective-permute-start.22
  88.5 1.5 %collective-permute-start.23 = (f32[64,256]{1,0:T(8,128)S(1)}, f32[64,256]{1,0:T(8,128)S(1)}, u32[]{:S(2)}, u32[]{:S(2)}) collective-permute-start(f32[64,256]{1,0:T(8,128)S(1)} %add_add_fusion.1), channel_id=1, source_target_pairs={{0,24},{1,25},{2,26},{3,27},{4,28},{5,29},{6,30},{7,31},{8,16},{9,... | collective-permute-start | bytes 196616 | tf_op jit(solution)/shard_map/ppermute | solution.py:36
  90.0 1.7 %collective-permute-start.24 = (f32[64,256]{1,0:T(8,128)S(1)}, f32[64,256]{1,0:T(8,128)S(1)}, u32[]{:S(2)}, u32[]{:S(2)}) collective-permute-start(f32[64,256]{1,0:T(8,128)S(1)} %add_add_fusion.1), channel_id=1, source_target_pairs={{0,16},{1,17},{2,18},{3,19},{4,20},{5,21},{6,22},{7,23},{8,24},{9,... | collective-permute-start | bytes 196616 | tf_op jit(solution)/shard_map/ppermute | solution.py:36
  91.7 3.8 %shard_map.99 = f32[608,256]{1,0:T(8,128)S(1)} custom-call(s32[1]{0:T(128)} %bitcast.me_ref, bf16[608,19456]{1,0:T(8,128)(2,1)} %bitcast.58, f32[32,768]{1,0:T(8,128)S(1)} %get-tuple-element.19.keep_ref, bf16[2,608,256]{2,1,0:T(8,128)(2,1)S(1)} %collective-permute-done.8.refs_2_.refs_0_, ...), custom_call_target="tpu_custom_call", output_to_operand_aliasing={{}: (5, {})} | custom-call | flops 956301312 | bytes 3735552 | tf_op jit(solution)/shard_map/pallas_call | solution.py:179
  95.6 0.5 fusion.8
  96.1 2.1 %collective-permute-start.25 = (f32[64,256]{1,0:T(8,128)S(1)}, f32[64,256]{1,0:T(8,128)S(1)}, u32[]{:S(2)}, u32[]{:S(2)}) collective-permute-start(f32[64,256]{1,0:T(8,128)S(1)} %add_add_fusion), channel_id=1, source_target_pairs={{0,1},{1,0},{2,3},{3,2},{4,5},{5,4},{6,7},{7,6},{8,9},{9,8},{10,11... | collective-permute-start | bytes 196616 | tf_op jit(solution)/shard_map/ppermute | solution.py:36
  98.2 0.8 convert_bitcast_fusion
  99.0 0.1 collective-permute-done.25
  99.1 0.7 maximum_bitcast_fusion
  99.8 0.5 collective-permute-done.21
  100.3 0.7 add_bitcast_fusion
  (65 shorter events, 0.3 us)
Async XLA Ops:
  0.6 11.6 %copy-start = (bf16[1,512,256]{2,1,0:T(8,128)(2,1)S(1)}, bf16[1,512,256]{2,1,0:T(8,128)(2,1)}, u32[]{:S(2)}) copy-start(bf16[1,512,256]{2,1,0:T(8,128)(2,1)} %param.9) | copy-start | bytes 786436
  0.6 14.7 %copy-start.5 = (bf16[1,608,256]{2,1,0:T(8,128)(2,1)S(1)}, bf16[1,608,256]{2,1,0:T(8,128)(2,1)}, u32[]{:S(2)}) copy-start(bf16[1,608,256]{2,1,0:T(8,128)(2,1)} %param.8) | copy-start | bytes 933892
  0.7 14.7 %collective-permute-start.1 = (bf16[608,256]{1,0:T(8,128)(2,1)}, bf16[608,256]{1,0:T(8,128)(2,1)S(1)}, u32[]{:S(2)}, u32[]{:S(2)}) collective-permute-start(bf16[608,256]{1,0:T(8,128)(2,1)} %bitcast.47), channel_id=1, source_target_pairs={{0,6},{1,25},{2,4},{3,27},{4,2},{5,29},{6,0},{7,31},{8,14},{9,17},... | collective-permute-start | bytes 933896 | tf_op jit(solution)/shard_map/ppermute | solution.py:36
  4.0 11.3 %collective-permute-start.2 = (bf16[608,256]{1,0:T(8,128)(2,1)}, bf16[608,256]{1,0:T(8,128)(2,1)S(1)}, u32[]{:S(2)}, u32[]{:S(2)}) collective-permute-start(bf16[608,256]{1,0:T(8,128)(2,1)} %bitcast.48), channel_id=1, source_target_pairs={{0,4},{1,17},{2,6},{3,19},{4,0},{5,21},{6,2},{7,23},{8,12},{9,25},... | collective-permute-start | bytes 933896 | tf_op jit(solution)/shard_map/ppermute | solution.py:36
  4.6 10.7 %collective-permute-start = (bf16[608,256]{1,0:T(8,128)(2,1)}, bf16[608,256]{1,0:T(8,128)(2,1)S(1)}, u32[]{:S(2)}, u32[]{:S(2)}) collective-permute-start(bf16[608,256]{1,0:T(8,128)(2,1)} %bitcast.49), channel_id=1, source_target_pairs={{0,2},{1,9},{2,0},{3,11},{4,6},{5,13},{6,4},{7,15},{8,10},{9,1},{1... | collective-permute-start | bytes 933896 | tf_op jit(solution)/shard_map/ppermute | solution.py:36
  8.0 0.7 copy-start.9
  12.2 7.2 %copy-start.12 = (s32[1,16384,1]{1,2,0:T(1,128)S(1)}, s32[1,16384,1]{1,2,0:T(1,128)}, u32[]{:S(2)}) copy-start(s32[1,16384,1]{1,2,0:T(1,128)} %param.10) | copy-start | bytes 196612
  15.5 8.6 %collective-permute-start.5 = (bf16[2,608,256]{2,1,0:T(8,128)(2,1)S(1)}, bf16[2,608,256]{2,1,0:T(8,128)(2,1)S(1)}, u32[]{:S(2)}, u32[]{:S(2)}) collective-permute-start(bf16[2,608,256]{2,1,0:T(8,128)(2,1)S(1)} %pad_maximum_fusion.refs_0_), channel_id=1, source_target_pairs={{0,1},{1,0},{2,3},{3,2},{4,5},{5,4},{6,7},{7,6},{8,9},{9,8},{10,11... | collective-permute-start | bytes 1867784 | tf_op jit(solution)/shard_map/ppermute | solution.py:36
  19.5 5.6 %collective-permute-start.6 = (bf16[2,608,256]{2,1,0:T(8,128)(2,1)S(1)}, bf16[2,608,256]{2,1,0:T(8,128)(2,1)S(1)}, u32[]{:S(2)}, u32[]{:S(2)}) collective-permute-start(bf16[2,608,256]{2,1,0:T(8,128)(2,1)S(1)} %pad_maximum_fusion.1.refs_2_), channel_id=1, source_target_pairs={{0,1},{1,0},{2,3},{3,2},{4,5},{5,4},{6,7},{7,6},{8,9},{9,8},{10,11... | collective-permute-start | bytes 1867784 | tf_op jit(solution)/shard_map/ppermute | solution.py:36
  19.7 13.6 %collective-permute-start.3 = (bf16[2,608,256]{2,1,0:T(8,128)(2,1)S(1)}, bf16[2,608,256]{2,1,0:T(8,128)(2,1)}, u32[]{:S(2)}, u32[]{:S(2)}) collective-permute-start(bf16[2,608,256]{2,1,0:T(8,128)(2,1)S(1)} %pad_maximum_fusion.refs_0_), channel_id=1, source_target_pairs={{0,24},{1,7},{2,26},{3,5},{4,28},{5,3},{6,30},{7,1},{8,16},{9,15},... | collective-permute-start | bytes 1867784 | tf_op jit(solution)/shard_map/ppermute | solution.py:36
  22.6 10.7 %collective-permute-start.4 = (bf16[2,608,256]{2,1,0:T(8,128)(2,1)S(1)}, bf16[2,608,256]{2,1,0:T(8,128)(2,1)}, u32[]{:S(2)}, u32[]{:S(2)}) collective-permute-start(bf16[2,608,256]{2,1,0:T(8,128)(2,1)S(1)} %pad_maximum_fusion.1.refs_2_), channel_id=1, source_target_pairs={{0,8},{1,3},{2,10},{3,1},{4,12},{5,7},{6,14},{7,5},{8,0},{9,11},{1... | collective-permute-start | bytes 1867784 | tf_op jit(solution)/shard_map/ppermute | solution.py:36
  22.6 16.2 %collective-permute-start.11 = (bf16[2,608,256]{2,1,0:T(8,128)(2,1)S(1)}, bf16[2,608,256]{2,1,0:T(8,128)(2,1)}, u32[]{:S(2)}, u32[]{:S(2)}) collective-permute-start(bf16[2,608,256]{2,1,0:T(8,128)(2,1)S(1)} %pad_maximum_fusion.refs_0_), channel_id=1, source_target_pairs={{0,8},{1,3},{2,10},{3,1},{4,12},{5,7},{6,14},{7,5},{8,0},{9,11},{1... | collective-permute-start | bytes 1867784 | tf_op jit(solution)/shard_map/ppermute | solution.py:36
  24.1 9.2 %copy-start.3 = (bf16[2,608,256]{2,1,0:T(8,128)(2,1)}, bf16[2,608,256]{2,1,0:T(8,128)(2,1)S(1)}, u32[]{:S(2)}) copy-start(bf16[2,608,256]{2,1,0:T(8,128)(2,1)S(1)} %collective-permute-done.5.refs_1_) | copy-start | bytes 1867780
  24.1 15.9 %collective-permute-start.13 = (bf16[2,608,256]{2,1,0:T(8,128)(2,1)S(1)}, bf16[2,608,256]{2,1,0:T(8,128)(2,1)}, u32[]{:S(2)}, u32[]{:S(2)}) collective-permute-start(bf16[2,608,256]{2,1,0:T(8,128)(2,1)S(1)} %pad_maximum_fusion.1.refs_2_), channel_id=1, source_target_pairs={{0,24},{1,7},{2,26},{3,5},{4,28},{5,3},{6,30},{7,1},{8,16},{9,15},... | collective-permute-start | bytes 1867784 | tf_op jit(solution)/shard_map/ppermute | solution.py:36
  25.1 0.8 copy-start.7
  26.0 1.1 %copy-start.8 = (bf16[2,608,256]{2,1,0:T(8,128)(2,1)S(1)}, bf16[2,608,256]{2,1,0:T(8,128)(2,1)}, u32[]{:S(2)}) copy-start(bf16[2,608,256]{2,1,0:T(8,128)(2,1)} %copy-done.7) | copy-start | bytes 1867780
  27.0 13.0 %copy-start.11 = (s32[128,128]{1,0:T(8,128)S(1)}, s32[128,128]{1,0:T(8,128)}, u32[]{:S(2)}) copy-start(s32[128,128]{1,0:T(8,128)} %fusion.6) | copy-start | bytes 196612
  33.3 9.0 %collective-permute-start.10 = (bf16[2,608,256]{2,1,0:T(8,128)(2,1)}, bf16[2,608,256]{2,1,0:T(8,128)(2,1)S(1)}, u32[]{:S(2)}, u32[]{:S(2)}) collective-permute-start(bf16[2,608,256]{2,1,0:T(8,128)(2,1)} %collective-permute-done.4.refs_2_), channel_id=1, source_target_pairs={{0,1},{1,0},{2,3},{3,2},{4,5},{5,4},{6,7},{7,6},{8,9},{9,8},{10,11... | collective-permute-start | bytes 1867784 | tf_op jit(solution)/shard_map/ppermute | solution.py:36
  34.7 10.0 %collective-permute-start.9 = (bf16[2,608,256]{2,1,0:T(8,128)(2,1)}, bf16[2,608,256]{2,1,0:T(8,128)(2,1)S(1)}, u32[]{:S(2)}, u32[]{:S(2)}) collective-permute-start(bf16[2,608,256]{2,1,0:T(8,128)(2,1)} %collective-permute-done.3.refs_0_), channel_id=1, source_target_pairs={{0,1},{1,0},{2,3},{3,2},{4,5},{5,4},{6,7},{7,6},{8,9},{9,8},{10,11... | collective-permute-start | bytes 1867784 | tf_op jit(solution)/shard_map/ppermute | solution.py:36
  38.8 5.9 %collective-permute-start.12 = (bf16[2,608,256]{2,1,0:T(8,128)(2,1)}, bf16[2,608,256]{2,1,0:T(8,128)(2,1)S(1)}, u32[]{:S(2)}, u32[]{:S(2)}) collective-permute-start(bf16[2,608,256]{2,1,0:T(8,128)(2,1)} %collective-permute-done.11.refs_4_), channel_id=1, source_target_pairs={{0,1},{1,0},{2,3},{3,2},{4,5},{5,4},{6,7},{7,6},{8,9},{9,8},{10,11... | collective-permute-start | bytes 1867784 | tf_op jit(solution)/shard_map/ppermute | solution.py:36
  40.0 4.7 %collective-permute-start.14 = (bf16[2,608,256]{2,1,0:T(8,128)(2,1)}, bf16[2,608,256]{2,1,0:T(8,128)(2,1)S(1)}, u32[]{:S(2)}, u32[]{:S(2)}) collective-permute-start(bf16[2,608,256]{2,1,0:T(8,128)(2,1)} %collective-permute-done.13.refs_6_), channel_id=1, source_target_pairs={{0,1},{1,0},{2,3},{3,2},{4,5},{5,4},{6,7},{7,6},{8,9},{9,8},{10,11... | collective-permute-start | bytes 1867784 | tf_op jit(solution)/shard_map/ppermute | solution.py:36
  41.6 14.9 %copy-start.13 = (s32[128]{0:T(128)S(1)}, s32[128]{0:T(128)}, u32[]{:S(2)}) copy-start(s32[128]{0:T(128)} %get-tuple-element.35) | copy-start | bytes 1540
  41.6 14.3 %collective-permute-start.7 = (bf16[2,608,256]{2,1,0:T(8,128)(2,1)}, bf16[2,608,256]{2,1,0:T(8,128)(2,1)S(1)}, u32[]{:S(2)}, u32[]{:S(2)}) collective-permute-start(bf16[2,608,256]{2,1,0:T(8,128)(2,1)} %collective-permute-done.3.refs_0_), channel_id=1, source_target_pairs={{0,8},{1,3},{2,10},{3,1},{4,12},{5,7},{6,14},{7,5},{8,0},{9,11},{1... | collective-permute-start | bytes 1867784 | tf_op jit(solution)/shard_map/ppermute | solution.py:36
  42.4 13.5 %collective-permute-start.8 = (bf16[2,608,256]{2,1,0:T(8,128)(2,1)}, bf16[2,608,256]{2,1,0:T(8,128)(2,1)S(1)}, u32[]{:S(2)}, u32[]{:S(2)}) collective-permute-start(bf16[2,608,256]{2,1,0:T(8,128)(2,1)} %collective-permute-done.4.refs_2_), channel_id=1, source_target_pairs={{0,24},{1,7},{2,26},{3,5},{4,28},{5,3},{6,30},{7,1},{8,16},{9,15},... | collective-permute-start | bytes 1867784 | tf_op jit(solution)/shard_map/ppermute | solution.py:36
  55.8 6.2 %copy-start.4 = (bf16[2,608,256]{2,1,0:T(8,128)(2,1)S(1)}, bf16[2,608,256]{2,1,0:T(8,128)(2,1)}, u32[]{:S(2)}) copy-start(bf16[2,608,256]{2,1,0:T(8,128)(2,1)} %copy-done.3) | copy-start | bytes 1867780
  55.9 10.7 %collective-permute-start.15 = (bf16[2,608,256]{2,1,0:T(8,128)(2,1)S(1)}, bf16[2,608,256]{2,1,0:T(8,128)(2,1)}, u32[]{:S(2)}, u32[]{:S(2)}) collective-permute-start(bf16[2,608,256]{2,1,0:T(8,128)(2,1)S(1)} %collective-permute-done.8.refs_2_.refs_0_), channel_id=1, source_target_pairs={{0,1},{1,0},{2,3},{3,2},{4,5},{5,4},{6,7},{7,6},{8,9},{9,8},{10,11... | collective-permute-start | bytes 1867784 | tf_op jit(solution)/shard_map/ppermute | solution.py:36
  55.9 10.6 %collective-permute-start.16 = (bf16[2,608,256]{2,1,0:T(8,128)(2,1)S(1)}, bf16[2,608,256]{2,1,0:T(8,128)(2,1)}, u32[]{:S(2)}, u32[]{:S(2)}) collective-permute-start(bf16[2,608,256]{2,1,0:T(8,128)(2,1)S(1)} %collective-permute-done.7.refs_0_), channel_id=1, source_target_pairs={{0,1},{1,0},{2,3},{3,2},{4,5},{5,4},{6,7},{7,6},{8,9},{9,8},{10,11... | collective-permute-start | bytes 1867784 | tf_op jit(solution)/shard_map/ppermute | solution.py:36
  56.5 22.5 %all-to-all-start = ((bf16[32,64,256]{2,1,0:T(8,128)(2,1)}), bf16[32,64,256]{2,1,0:T(8,128)(2,1)}, u32[]{:S(2)}, u32[]{:S(2)}) async-start(bf16[32,64,256]{2,1,0:T(8,128)(2,1)} %bitcast.59), calls=%async_computation | async-start | bytes 2097152 | tf_op jit(solution)/shard_map/all_to_all | solution.py:290
  62.1 1.0 copy-start.6
  65.6 0.8 copy-start.1
  66.6 6.2 %copy-start.10 = (f32[128,256]{1,0:T(8,128)S(1)}, f32[128,256]{1,0:T(8,128)}, u32[]{:S(2)}) copy-start(f32[128,256]{1,0:T(8,128)} %fusion.11) | copy-start | bytes 393220
  73.2 7.9 %collective-permute-start.17 = (f32[64,256]{1,0:T(8,128)S(1)}, f32[64,256]{1,0:T(8,128)S(1)}, u32[]{:S(2)}, u32[]{:S(2)}) collective-permute-start(f32[64,256]{1,0:T(8,128)S(1)} %slice_select_fusion), channel_id=1, source_target_pairs={{0,1},{1,0},{2,3},{3,2},{4,5},{5,4},{6,7},{7,6},{8,9},{9,8},{10,11... | collective-permute-start | bytes 196616 | tf_op jit(solution)/shard_map/ppermute | solution.py:36
  81.2 7.2 %collective-permute-start.18 = (f32[64,256]{1,0:T(8,128)S(1)}, f32[64,256]{1,0:T(8,128)S(1)}, u32[]{:S(2)}, u32[]{:S(2)}) collective-permute-start(f32[64,256]{1,0:T(8,128)S(1)} %select_add_fusion), channel_id=1, source_target_pairs={{0,2},{1,3},{2,0},{3,1},{4,6},{5,7},{6,4},{7,5},{8,10},{9,11},{10,... | collective-permute-start | bytes 196616 | tf_op jit(solution)/shard_map/ppermute | solution.py:36
  81.3 7.1 %collective-permute-start.19 = (f32[64,256]{1,0:T(8,128)S(1)}, f32[64,256]{1,0:T(8,128)S(1)}, u32[]{:S(2)}, u32[]{:S(2)}) collective-permute-start(f32[64,256]{1,0:T(8,128)S(1)} %select_add_fusion), channel_id=1, source_target_pairs={{0,6},{1,7},{2,4},{3,5},{4,2},{5,3},{6,0},{7,1},{8,14},{9,15},{10,... | collective-permute-start | bytes 196616 | tf_op jit(solution)/shard_map/ppermute | solution.py:36
  82.6 5.8 %collective-permute-start.20 = (f32[64,256]{1,0:T(8,128)S(1)}, f32[64,256]{1,0:T(8,128)S(1)}, u32[]{:S(2)}, u32[]{:S(2)}) collective-permute-start(f32[64,256]{1,0:T(8,128)S(1)} %select_add_fusion), channel_id=1, source_target_pairs={{0,4},{1,5},{2,6},{3,7},{4,0},{5,1},{6,2},{7,3},{8,12},{9,13},{10,... | collective-permute-start | bytes 196616 | tf_op jit(solution)/shard_map/ppermute | solution.py:36
  88.4 7.2 %copy-start.2 = (f32[608,256]{1,0:T(8,128)S(1)}, f32[608,256]{1,0:T(8,128)}, u32[]{:S(2)}) copy-start(f32[608,256]{1,0:T(8,128)} %copy-done.1) | copy-start | bytes 1867780
  88.4 7.7 %collective-permute-start.22 = (f32[64,256]{1,0:T(8,128)S(1)}, f32[64,256]{1,0:T(8,128)S(1)}, u32[]{:S(2)}, u32[]{:S(2)}) collective-permute-start(f32[64,256]{1,0:T(8,128)S(1)} %add_add_fusion.1), channel_id=1, source_target_pairs={{0,8},{1,9},{2,10},{3,11},{4,12},{5,13},{6,14},{7,15},{8,0},{9,1},... | collective-permute-start | bytes 196616 | tf_op jit(solution)/shard_map/ppermute | solution.py:36
  88.5 7.6 %collective-permute-start.23 = (f32[64,256]{1,0:T(8,128)S(1)}, f32[64,256]{1,0:T(8,128)S(1)}, u32[]{:S(2)}, u32[]{:S(2)}) collective-permute-start(f32[64,256]{1,0:T(8,128)S(1)} %add_add_fusion.1), channel_id=1, source_target_pairs={{0,24},{1,25},{2,26},{3,27},{4,28},{5,29},{6,30},{7,31},{8,16},{9,... | collective-permute-start | bytes 196616 | tf_op jit(solution)/shard_map/ppermute | solution.py:36
  90.0 6.1 %collective-permute-start.24 = (f32[64,256]{1,0:T(8,128)S(1)}, f32[64,256]{1,0:T(8,128)S(1)}, u32[]{:S(2)}, u32[]{:S(2)}) collective-permute-start(f32[64,256]{1,0:T(8,128)S(1)} %add_add_fusion.1), channel_id=1, source_target_pairs={{0,16},{1,17},{2,18},{3,19},{4,20},{5,21},{6,22},{7,23},{8,24},{9,... | collective-permute-start | bytes 196616 | tf_op jit(solution)/shard_map/ppermute | solution.py:36
  96.1 3.0 %collective-permute-start.25 = (f32[64,256]{1,0:T(8,128)S(1)}, f32[64,256]{1,0:T(8,128)S(1)}, u32[]{:S(2)}, u32[]{:S(2)}) collective-permute-start(f32[64,256]{1,0:T(8,128)S(1)} %add_add_fusion), channel_id=1, source_target_pairs={{0,1},{1,0},{2,3},{3,2},{4,5},{5,4},{6,7},{7,6},{8,9},{9,8},{10,11... | collective-permute-start | bytes 196616 | tf_op jit(solution)/shard_map/ppermute | solution.py:36
  99.0 1.3 %collective-permute-start.21 = (f32[128,256]{1,0:T(8,128)S(1)}, f32[128,256]{1,0:T(8,128)S(1)}, u32[]{:S(2)}, u32[]{:S(2)}) collective-permute-start(f32[128,256]{1,0:T(8,128)S(1)} %fusion.8), channel_id=1, source_target_pairs={{0,1},{1,0},{2,3},{3,2},{4,5},{5,4},{6,7},{7,6},{8,9},{9,8},{10,11... | collective-permute-start | bytes 393224 | tf_op jit(solution)/shard_map/ppermute | solution.py:36

commit v2 on v1

--- a/solution.py
+++ b/solution.py
@@ -126,7 +126,7 @@
 
     def copies(u):
         block, row = units[u][:2]
-        slot, half = u // 2, u % 2
+        slot, half = u // 2 % (AHEAD + 1), u % 2
         columns = pl.ds(pl.multiple_of(window_tile(leaves[u]) * LANES, LANES), WINDOW)
         rows = pl.ds(pl.multiple_of(half * WINDOW + window_place(leaves[u]), 32), ROWS)
         return (
@@ -138,9 +138,9 @@
 
     def begin(slot):
         for u in (2 * slot, 2 * slot + 1):
-            edge = (u % 2) * WINDOW
-            right_buf[slot, edge : edge + PLACES[-1], :] = jnp.zeros((PLACES[-1], SAMPLES), BF)
-            right_buf[slot, edge + ROWS : edge + WINDOW, :] = jnp.zeros((WINDOW - ROWS, SAMPLES), BF)
+            edge, into = (u % 2) * WINDOW, slot % (AHEAD + 1)
+            right_buf[into, edge : edge + PLACES[-1], :] = jnp.zeros((PLACES[-1], SAMPLES), BF)
+            right_buf[into, edge + ROWS : edge + WINDOW, :] = jnp.zeros((WINDOW - ROWS, SAMPLES), BF)
             for copy in copies(u):
                 copy.start()
 
@@ -155,11 +155,11 @@
             begin(slot + AHEAD)
         at = 0
         for kind in [0] * plain + [1] * masked:
-            left = left_buf[slot]
+            left = left_buf[slot % (AHEAD + 1)]
             if kind:
                 keep = [keep_ref[pl.ds(leaves[2 * slot + half], 1), :].astype(BF) for half in range(2)]
                 left = left * jnp.concatenate(keep, axis=1)
-            value = jnp.dot(left, right_buf[slot], preferred_element_type=F32)
+            value = jnp.dot(left, right_buf[slot % (AHEAD + 1)], preferred_element_type=F32)
             rows = pl.ds(at, ROWS)
             if slot:
                 out_ref[rows, :] += value
@@ -184,8 +184,8 @@
             in_specs=[anywhere, whole(keep)] + [anywhere] * len(blocks) + ([] if start is None else [whole(start)]),
             out_specs=whole(out),
             scratch_shapes=[
-                pltpu.VMEM((len(units) // 2, ROWS, 2 * WINDOW), BF),
-                pltpu.VMEM((len(units) // 2, 2 * WINDOW, SAMPLES), BF),
+                pltpu.VMEM((AHEAD + 1, ROWS, 2 * WINDOW), BF),
+                pltpu.VMEM((AHEAD + 1, 2 * WINDOW, SAMPLES), BF),
                 pltpu.SemaphoreType.DMA((len(units), 2)),
             ],
         ),
@@ -253,8 +253,6 @@
 
     own = samples[0]
     turned = [own] + [shifted(own, first(turn)) for turn in (1, 2, 3)]
-    lines = [jnp.stack(turned[:2]), jnp.stack(turned[2:])]
-
     root_slot, keep = fates(myself, merge_select[0], skeletons)
 
     groups = CHILD // LANES
@@ -274,11 +272,10 @@
     root_hits = (root_ids[:, None] == my_targets[None, :]).astype(BF)
     root_arrivals = jnp.dot(root_hits, child_rows[0], preferred_element_type=F32)
 
-    lines, outgoing = lax.optimization_barrier((lines, outgoing))
+    turned, keep, outgoing, root_arrivals = lax.optimization_barrier((turned, keep, outgoing, root_arrivals))
+    lines = [jnp.stack(turned[:2]), jnp.stack(turned[2:])]
     far_a = shifted(lines[0], second(2))
     near_b = shifted(lines[1], second(1))
-    near_a = shifted(lines[0], second(1))
-    far_b = shifted(lines[1], second(2))
 
     def both(block, step, turn):
         return [(block, 0, step, turn), (shifted(block, cores), 1, step, turn)]
@@ -286,17 +283,20 @@
     parts = both(lines[0], 0, 0) + both(lines[1], 0, 2)
     total = products(front, myself, keep, parts)
     yours = parts[1][0][0]
-    far_a, near_b, outgoing, total = lax.optimization_barrier((far_a, near_b, outgoing, total))
+    far_a, near_b, lines, total = lax.optimization_barrier((far_a, near_b, lines, total))
+    opposite = [shifted(far_a, second(1)), shifted(near_b, second(2))]
+    near_a = shifted(lines[0], second(1))
+    far_b = shifted(lines[1], second(2))
+    total = products(front, myself, keep, both(far_a, 2, 0) + both(near_b, 1, 2), total)
+    outgoing, near_a, far_b, total = lax.optimization_barrier((outgoing, near_a, far_b, total))
     incoming = lax.all_to_all(
         outgoing.reshape(leaf_total, CAP, SAMPLES), "hss", split_axis=0, concat_axis=0, tiled=True
     ).reshape(leaf_total * CAP, SAMPLES)
-    opposite = [shifted(far_a, second(1)), shifted(near_b, second(2))]
-    parts = both(far_a, 2, 0) + both(near_b, 1, 2) + both(near_a, 1, 0) + both(far_b, 2, 2)
-    total = products(front, myself, keep, parts, total)
+    total = products(front, myself, keep, both(near_a, 1, 0) + both(far_b, 2, 2), total)
     opposite, total = lax.optimization_barrier((opposite, total))
+    total = products(front, myself, keep, both(opposite[0], 3, 0) + both(opposite[1], 3, 2), total)
+    total, incoming = lax.optimization_barrier((total, incoming))
     full, root = total[:ROWS], total[ROWS:]
-    parts = both(opposite[0], 3, 0) + both(opposite[1], 3, 2)
-    root = products(front, myself, keep, parts, root, plain=False)
     my_root_slot = pick_index(root_slot, myself)
     my_skeleton = pick_index(skeletons, myself)
     root_rows = jnp.sum(jnp.where(my_root_slot[:, None] == iota(RANK)[None, :] + 1, my_skeleton[:, None] + 1, 0), axis=0) - 1
@@ -306,11 +306,9 @@
     half = RANK // 2
     kept = jnp.where(side == 0, root[:half], root[half:])
     kept = kept + shifted(jnp.where(side == 0, root[half:], root[:half]), cores)
-    kept, full = lax.optimization_barrier((kept, full))
-    full = products(front, myself, keep, parts[:2], full, masked=False)
+    kept, owners, targets, incoming = lax.optimization_barrier((kept, owners, targets, incoming))
     kept = total_over_ring(kept, along_z)
-    kept, full = lax.optimization_barrier((kept, full))
-    full = products(front, myself, keep, parts[2:], full, masked=False)
+    kept, yours = lax.optimization_barrier((kept, yours))
     kept = total_over_ring(kept, along_x)
     other = shifted(kept, cores)
     root = jnp.concatenate([jnp.where(side == 0, kept, other), jnp.where(side == 0, other, kept)], axis=0)

time: 102 us -> 92.2 us (0.904)
  Pallas kernels: 36.4 us -> 30.5 us
  local copies, waits for them, and re-layouts: 5.37 us -> 1.57 us
  starting transfers between devices: 32.3 us -> 35.3 us
  other arithmetic: 8.99 us -> 7.61 us
  matrix products: 6.77 us -> 5.49 us
    pallas_call x5 -> x4, Pallas kernels: 31.2 us -> 25.3 us  [products(): pl.pallas_call(functools.partial(product_kernel, units, plain, masked, st...]
    ppermute x26, waiting for transfers between devices: 4.66 us -> 9.18 us  [shifted(): lax.ppermute(x, 'hss', [(i, move(i)) for i in range(lax.axis_size('hss'))])]
    all_to_all x1, waiting for transfers between devices: 5.42 us -> 1.12 us  [body(): lax.all_to_all(outgoing.reshape(leaf_total, CAP, SAMPLES), 'hss', split_a...]
    unnamed x29 -> x11, local copies, waits for them, and re-layouts: 5.19 us -> 1.47 us
    ppermute x26, starting transfers between devices: 26.8 us -> 29.6 us  [shifted(): lax.ppermute(x, 'hss', [(i, move(i)) for i in range(lax.axis_size('hss'))])]
  transfers between devices with their start and end apart: 27 -> 27, of which waited for: 4 -> 13; matrix products, arithmetic and copies ran while one was open for 16% -> 14% of each run, Pallas kernels for 36% -> 33%
where the time goes in v2:
time: 92.2 us; the launch traced here: 91.7 us
  starting transfers between devices  35.3 us (38%)
  Pallas kernels  30.5 us (33%)
  waiting for transfers between devices  10.3 us (11%)
  other arithmetic  7.61 us (8%)
  matrix products  5.49 us (6%)
  local copies, waits for them, and re-layouts  1.57 us (2%)
  between operations  0.94 us (1%)
    ppermute x26, starting transfers between devices, shifted(): lax.ppermute(x, 'hss', [(i, move(i)) for i in range(lax.axis_size('hss'))])  29.6 us
    pallas_call x4, Pallas kernels, products(): pl.pallas_call(functools.partial(product_kernel, units, plain, masked, st...  25.3 us
    ppermute x26, waiting for transfers between devices, shifted(): lax.ppermute(x, 'hss', [(i, move(i)) for i in range(lax.axis_size('hss'))])  9.18 us
    all_to_all x1, starting transfers between devices, body(): lax.all_to_all(outgoing.reshape(leaf_total, CAP, SAMPLES), 'hss', split_a...  5.68 us
    pallas_call x1, Pallas kernels, fates(): pl.pallas_call(fate_kernel, in_specs=[pl.BlockSpec(memory_space=pltpu.SME...  2.65 us
    pallas_call x1, Pallas kernels, pair_terms(): pl.pallas_call(pair_kernel, grid_spec=pltpu.PrefetchScalarGridSpec(num_sc...  2.55 us
    broadcast_in_dim x3, other arithmetic, body(): return (parent[None], pair[None], root[None])  2.14 us
    dot_general x1, matrix products, body(): full = full + jnp.dot(selector, incoming, preferred_element_type=F32)  2.11 us
  transfers between devices with their start and end apart: 27, of which 13 were waited for; matrix products, arithmetic and copies ran while one was open for 14% of the time, Pallas kernels for 33%

profile of v2, /device:TPU:1, one launch (start us, length us, event | category | flops | bytes accessed | tf_op | source)
XLA Modules:
  0.0 91.7 jit_solution(5037823027236975502)
XLA Ops:
  0.6 2.1 %collective-permute-start = (bf16[608,256]{1,0:T(8,128)(2,1)}, bf16[608,256]{1,0:T(8,128)(2,1)S(1)}, u32[]{:S(2)}, u32[]{:S(2)}) collective-permute-start(bf16[608,256]{1,0:T(8,128)(2,1)} %bitcast.47), channel_id=1, source_target_pairs={{0,2},{1,9},{2,0},{3,11},{4,6},{5,13},{6,4},{7,15},{8,10},{9,1},{1... | collective-permute-start | bytes 933896 | tf_op jit(solution)/shard_map/ppermute | solution.py:36
  2.8 1.8 %collective-permute-start.1 = (bf16[608,256]{1,0:T(8,128)(2,1)}, bf16[608,256]{1,0:T(8,128)(2,1)S(1)}, u32[]{:S(2)}, u32[]{:S(2)}) collective-permute-start(bf16[608,256]{1,0:T(8,128)(2,1)} %bitcast.48), channel_id=1, source_target_pairs={{0,6},{1,25},{2,4},{3,27},{4,2},{5,29},{6,0},{7,31},{8,14},{9,17},... | collective-permute-start | bytes 933896 | tf_op jit(solution)/shard_map/ppermute | solution.py:36
  4.6 0.6 collective-permute-start.2
  5.2 0.7 bitcast_add_fusion
  5.9 0.2 convert_reduce_fusion
  6.1 0.7 copy.15
  6.8 0.8 add_add_fusion.2
  7.6 0.7 copy-done.2
  8.3 2.6 %shard_map.94 = (s32[32,128]{1,0:T(8,128)S(1)}, f32[32,768]{1,0:T(8,128)S(1)}) custom-call(s32[1]{0:T(128)} %bitcast.me_ref, s32[31,128]{1,0:T(8,128)S(1)} %bitcast.52, s32[32,128]{1,0:T(8,128)S(1)} %bitcast.51), custom_call_target="tpu_custom_call" | custom-call | flops 33554432 | bytes 131072 | tf_op jit(solution)/shard_map/pallas_call | solution.py:96
  11.0 1.4 %select_reduce_fusion.1 = s32[128]{0:T(128)S(1)} fusion(s32[32,128]{1,0:T(8,128)S(1)} %add_add_fusion.2, s32[128]{0:T(128)S(1)} %iota_add_fusion, s32[32,128]{1,0:T(8,128)S(1)} %get-tuple-element.33), kind=kLoop, calls=%fused_computation.8 | loop fusion | flops 1572736 | bytes 33792 | tf_op jit(solution)/shard_map/reduce_sum | solution.py:269
  12.4 0.2 fusion.15
  12.7 1.8 %fusion.2 = bf16[2048,256]{1,0:T(8,128)(2,1)} fusion(s32[512]{0:T(512)S(1)} %multiply_add_fusion, bf16[1,512,256]{2,1,0:T(8,128)(2,1)S(1)} %copy-done), kind=kOutput, calls=%fused_computation.6 | convolution fusion | flops 538443776 | bytes 1312768 | tf_op jit(solution)/shard_map/dot_general | solution.py:267
  14.6 2.6 %collective-permute-start.6 = (bf16[2,608,256]{2,1,0:T(8,128)(2,1)S(1)}, bf16[2,608,256]{2,1,0:T(8,128)(2,1)S(1)}, u32[]{:S(2)}, u32[]{:S(2)}) collective-permute-start(bf16[2,608,256]{2,1,0:T(8,128)(2,1)S(1)} %pad_maximum_fusion.1.refs_2_), channel_id=1, source_target_pairs={{0,1},{1,0},{2,3},{3,2},{4,5},{5,4},{6,7},{7,6},{8,9},{9,8},{10,11... | collective-permute-start | bytes 1867784 | tf_op jit(solution)/shard_map/ppermute | solution.py:36
  17.2 0.1 collective-permute-start.5
  17.3 0.3 collective-permute-start.4
  17.6 2.2 %collective-permute-start.3 = (bf16[2,608,256]{2,1,0:T(8,128)(2,1)S(1)}, bf16[2,608,256]{2,1,0:T(8,128)(2,1)}, u32[]{:S(2)}, u32[]{:S(2)}) collective-permute-start(bf16[2,608,256]{2,1,0:T(8,128)(2,1)S(1)} %pad_maximum_fusion.refs_0_), channel_id=1, source_target_pairs={{0,24},{1,7},{2,26},{3,5},{4,28},{5,3},{6,30},{7,1},{8,16},{9,15},... | collective-permute-start | bytes 1867784 | tf_op jit(solution)/shard_map/ppermute | solution.py:36
  19.9 6.2 %shard_map.95.refs_4_ = f32[1216,256]{1,0:T(8,128)S(1)} custom-call(s32[1]{0:T(128)} %bitcast.me_ref, bf16[608,19456]{1,0:T(8,128)(2,1)} %bitcast.53, f32[32,768]{1,0:T(8,128)S(1)} %get-tuple-element.34.keep_ref, bf16[2,608,256]{2,1,0:T(8,128)(2,1)S(1)} %pad_maximum_fusion.refs_0_, bf16[2,608,256]{2,1,0:T(8,128)(2,1)S(1)} %collective-permute-done.5.refs_1_, ...), custom_call_target="tpu_custom_call" | custom-call | flops 3825205248 | bytes 7471104 | tf_op jit(solution)/shard_map/pallas_call | solution.py:179
  26.1 0.8 collective-permute-done.4.refs_2_
  26.9 1.4 %collective-permute-done.3.refs_0_ = bf16[2,608,256]{2,1,0:T(8,128)(2,1)} collective-permute-done((bf16[2,608,256]{2,1,0:T(8,128)(2,1)S(1)}, bf16[2,608,256]{2,1,0:T(8,128)(2,1)}, u32[]{:S(2)}, u32[]{:S(2)}) %collective-permute-start.3) | collective-permute-done | bytes 622624 | tf_op jit(solution)/shard_map/ppermute | solution.py:36
  28.3 2.5 %collective-permute-start.11 = (bf16[2,608,256]{2,1,0:T(8,128)(2,1)}, bf16[2,608,256]{2,1,0:T(8,128)(2,1)S(1)}, u32[]{:S(2)}, u32[]{:S(2)}) collective-permute-start(bf16[2,608,256]{2,1,0:T(8,128)(2,1)} %collective-permute-done.3.refs_0_), channel_id=1, source_target_pairs={{0,1},{1,0},{2,3},{3,2},{4,5},{5,4},{6,7},{7,6},{8,9},{9,8},{10,11... | collective-permute-start | bytes 1867784 | tf_op jit(solution)/shard_map/ppermute | solution.py:36
  30.9 2.3 %collective-permute-start.10 = (bf16[2,608,256]{2,1,0:T(8,128)(2,1)S(1)}, bf16[2,608,256]{2,1,0:T(8,128)(2,1)}, u32[]{:S(2)}, u32[]{:S(2)}) collective-permute-start(bf16[2,608,256]{2,1,0:T(8,128)(2,1)S(1)} %pad_maximum_fusion.1.refs_2_), channel_id=1, source_target_pairs={{0,24},{1,7},{2,26},{3,5},{4,28},{5,3},{6,30},{7,1},{8,16},{9,15},... | collective-permute-start | bytes 1867784 | tf_op jit(solution)/shard_map/ppermute | solution.py:36
  33.2 0.4 collective-permute-done.11.refs_1_
  33.6 6.5 %shard_map.96.refs_4_ = f32[1216,256]{1,0:T(8,128)S(1)} custom-call(s32[1]{0:T(128)} %bitcast.me_ref, bf16[608,19456]{1,0:T(8,128)(2,1)} %bitcast.54, f32[32,768]{1,0:T(8,128)S(1)} %get-tuple-element.34.keep_ref, bf16[2,608,256]{2,1,0:T(8,128)(2,1)} %collective-permute-done.3.refs_0_, ...), custom_call_target="tpu_custom_call", output_to_operand_aliasing={{}: (7, {})} | custom-call | flops 3825205248 | bytes 7471104 | tf_op jit(solution)/shard_map/pallas_call | solution.py:179
  40.1 1.4 %collective-permute-done.10.refs_2_ = bf16[2,608,256]{2,1,0:T(8,128)(2,1)} collective-permute-done((bf16[2,608,256]{2,1,0:T(8,128)(2,1)S(1)}, bf16[2,608,256]{2,1,0:T(8,128)(2,1)}, u32[]{:S(2)}, u32[]{:S(2)}) %collective-permute-start.10) | collective-permute-done | bytes 622624 | tf_op jit(solution)/shard_map/ppermute | solution.py:36
  41.6 1.1 %collective-permute-done.9.refs_0_ = bf16[2,608,256]{2,1,0:T(8,128)(2,1)} collective-permute-done((bf16[2,608,256]{2,1,0:T(8,128)(2,1)S(1)}, bf16[2,608,256]{2,1,0:T(8,128)(2,1)}, u32[]{:S(2)}, u32[]{:S(2)}) %collective-permute-start.9) | collective-permute-done | bytes 622624 | tf_op jit(solution)/shard_map/ppermute | solution.py:36
  42.7 1.1 %collective-permute-start.13 = (bf16[2,608,256]{2,1,0:T(8,128)(2,1)}, bf16[2,608,256]{2,1,0:T(8,128)(2,1)}, u32[]{:S(2)}, u32[]{:S(2)}) collective-permute-start(bf16[2,608,256]{2,1,0:T(8,128)(2,1)} %collective-permute-done.9.refs_0_), channel_id=1, source_target_pairs={{0,1},{1,0},{2,3},{3,2},{4,5},{5,4},{6,7},{7,6},{8,9},{9,8},{10,11... | collective-permute-start | bytes 1867784 | tf_op jit(solution)/shard_map/ppermute | solution.py:36
  43.8 0.2 collective-permute-start.7
  44.0 2.2 %collective-permute-start.8 = (bf16[2,608,256]{2,1,0:T(8,128)(2,1)S(1)}, bf16[2,608,256]{2,1,0:T(8,128)(2,1)}, u32[]{:S(2)}, u32[]{:S(2)}) collective-permute-start(bf16[2,608,256]{2,1,0:T(8,128)(2,1)S(1)} %collective-permute-done.4.refs_2_), channel_id=1, source_target_pairs={{0,24},{1,7},{2,26},{3,5},{4,28},{5,3},{6,30},{7,1},{8,16},{9,15},... | collective-permute-start | bytes 1867784 | tf_op jit(solution)/shard_map/ppermute | solution.py:36
  46.3 5.7 %all-to-all-start = ((bf16[32,64,256]{2,1,0:T(8,128)(2,1)}), bf16[32,64,256]{2,1,0:T(8,128)(2,1)}, u32[]{:S(2)}, u32[]{:S(2)}) async-start(bf16[32,64,256]{2,1,0:T(8,128)(2,1)} %bitcast.58), calls=%async_computation | async-start | bytes 2097152 | tf_op jit(solution)/shard_map/all_to_all | solution.py:292
  52.0 6.2 %shard_map.97.refs_4_ = f32[1216,256]{1,0:T(8,128)S(1)} custom-call(s32[1]{0:T(128)} %bitcast.me_ref, bf16[608,19456]{1,0:T(8,128)(2,1)} %bitcast.55, f32[32,768]{1,0:T(8,128)S(1)} %get-tuple-element.34.keep_ref, bf16[2,608,256]{2,1,0:T(8,128)(2,1)} %collective-permute-done.9.refs_0_, ...), custom_call_target="tpu_custom_call", output_to_operand_aliasing={{}: (7, {})} | custom-call | flops 3825205248 | bytes 7471104 | tf_op jit(solution)/shard_map/pallas_call | solution.py:179
  58.2 0.4 collective-permute-start.15
  58.6 0.2 collective-permute-start.16
  58.8 0.8 fusion.34
  59.6 0.7 fusion.36
  60.2 0.1 select_reduce_fusion.2
  60.4 0.2 collective-permute-done.15.refs_1_
  60.6 0.9 collective-permute-done.16.refs_3_
  61.4 6.4 %shard_map.98 = f32[1216,256]{1,0:T(8,128)S(1)} custom-call(s32[1]{0:T(128)} %bitcast.me_ref, bf16[608,19456]{1,0:T(8,128)(2,1)} %bitcast.56, f32[32,768]{1,0:T(8,128)S(1)} %get-tuple-element.34.keep_ref, bf16[2,608,256]{2,1,0:T(8,128)(2,1)} %collective-permute-done.7.refs_0_, ...), custom_call_target="tpu_custom_call", output_to_operand_aliasing={{}: (7, {})} | custom-call | flops 3825205248 | bytes 7471104 | tf_op jit(solution)/shard_map/pallas_call | solution.py:179
  67.8 1.1 %all-to-all-done = bf16[32,64,256]{2,1,0:T(8,128)(2,1)} async-done(((bf16[32,64,256]{2,1,0:T(8,128)(2,1)}), bf16[32,64,256]{2,1,0:T(8,128)(2,1)}, u32[]{:S(2)}, u32[]{:S(2)}) %all-to-all-start) | async-done | bytes 1048608 | tf_op jit(solution)/shard_map/all_to_all | solution.py:292
  68.9 0.4 fusion.12
  69.4 0.2 collective-permute-start.17
  69.6 1.1 %collective-permute-done.17 = f32[64,256]{1,0:T(8,128)S(1)} collective-permute-done((f32[64,256]{1,0:T(8,128)S(1)}, f32[64,256]{1,0:T(8,128)S(1)}, u32[]{:S(2)}, u32[]{:S(2)}) %collective-permute-start.17) | collective-permute-done | bytes 65568 | tf_op jit(solution)/shard_map/ppermute | solution.py:36
  70.7 0.4 collective-permute-start.18
  71.1 1.8 %collective-permute-start.19 = (f32[64,256]{1,0:T(8,128)S(1)}, f32[64,256]{1,0:T(8,128)S(1)}, u32[]{:S(2)}, u32[]{:S(2)}) collective-permute-start(f32[64,256]{1,0:T(8,128)S(1)} %select_add_fusion), channel_id=1, source_target_pairs={{0,6},{1,7},{2,4},{3,5},{4,2},{5,3},{6,0},{7,1},{8,14},{9,15},{10,... | collective-permute-start | bytes 196616 | tf_op jit(solution)/shard_map/ppermute | solution.py:36
  72.9 1.1 %collective-permute-start.20 = (f32[64,256]{1,0:T(8,128)S(1)}, f32[64,256]{1,0:T(8,128)S(1)}, u32[]{:S(2)}, u32[]{:S(2)}) collective-permute-start(f32[64,256]{1,0:T(8,128)S(1)} %select_add_fusion), channel_id=1, source_target_pairs={{0,4},{1,5},{2,6},{3,7},{4,0},{5,1},{6,2},{7,3},{8,12},{9,13},{10,... | collective-permute-start | bytes 196616 | tf_op jit(solution)/shard_map/ppermute | solution.py:36
  74.1 0.1 fusion.23
  74.3 0.3 fusion.6
  74.5 0.6 select_reduce_fusion
  75.2 0.1 sub.45
  75.3 2.1 %fusion = f32[608,256]{1,0:T(8,128)S(1)} fusion(bf16[2048,256]{1,0:T(8,128)(2,1)} %bitcast.14, s32[2048]{0:T(1024)S(1)} %sub.45), kind=kOutput, calls=%fused_computation.1 | convolution fusion | flops 638779392 | bytes 1679360 | tf_op jit(solution)/shard_map/dot_general | solution.py:326
  77.4 0.2 collective-permute-done.20
  77.6 1.3 %collective-permute-start.22 = (f32[64,256]{1,0:T(8,128)S(1)}, f32[64,256]{1,0:T(8,128)S(1)}, u32[]{:S(2)}, u32[]{:S(2)}) collective-permute-start(f32[64,256]{1,0:T(8,128)S(1)} %add_add_fusion.1), channel_id=1, source_target_pairs={{0,8},{1,9},{2,10},{3,11},{4,12},{5,13},{6,14},{7,15},{8,0},{9,1},... | collective-permute-start | bytes 196616 | tf_op jit(solution)/shard_map/ppermute | solution.py:36
  78.8 1.8 %collective-permute-start.23 = (f32[64,256]{1,0:T(8,128)S(1)}, f32[64,256]{1,0:T(8,128)S(1)}, u32[]{:S(2)}, u32[]{:S(2)}) collective-permute-start(f32[64,256]{1,0:T(8,128)S(1)} %add_add_fusion.1), channel_id=1, source_target_pairs={{0,24},{1,25},{2,26},{3,27},{4,28},{5,29},{6,30},{7,31},{8,16},{9,... | collective-permute-start | bytes 196616 | tf_op jit(solution)/shard_map/ppermute | solution.py:36
  80.6 0.7 collective-permute-start.24
  81.3 0.8 convert_bitcast_fusion
  82.1 2.5 %shard_map.99 = f32[608,256]{1,0:T(8,128)S(1)} custom-call(s32[1]{0:T(128)} %bitcast.me_ref, bf16[608,19456]{1,0:T(8,128)(2,1)} %bitcast.57, bf16[608,256]{1,0:T(8,128)(2,1)S(1)} %bitcast.50, bf16[608,256]{1,0:T(8,128)(2,1)S(1)} %slice_bitcast_fusion.yours_ref, s32[1,128]{1,0:T(1,128)S(1)} %get-tuple-element.67.names_ref), custom_call_target="tpu_custom_call" | custom-call | flops 478150656 | bytes 1867776 | tf_op jit(solution)/shard_map/pallas_call | solution.py:228
  84.7 1.0 %collective-permute-done.24 = f32[64,256]{1,0:T(8,128)S(1)} collective-permute-done((f32[64,256]{1,0:T(8,128)S(1)}, f32[64,256]{1,0:T(8,128)S(1)}, u32[]{:S(2)}, u32[]{:S(2)}) %collective-permute-start.24) | collective-permute-done | bytes 65568 | tf_op jit(solution)/shard_map/ppermute | solution.py:36
  85.7 3.4 %collective-permute-start.25 = (f32[64,256]{1,0:T(8,128)S(1)}, f32[64,256]{1,0:T(8,128)S(1)}, u32[]{:S(2)}, u32[]{:S(2)}) collective-permute-start(f32[64,256]{1,0:T(8,128)S(1)} %add_add_fusion), channel_id=1, source_target_pairs={{0,1},{1,0},{2,3},{3,2},{4,5},{5,4},{6,7},{7,6},{8,9},{9,8},{10,11... | collective-permute-start | bytes 196616 | tf_op jit(solution)/shard_map/ppermute | solution.py:36
  89.1 0.5 fusion.8
  89.6 0.1 collective-permute-start.21
  89.7 0.3 collective-permute-done.25
  90.0 0.7 maximum_bitcast_fusion
  90.7 0.3 collective-permute-done.21
  91.0 0.7 add_bitcast_fusion
  (44 shorter events, 0.3 us)
Async XLA Ops:
  0.6 11.8 %copy-start = (bf16[1,512,256]{2,1,0:T(8,128)(2,1)S(1)}, bf16[1,512,256]{2,1,0:T(8,128)(2,1)}, u32[]{:S(2)}) copy-start(bf16[1,512,256]{2,1,0:T(8,128)(2,1)} %param.9) | copy-start | bytes 786436
  0.6 13.9 %collective-permute-start = (bf16[608,256]{1,0:T(8,128)(2,1)}, bf16[608,256]{1,0:T(8,128)(2,1)S(1)}, u32[]{:S(2)}, u32[]{:S(2)}) collective-permute-start(bf16[608,256]{1,0:T(8,128)(2,1)} %bitcast.47), channel_id=1, source_target_pairs={{0,2},{1,9},{2,0},{3,11},{4,6},{5,13},{6,4},{7,15},{8,10},{9,1},{1... | collective-permute-start | bytes 933896 | tf_op jit(solution)/shard_map/ppermute | solution.py:36
  2.8 11.7 %collective-permute-start.1 = (bf16[608,256]{1,0:T(8,128)(2,1)}, bf16[608,256]{1,0:T(8,128)(2,1)S(1)}, u32[]{:S(2)}, u32[]{:S(2)}) collective-permute-start(bf16[608,256]{1,0:T(8,128)(2,1)} %bitcast.48), channel_id=1, source_target_pairs={{0,6},{1,25},{2,4},{3,27},{4,2},{5,29},{6,0},{7,31},{8,14},{9,17},... | collective-permute-start | bytes 933896 | tf_op jit(solution)/shard_map/ppermute | solution.py:36
  4.6 9.9 %collective-permute-start.2 = (bf16[608,256]{1,0:T(8,128)(2,1)}, bf16[608,256]{1,0:T(8,128)(2,1)S(1)}, u32[]{:S(2)}, u32[]{:S(2)}) collective-permute-start(bf16[608,256]{1,0:T(8,128)(2,1)} %bitcast.49), channel_id=1, source_target_pairs={{0,4},{1,17},{2,6},{3,19},{4,0},{5,21},{6,2},{7,23},{8,12},{9,25},... | collective-permute-start | bytes 933896 | tf_op jit(solution)/shard_map/ppermute | solution.py:36
  7.6 0.7 copy-start.2
  12.7 4.5 %copy-start.1 = (bf16[1,608,256]{2,1,0:T(8,128)(2,1)S(1)}, bf16[1,608,256]{2,1,0:T(8,128)(2,1)}, u32[]{:S(2)}) copy-start(bf16[1,608,256]{2,1,0:T(8,128)(2,1)} %param.8) | copy-start | bytes 933892
  14.6 5.3 %collective-permute-start.6 = (bf16[2,608,256]{2,1,0:T(8,128)(2,1)S(1)}, bf16[2,608,256]{2,1,0:T(8,128)(2,1)S(1)}, u32[]{:S(2)}, u32[]{:S(2)}) collective-permute-start(bf16[2,608,256]{2,1,0:T(8,128)(2,1)S(1)} %pad_maximum_fusion.1.refs_2_), channel_id=1, source_target_pairs={{0,1},{1,0},{2,3},{3,2},{4,5},{5,4},{6,7},{7,6},{8,9},{9,8},{10,11... | collective-permute-start | bytes 1867784 | tf_op jit(solution)/shard_map/ppermute | solution.py:36
  17.2 2.7 %collective-permute-start.5 = (bf16[2,608,256]{2,1,0:T(8,128)(2,1)S(1)}, bf16[2,608,256]{2,1,0:T(8,128)(2,1)S(1)}, u32[]{:S(2)}, u32[]{:S(2)}) collective-permute-start(bf16[2,608,256]{2,1,0:T(8,128)(2,1)S(1)} %pad_maximum_fusion.refs_0_), channel_id=1, source_target_pairs={{0,1},{1,0},{2,3},{3,2},{4,5},{5,4},{6,7},{7,6},{8,9},{9,8},{10,11... | collective-permute-start | bytes 1867784 | tf_op jit(solution)/shard_map/ppermute | solution.py:36
  17.3 9.6 %collective-permute-start.4 = (bf16[2,608,256]{2,1,0:T(8,128)(2,1)S(1)}, bf16[2,608,256]{2,1,0:T(8,128)(2,1)S(1)}, u32[]{:S(2)}, u32[]{:S(2)}) collective-permute-start(bf16[2,608,256]{2,1,0:T(8,128)(2,1)S(1)} %pad_maximum_fusion.1.refs_2_), channel_id=1, source_target_pairs={{0,8},{1,3},{2,10},{3,1},{4,12},{5,7},{6,14},{7,5},{8,0},{9,11},{1... | collective-permute-start | bytes 1867784 | tf_op jit(solution)/shard_map/ppermute | solution.py:36
  17.6 10.7 %collective-permute-start.3 = (bf16[2,608,256]{2,1,0:T(8,128)(2,1)S(1)}, bf16[2,608,256]{2,1,0:T(8,128)(2,1)}, u32[]{:S(2)}, u32[]{:S(2)}) collective-permute-start(bf16[2,608,256]{2,1,0:T(8,128)(2,1)S(1)} %pad_maximum_fusion.refs_0_), channel_id=1, source_target_pairs={{0,24},{1,7},{2,26},{3,5},{4,28},{5,3},{6,30},{7,1},{8,16},{9,15},... | collective-permute-start | bytes 1867784 | tf_op jit(solution)/shard_map/ppermute | solution.py:36
  28.3 5.3 %collective-permute-start.11 = (bf16[2,608,256]{2,1,0:T(8,128)(2,1)}, bf16[2,608,256]{2,1,0:T(8,128)(2,1)S(1)}, u32[]{:S(2)}, u32[]{:S(2)}) collective-permute-start(bf16[2,608,256]{2,1,0:T(8,128)(2,1)} %collective-permute-done.3.refs_0_), channel_id=1, source_target_pairs={{0,1},{1,0},{2,3},{3,2},{4,5},{5,4},{6,7},{7,6},{8,9},{9,8},{10,11... | collective-permute-start | bytes 1867784 | tf_op jit(solution)/shard_map/ppermute | solution.py:36
  30.9 2.7 %collective-permute-start.12 = (bf16[2,608,256]{2,1,0:T(8,128)(2,1)S(1)}, bf16[2,608,256]{2,1,0:T(8,128)(2,1)S(1)}, u32[]{:S(2)}, u32[]{:S(2)}) collective-permute-start(bf16[2,608,256]{2,1,0:T(8,128)(2,1)S(1)} %collective-permute-done.4.refs_2_), channel_id=1, source_target_pairs={{0,1},{1,0},{2,3},{3,2},{4,5},{5,4},{6,7},{7,6},{8,9},{9,8},{10,11... | collective-permute-start | bytes 1867784 | tf_op jit(solution)/shard_map/ppermute | solution.py:36
  30.9 10.7 %collective-permute-start.10 = (bf16[2,608,256]{2,1,0:T(8,128)(2,1)S(1)}, bf16[2,608,256]{2,1,0:T(8,128)(2,1)}, u32[]{:S(2)}, u32[]{:S(2)}) collective-permute-start(bf16[2,608,256]{2,1,0:T(8,128)(2,1)S(1)} %pad_maximum_fusion.1.refs_2_), channel_id=1, source_target_pairs={{0,24},{1,7},{2,26},{3,5},{4,28},{5,3},{6,30},{7,1},{8,16},{9,15},... | collective-permute-start | bytes 1867784 | tf_op jit(solution)/shard_map/ppermute | solution.py:36
  33.2 9.5 %collective-permute-start.9 = (bf16[2,608,256]{2,1,0:T(8,128)(2,1)S(1)}, bf16[2,608,256]{2,1,0:T(8,128)(2,1)}, u32[]{:S(2)}, u32[]{:S(2)}) collective-permute-start(bf16[2,608,256]{2,1,0:T(8,128)(2,1)S(1)} %pad_maximum_fusion.refs_0_), channel_id=1, source_target_pairs={{0,8},{1,3},{2,10},{3,1},{4,12},{5,7},{6,14},{7,5},{8,0},{9,11},{1... | collective-permute-start | bytes 1867784 | tf_op jit(solution)/shard_map/ppermute | solution.py:36
  42.7 9.3 %collective-permute-start.13 = (bf16[2,608,256]{2,1,0:T(8,128)(2,1)}, bf16[2,608,256]{2,1,0:T(8,128)(2,1)}, u32[]{:S(2)}, u32[]{:S(2)}) collective-permute-start(bf16[2,608,256]{2,1,0:T(8,128)(2,1)} %collective-permute-done.9.refs_0_), channel_id=1, source_target_pairs={{0,1},{1,0},{2,3},{3,2},{4,5},{5,4},{6,7},{7,6},{8,9},{9,8},{10,11... | collective-permute-start | bytes 1867784 | tf_op jit(solution)/shard_map/ppermute | solution.py:36
  43.8 8.2 %collective-permute-start.14 = (bf16[2,608,256]{2,1,0:T(8,128)(2,1)}, bf16[2,608,256]{2,1,0:T(8,128)(2,1)}, u32[]{:S(2)}, u32[]{:S(2)}) collective-permute-start(bf16[2,608,256]{2,1,0:T(8,128)(2,1)} %collective-permute-done.10.refs_2_), channel_id=1, source_target_pairs={{0,1},{1,0},{2,3},{3,2},{4,5},{5,4},{6,7},{7,6},{8,9},{9,8},{10,11... | collective-permute-start | bytes 1867784 | tf_op jit(solution)/shard_map/ppermute | solution.py:36
  43.8 14.4 %collective-permute-start.7 = (bf16[2,608,256]{2,1,0:T(8,128)(2,1)}, bf16[2,608,256]{2,1,0:T(8,128)(2,1)}, u32[]{:S(2)}, u32[]{:S(2)}) collective-permute-start(bf16[2,608,256]{2,1,0:T(8,128)(2,1)} %collective-permute-done.3.refs_0_), channel_id=1, source_target_pairs={{0,8},{1,3},{2,10},{3,1},{4,12},{5,7},{6,14},{7,5},{8,0},{9,11},{1... | collective-permute-start | bytes 1867784 | tf_op jit(solution)/shard_map/ppermute | solution.py:36
  44.0 14.2 %collective-permute-start.8 = (bf16[2,608,256]{2,1,0:T(8,128)(2,1)S(1)}, bf16[2,608,256]{2,1,0:T(8,128)(2,1)}, u32[]{:S(2)}, u32[]{:S(2)}) collective-permute-start(bf16[2,608,256]{2,1,0:T(8,128)(2,1)S(1)} %collective-permute-done.4.refs_2_), channel_id=1, source_target_pairs={{0,24},{1,7},{2,26},{3,5},{4,28},{5,3},{6,30},{7,1},{8,16},{9,15},... | collective-permute-start | bytes 1867784 | tf_op jit(solution)/shard_map/ppermute | solution.py:36
  46.3 22.6 %all-to-all-start = ((bf16[32,64,256]{2,1,0:T(8,128)(2,1)}), bf16[32,64,256]{2,1,0:T(8,128)(2,1)}, u32[]{:S(2)}, u32[]{:S(2)}) async-start(bf16[32,64,256]{2,1,0:T(8,128)(2,1)} %bitcast.58), calls=%async_computation | async-start | bytes 2097152 | tf_op jit(solution)/shard_map/all_to_all | solution.py:292
  58.2 2.3 %collective-permute-start.15 = (bf16[2,608,256]{2,1,0:T(8,128)(2,1)}, bf16[2,608,256]{2,1,0:T(8,128)(2,1)S(1)}, u32[]{:S(2)}, u32[]{:S(2)}) collective-permute-start(bf16[2,608,256]{2,1,0:T(8,128)(2,1)} %collective-permute-done.7.refs_0_), channel_id=1, source_target_pairs={{0,1},{1,0},{2,3},{3,2},{4,5},{5,4},{6,7},{7,6},{8,9},{9,8},{10,11... | collective-permute-start | bytes 1867784 | tf_op jit(solution)/shard_map/ppermute | solution.py:36
  58.6 2.8 %collective-permute-start.16 = (bf16[2,608,256]{2,1,0:T(8,128)(2,1)}, bf16[2,608,256]{2,1,0:T(8,128)(2,1)S(1)}, u32[]{:S(2)}, u32[]{:S(2)}) collective-permute-start(bf16[2,608,256]{2,1,0:T(8,128)(2,1)} %collective-permute-done.8.refs_2_), channel_id=1, source_target_pairs={{0,1},{1,0},{2,3},{3,2},{4,5},{5,4},{6,7},{7,6},{8,9},{9,8},{10,11... | collective-permute-start | bytes 1867784 | tf_op jit(solution)/shard_map/ppermute | solution.py:36
  60.4 13.7 %copy-start.3 = (s32[1,16384,1]{1,2,0:T(1,128)S(1)}, s32[1,16384,1]{1,2,0:T(1,128)}, u32[]{:S(2)}) copy-start(s32[1,16384,1]{1,2,0:T(1,128)} %param.10) | copy-start | bytes 196612
  67.8 6.4 %copy-start.4 = (s32[1,16384]{1,0:T(1,128)S(1)}, s32[1,16384]{1,0:T(1,128)}, u32[]{:S(2)}) copy-start(s32[1,16384]{1,0:T(1,128)} %param.11) | copy-start | bytes 196612
  69.4 1.3 %collective-permute-start.17 = (f32[64,256]{1,0:T(8,128)S(1)}, f32[64,256]{1,0:T(8,128)S(1)}, u32[]{:S(2)}, u32[]{:S(2)}) collective-permute-start(f32[64,256]{1,0:T(8,128)S(1)} %slice_select_fusion), channel_id=1, source_target_pairs={{0,1},{1,0},{2,3},{3,2},{4,5},{5,4},{6,7},{7,6},{8,9},{9,8},{10,11... | collective-permute-start | bytes 196616 | tf_op jit(solution)/shard_map/ppermute | solution.py:36
  70.7 6.6 %collective-permute-start.18 = (f32[64,256]{1,0:T(8,128)S(1)}, f32[64,256]{1,0:T(8,128)S(1)}, u32[]{:S(2)}, u32[]{:S(2)}) collective-permute-start(f32[64,256]{1,0:T(8,128)S(1)} %select_add_fusion), channel_id=1, source_target_pairs={{0,2},{1,3},{2,0},{3,1},{4,6},{5,7},{6,4},{7,5},{8,10},{9,11},{10,... | collective-permute-start | bytes 196616 | tf_op jit(solution)/shard_map/ppermute | solution.py:36
  71.1 6.3 %collective-permute-start.19 = (f32[64,256]{1,0:T(8,128)S(1)}, f32[64,256]{1,0:T(8,128)S(1)}, u32[]{:S(2)}, u32[]{:S(2)}) collective-permute-start(f32[64,256]{1,0:T(8,128)S(1)} %select_add_fusion), channel_id=1, source_target_pairs={{0,6},{1,7},{2,4},{3,5},{4,2},{5,3},{6,0},{7,1},{8,14},{9,15},{10,... | collective-permute-start | bytes 196616 | tf_op jit(solution)/shard_map/ppermute | solution.py:36
  72.9 4.6 %collective-permute-start.20 = (f32[64,256]{1,0:T(8,128)S(1)}, f32[64,256]{1,0:T(8,128)S(1)}, u32[]{:S(2)}, u32[]{:S(2)}) collective-permute-start(f32[64,256]{1,0:T(8,128)S(1)} %select_add_fusion), channel_id=1, source_target_pairs={{0,4},{1,5},{2,6},{3,7},{4,0},{5,1},{6,2},{7,3},{8,12},{9,13},{10,... | collective-permute-start | bytes 196616 | tf_op jit(solution)/shard_map/ppermute | solution.py:36
  77.6 7.1 %collective-permute-start.22 = (f32[64,256]{1,0:T(8,128)S(1)}, f32[64,256]{1,0:T(8,128)S(1)}, u32[]{:S(2)}, u32[]{:S(2)}) collective-permute-start(f32[64,256]{1,0:T(8,128)S(1)} %add_add_fusion.1), channel_id=1, source_target_pairs={{0,8},{1,9},{2,10},{3,11},{4,12},{5,13},{6,14},{7,15},{8,0},{9,1},... | collective-permute-start | bytes 196616 | tf_op jit(solution)/shard_map/ppermute | solution.py:36
  78.8 5.8 %collective-permute-start.23 = (f32[64,256]{1,0:T(8,128)S(1)}, f32[64,256]{1,0:T(8,128)S(1)}, u32[]{:S(2)}, u32[]{:S(2)}) collective-permute-start(f32[64,256]{1,0:T(8,128)S(1)} %add_add_fusion.1), channel_id=1, source_target_pairs={{0,24},{1,25},{2,26},{3,27},{4,28},{5,29},{6,30},{7,31},{8,16},{9,... | collective-permute-start | bytes 196616 | tf_op jit(solution)/shard_map/ppermute | solution.py:36
  80.6 5.1 %collective-permute-start.24 = (f32[64,256]{1,0:T(8,128)S(1)}, f32[64,256]{1,0:T(8,128)S(1)}, u32[]{:S(2)}, u32[]{:S(2)}) collective-permute-start(f32[64,256]{1,0:T(8,128)S(1)} %add_add_fusion.1), channel_id=1, source_target_pairs={{0,16},{1,17},{2,18},{3,19},{4,20},{5,21},{6,22},{7,23},{8,24},{9,... | collective-permute-start | bytes 196616 | tf_op jit(solution)/shard_map/ppermute | solution.py:36
  85.7 4.3 %collective-permute-start.25 = (f32[64,256]{1,0:T(8,128)S(1)}, f32[64,256]{1,0:T(8,128)S(1)}, u32[]{:S(2)}, u32[]{:S(2)}) collective-permute-start(f32[64,256]{1,0:T(8,128)S(1)} %add_add_fusion), channel_id=1, source_target_pairs={{0,1},{1,0},{2,3},{3,2},{4,5},{5,4},{6,7},{7,6},{8,9},{9,8},{10,11... | collective-permute-start | bytes 196616 | tf_op jit(solution)/shard_map/ppermute | solution.py:36
  89.6 1.4 %collective-permute-start.21 = (f32[128,256]{1,0:T(8,128)S(1)}, f32[128,256]{1,0:T(8,128)S(1)}, u32[]{:S(2)}, u32[]{:S(2)}) collective-permute-start(f32[128,256]{1,0:T(8,128)S(1)} %fusion.8), channel_id=1, source_target_pairs={{0,1},{1,0},{2,3},{3,2},{4,5},{5,4},{6,7},{7,6},{8,9},{9,8},{10,11... | collective-permute-start | bytes 393224 | tf_op jit(solution)/shard_map/ppermute | solution.py:36

commit v3 on v2

--- a/solution.py
+++ b/solution.py
@@ -193,8 +193,8 @@
         input_output_aliases={} if start is None else {3 + len(blocks): 0},
         compiler_params=pltpu.CompilerParams(vmem_limit_bytes=VMEM),
         cost_estimate=pl.CostEstimate(
-            flops=2 * len(units) * out.shape[0] * WINDOW * SAMPLES,
-            bytes_accessed=2 * len(units) * ROWS * WINDOW,
+            flops=len(units) * out.shape[0] * WINDOW * SAMPLES // 2,
+            bytes_accessed=len(units) * ROWS * WINDOW // 2,
             transcendentals=0,
         ),
     )(me[None], front, keep, *blocks, *([] if start is None else [start]))
@@ -288,12 +288,12 @@
     near_a = shifted(lines[0], second(1))
     far_b = shifted(lines[1], second(2))
     total = products(front, myself, keep, both(far_a, 2, 0) + both(near_b, 1, 2), total)
-    outgoing, near_a, far_b, total = lax.optimization_barrier((outgoing, near_a, far_b, total))
+    outgoing, total = lax.optimization_barrier((outgoing, total))
+    near_a, far_b, opposite, total = lax.optimization_barrier((near_a, far_b, opposite, total))
     incoming = lax.all_to_all(
         outgoing.reshape(leaf_total, CAP, SAMPLES), "hss", split_axis=0, concat_axis=0, tiled=True
     ).reshape(leaf_total * CAP, SAMPLES)
     total = products(front, myself, keep, both(near_a, 1, 0) + both(far_b, 2, 2), total)
-    opposite, total = lax.optimization_barrier((opposite, total))
     total = products(front, myself, keep, both(opposite[0], 3, 0) + both(opposite[1], 3, 2), total)
     total, incoming = lax.optimization_barrier((total, incoming))
     full, root = total[:ROWS], total[ROWS:]

time: 92.2 us -> 89.4 us (0.970)
  waiting for transfers between devices: 10.3 us -> 6.24 us
    ppermute x26, waiting for transfers between devices: 9.18 us -> 6.24 us  [shifted(): lax.ppermute(x, 'hss', [(i, move(i)) for i in range(lax.axis_size('hss'))])]
    all_to_all x1, starting transfers between devices: 5.68 us -> 7.05 us  [body(): lax.all_to_all(outgoing.reshape(leaf_total, CAP, SAMPLES), 'hss', split_a...]
    all_to_all x1, waiting for transfers between devices: 1.12 us -> 0.01 us  [body(): lax.all_to_all(outgoing.reshape(leaf_total, CAP, SAMPLES), 'hss', split_a...]
    ppermute x26, starting transfers between devices: 29.6 us -> 28.6 us  [shifted(): lax.ppermute(x, 'hss', [(i, move(i)) for i in range(lax.axis_size('hss'))])]
  transfers between devices with their start and end apart: 27 -> 27, of which waited for: 13 -> 10; matrix products, arithmetic and copies ran while one was open for 14% -> 15% of each run, Pallas kernels for 33% -> 34%
where the time goes in v3:
time: 89.4 us; the launch traced here: 88.8 us
  starting transfers between devices  35.7 us (40%)
  Pallas kernels  30.6 us (34%)
  other arithmetic  7.59 us (8%)
  waiting for transfers between devices  6.24 us (7%)
  matrix products  6.17 us (7%)
  local copies, waits for them, and re-layouts  1.58 us (2%)
  between operations  0.98 us (1%)
    ppermute x26, starting transfers between devices, shifted(): lax.ppermute(x, 'hss', [(i, move(i)) for i in range(lax.axis_size('hss'))])  28.6 us
    pallas_call x4, Pallas kernels, products(): pl.pallas_call(functools.partial(product_kernel, units, plain, masked, st...  25.4 us
    all_to_all x1, starting transfers between devices, body(): lax.all_to_all(outgoing.reshape(leaf_total, CAP, SAMPLES), 'hss', split_a...  7.05 us
    ppermute x26, waiting for transfers between devices, shifted(): lax.ppermute(x, 'hss', [(i, move(i)) for i in range(lax.axis_size('hss'))])  6.24 us
    pallas_call x1, Pallas kernels, fates(): pl.pallas_call(fate_kernel, in_specs=[pl.BlockSpec(memory_space=pltpu.SME...  2.65 us
    pallas_call x1, Pallas kernels, pair_terms(): pl.pallas_call(pair_kernel, grid_spec=pltpu.PrefetchScalarGridSpec(num_sc...  2.55 us
    broadcast_in_dim x3, other arithmetic, body(): return (parent[None], pair[None], root[None])  2.12 us
    dot_general x1, matrix products, body(): full = full + jnp.dot(selector, incoming, preferred_element_type=F32)  2.11 us
  transfers between devices with their start and end apart: 27, of which 10 were waited for; matrix products, arithmetic and copies ran while one was open for 15% of the time, Pallas kernels for 34%

profile of v3, /device:TPU:1, one launch (start us, length us, event | category | flops | bytes accessed | tf_op | source)
XLA Modules:
  0.0 88.8 jit_solution(7187364041392245609)
XLA Ops:
  0.6 0.0 copy-start
  0.6 2.1 %collective-permute-start = (bf16[608,256]{1,0:T(8,128)(2,1)}, bf16[608,256]{1,0:T(8,128)(2,1)S(1)}, u32[]{:S(2)}, u32[]{:S(2)}) collective-permute-start(bf16[608,256]{1,0:T(8,128)(2,1)} %bitcast.47), channel_id=1, source_target_pairs={{0,2},{1,9},{2,0},{3,11},{4,6},{5,13},{6,4},{7,15},{8,10},{9,1},{1... | collective-permute-start | bytes 933896 | tf_op jit(solution)/shard_map/ppermute | solution.py:36
  2.8 1.8 %collective-permute-start.1 = (bf16[608,256]{1,0:T(8,128)(2,1)}, bf16[608,256]{1,0:T(8,128)(2,1)S(1)}, u32[]{:S(2)}, u32[]{:S(2)}) collective-permute-start(bf16[608,256]{1,0:T(8,128)(2,1)} %bitcast.48), channel_id=1, source_target_pairs={{0,6},{1,25},{2,4},{3,27},{4,2},{5,29},{6,0},{7,31},{8,14},{9,17},... | collective-permute-start | bytes 933896 | tf_op jit(solution)/shard_map/ppermute | solution.py:36
  4.6 0.6 collective-permute-start.2
  5.2 0.7 bitcast_add_fusion
  5.9 0.2 convert_reduce_fusion
  6.1 0.7 copy.15
  6.8 0.8 add_add_fusion.2
  7.6 0.7 copy-done.3
  8.3 2.6 %shard_map.94 = (s32[32,128]{1,0:T(8,128)S(1)}, f32[32,768]{1,0:T(8,128)S(1)}) custom-call(s32[1]{0:T(128)} %bitcast.me_ref, s32[31,128]{1,0:T(8,128)S(1)} %bitcast.52, s32[32,128]{1,0:T(8,128)S(1)} %bitcast.51), custom_call_target="tpu_custom_call" | custom-call | flops 33554432 | bytes 131072 | tf_op jit(solution)/shard_map/pallas_call | solution.py:96
  11.0 1.4 %select_reduce_fusion.1 = s32[128]{0:T(128)S(1)} fusion(s32[32,128]{1,0:T(8,128)S(1)} %add_add_fusion.2, s32[128]{0:T(128)S(1)} %iota_add_fusion, s32[32,128]{1,0:T(8,128)S(1)} %get-tuple-element.33), kind=kLoop, calls=%fused_computation.8 | loop fusion | flops 1572736 | bytes 33792 | tf_op jit(solution)/shard_map/reduce_sum | solution.py:269
  12.4 0.9 fusion.15
  13.3 1.8 %fusion.2 = bf16[2048,256]{1,0:T(8,128)(2,1)} fusion(s32[512]{0:T(512)S(1)} %multiply_add_fusion, bf16[1,512,256]{2,1,0:T(8,128)(2,1)S(1)} %copy-done), kind=kOutput, calls=%fused_computation.6 | convolution fusion | flops 538443776 | bytes 1312768 | tf_op jit(solution)/shard_map/dot_general | solution.py:267
  15.2 0.1 pad_maximum_fusion.1.refs_2_
  15.2 2.6 %collective-permute-start.6 = (bf16[2,608,256]{2,1,0:T(8,128)(2,1)S(1)}, bf16[2,608,256]{2,1,0:T(8,128)(2,1)S(1)}, u32[]{:S(2)}, u32[]{:S(2)}) collective-permute-start(bf16[2,608,256]{2,1,0:T(8,128)(2,1)S(1)} %pad_maximum_fusion.1.refs_2_), channel_id=1, source_target_pairs={{0,1},{1,0},{2,3},{3,2},{4,5},{5,4},{6,7},{7,6},{8,9},{9,8},{10,11... | collective-permute-start | bytes 1867784 | tf_op jit(solution)/shard_map/ppermute | solution.py:36
  17.8 0.1 pad_maximum_fusion.refs_0_
  17.9 0.1 collective-permute-start.5
  18.0 0.3 collective-permute-start.4
  18.3 2.2 %collective-permute-start.3 = (bf16[2,608,256]{2,1,0:T(8,128)(2,1)S(1)}, bf16[2,608,256]{2,1,0:T(8,128)(2,1)}, u32[]{:S(2)}, u32[]{:S(2)}) collective-permute-start(bf16[2,608,256]{2,1,0:T(8,128)(2,1)S(1)} %pad_maximum_fusion.refs_0_), channel_id=1, source_target_pairs={{0,24},{1,7},{2,26},{3,5},{4,28},{5,3},{6,30},{7,1},{8,16},{9,15},... | collective-permute-start | bytes 1867784 | tf_op jit(solution)/shard_map/ppermute | solution.py:36
  20.5 6.2 %shard_map.95.refs_4_ = f32[1216,256]{1,0:T(8,128)S(1)} custom-call(s32[1]{0:T(128)} %bitcast.me_ref, bf16[608,19456]{1,0:T(8,128)(2,1)} %bitcast.53, f32[32,768]{1,0:T(8,128)S(1)} %get-tuple-element.34.keep_ref, bf16[2,608,256]{2,1,0:T(8,128)(2,1)S(1)} %pad_maximum_fusion.refs_0_, bf16[2,608,256]{2,1,0:T(8,128)(2,1)S(1)} %collective-permute-done.5.refs_1_, ...), custom_call_target="tpu_custom_call" | custom-call | flops 956301312 | bytes 1867776 | tf_op jit(solution)/shard_map/pallas_call | solution.py:179
  26.8 0.8 collective-permute-done.4.refs_2_
  27.6 1.4 %collective-permute-done.3.refs_0_ = bf16[2,608,256]{2,1,0:T(8,128)(2,1)} collective-permute-done((bf16[2,608,256]{2,1,0:T(8,128)(2,1)S(1)}, bf16[2,608,256]{2,1,0:T(8,128)(2,1)}, u32[]{:S(2)}, u32[]{:S(2)}) %collective-permute-start.3) | collective-permute-done | bytes 622624 | tf_op jit(solution)/shard_map/ppermute | solution.py:36
  29.0 2.5 %collective-permute-start.11 = (bf16[2,608,256]{2,1,0:T(8,128)(2,1)}, bf16[2,608,256]{2,1,0:T(8,128)(2,1)S(1)}, u32[]{:S(2)}, u32[]{:S(2)}) collective-permute-start(bf16[2,608,256]{2,1,0:T(8,128)(2,1)} %collective-permute-done.3.refs_0_), channel_id=1, source_target_pairs={{0,1},{1,0},{2,3},{3,2},{4,5},{5,4},{6,7},{7,6},{8,9},{9,8},{10,11... | collective-permute-start | bytes 1867784 | tf_op jit(solution)/shard_map/ppermute | solution.py:36
  31.5 2.3 %collective-permute-start.10 = (bf16[2,608,256]{2,1,0:T(8,128)(2,1)}, bf16[2,608,256]{2,1,0:T(8,128)(2,1)}, u32[]{:S(2)}, u32[]{:S(2)}) collective-permute-start(bf16[2,608,256]{2,1,0:T(8,128)(2,1)} %collective-permute-done.4.refs_2_), channel_id=1, source_target_pairs={{0,24},{1,7},{2,26},{3,5},{4,28},{5,3},{6,30},{7,1},{8,16},{9,15},... | collective-permute-start | bytes 1867784 | tf_op jit(solution)/shard_map/ppermute | solution.py:36
  33.9 0.3 collective-permute-start.8
  34.2 1.1 %collective-permute-start.9 = (bf16[2,608,256]{2,1,0:T(8,128)(2,1)}, bf16[2,608,256]{2,1,0:T(8,128)(2,1)}, u32[]{:S(2)}, u32[]{:S(2)}) collective-permute-start(bf16[2,608,256]{2,1,0:T(8,128)(2,1)} %collective-permute-done.3.refs_0_), channel_id=1, source_target_pairs={{0,8},{1,3},{2,10},{3,1},{4,12},{5,7},{6,14},{7,5},{8,0},{9,11},{1... | collective-permute-start | bytes 1867784 | tf_op jit(solution)/shard_map/ppermute | solution.py:36
  35.4 6.4 %shard_map.96.refs_4_ = f32[1216,256]{1,0:T(8,128)S(1)} custom-call(s32[1]{0:T(128)} %bitcast.me_ref, bf16[608,19456]{1,0:T(8,128)(2,1)} %bitcast.54, f32[32,768]{1,0:T(8,128)S(1)} %get-tuple-element.34.keep_ref, bf16[2,608,256]{2,1,0:T(8,128)(2,1)} %collective-permute-done.3.refs_0_, ...), custom_call_target="tpu_custom_call", output_to_operand_aliasing={{}: (7, {})} | custom-call | flops 956301312 | bytes 1867776 | tf_op jit(solution)/shard_map/pallas_call | solution.py:179
  41.7 7.0 %all-to-all-start = ((bf16[32,64,256]{2,1,0:T(8,128)(2,1)}), bf16[32,64,256]{2,1,0:T(8,128)(2,1)}, u32[]{:S(2)}, u32[]{:S(2)}) async-start(bf16[32,64,256]{2,1,0:T(8,128)(2,1)} %bitcast.58), calls=%async_computation | async-start | bytes 2097152 | tf_op jit(solution)/shard_map/all_to_all | solution.py:293
  48.8 0.3 collective-permute-done.8.refs_2_
  49.1 0.9 %collective-permute-done.9.refs_0_ = bf16[2,608,256]{2,1,0:T(8,128)(2,1)} collective-permute-done((bf16[2,608,256]{2,1,0:T(8,128)(2,1)}, bf16[2,608,256]{2,1,0:T(8,128)(2,1)}, u32[]{:S(2)}, u32[]{:S(2)}) %collective-permute-start.9) | collective-permute-done | bytes 622624 | tf_op jit(solution)/shard_map/ppermute | solution.py:36
  50.0 1.1 %collective-permute-start.15 = (bf16[2,608,256]{2,1,0:T(8,128)(2,1)}, bf16[2,608,256]{2,1,0:T(8,128)(2,1)S(1)}, u32[]{:S(2)}, u32[]{:S(2)}) collective-permute-start(bf16[2,608,256]{2,1,0:T(8,128)(2,1)} %collective-permute-done.7.refs_0_), channel_id=1, source_target_pairs={{0,1},{1,0},{2,3},{3,2},{4,5},{5,4},{6,7},{7,6},{8,9},{9,8},{10,11... | collective-permute-start | bytes 1867784 | tf_op jit(solution)/shard_map/ppermute | solution.py:36
  51.2 0.5 collective-permute-start.13
  51.7 0.1 collective-permute-start.14
  51.7 0.8 fusion.34
  52.5 0.7 fusion.36
  53.2 0.1 select_reduce_fusion.2
  53.3 0.6 collective-permute-done.16.refs_3_
  53.9 6.4 %shard_map.97.refs_4_ = f32[1216,256]{1,0:T(8,128)S(1)} custom-call(s32[1]{0:T(128)} %bitcast.me_ref, bf16[608,19456]{1,0:T(8,128)(2,1)} %bitcast.55, f32[32,768]{1,0:T(8,128)S(1)} %get-tuple-element.34.keep_ref, bf16[2,608,256]{2,1,0:T(8,128)(2,1)} %collective-permute-done.7.refs_0_, ...), custom_call_target="tpu_custom_call", output_to_operand_aliasing={{}: (7, {})} | custom-call | flops 956301312 | bytes 1867776 | tf_op jit(solution)/shard_map/pallas_call | solution.py:179
  60.3 6.4 %shard_map.98 = f32[1216,256]{1,0:T(8,128)S(1)} custom-call(s32[1]{0:T(128)} %bitcast.me_ref, bf16[608,19456]{1,0:T(8,128)(2,1)} %bitcast.56, f32[32,768]{1,0:T(8,128)S(1)} %get-tuple-element.34.keep_ref, bf16[2,608,256]{2,1,0:T(8,128)(2,1)} %collective-permute-done.9.refs_0_, ...), custom_call_target="tpu_custom_call", output_to_operand_aliasing={{}: (7, {})} | custom-call | flops 956301312 | bytes 1867776 | tf_op jit(solution)/shard_map/pallas_call | solution.py:179
  66.8 0.4 fusion.12
  67.2 0.5 collective-permute-start.17
  67.7 0.9 collective-permute-done.17
  68.6 0.3 collective-permute-start.18
  68.9 2.2 %collective-permute-start.19 = (f32[64,256]{1,0:T(8,128)S(1)}, f32[64,256]{1,0:T(8,128)S(1)}, u32[]{:S(2)}, u32[]{:S(2)}) collective-permute-start(f32[64,256]{1,0:T(8,128)S(1)} %select_add_fusion), channel_id=1, source_target_pairs={{0,6},{1,7},{2,4},{3,5},{4,2},{5,3},{6,0},{7,1},{8,14},{9,15},{10,... | collective-permute-start | bytes 196616 | tf_op jit(solution)/shard_map/ppermute | solution.py:36
  71.2 1.1 %collective-permute-start.20 = (f32[64,256]{1,0:T(8,128)S(1)}, f32[64,256]{1,0:T(8,128)S(1)}, u32[]{:S(2)}, u32[]{:S(2)}) collective-permute-start(f32[64,256]{1,0:T(8,128)S(1)} %select_add_fusion), channel_id=1, source_target_pairs={{0,4},{1,5},{2,6},{3,7},{4,0},{5,1},{6,2},{7,3},{8,12},{9,13},{10,... | collective-permute-start | bytes 196616 | tf_op jit(solution)/shard_map/ppermute | solution.py:36
  72.2 0.1 fusion.23
  72.4 0.3 fusion.6
  72.7 0.6 select_reduce_fusion
  73.3 0.1 sub.45
  73.4 2.1 %fusion = f32[608,256]{1,0:T(8,128)S(1)} fusion(bf16[2048,256]{1,0:T(8,128)(2,1)} %bitcast.14, s32[2048]{0:T(1024)S(1)} %sub.45), kind=kOutput, calls=%fused_computation.1 | convolution fusion | flops 638779392 | bytes 1679360 | tf_op jit(solution)/shard_map/dot_general | solution.py:326
  75.6 0.2 collective-permute-done.20
  75.8 0.1 collective-permute-start.22
  75.9 1.8 %collective-permute-start.23 = (f32[64,256]{1,0:T(8,128)S(1)}, f32[64,256]{1,0:T(8,128)S(1)}, u32[]{:S(2)}, u32[]{:S(2)}) collective-permute-start(f32[64,256]{1,0:T(8,128)S(1)} %add_add_fusion.1), channel_id=1, source_target_pairs={{0,24},{1,25},{2,26},{3,27},{4,28},{5,29},{6,30},{7,31},{8,16},{9,... | collective-permute-start | bytes 196616 | tf_op jit(solution)/shard_map/ppermute | solution.py:36
  77.8 1.4 %collective-permute-start.24 = (f32[64,256]{1,0:T(8,128)S(1)}, f32[64,256]{1,0:T(8,128)S(1)}, u32[]{:S(2)}, u32[]{:S(2)}) collective-permute-start(f32[64,256]{1,0:T(8,128)S(1)} %add_add_fusion.1), channel_id=1, source_target_pairs={{0,16},{1,17},{2,18},{3,19},{4,20},{5,21},{6,22},{7,23},{8,24},{9,... | collective-permute-start | bytes 196616 | tf_op jit(solution)/shard_map/ppermute | solution.py:36
  79.1 0.8 convert_bitcast_fusion
  79.9 2.5 %shard_map.99 = f32[608,256]{1,0:T(8,128)S(1)} custom-call(s32[1]{0:T(128)} %bitcast.me_ref, bf16[608,19456]{1,0:T(8,128)(2,1)} %bitcast.57, bf16[608,256]{1,0:T(8,128)(2,1)S(1)} %bitcast.50, bf16[608,256]{1,0:T(8,128)(2,1)S(1)} %slice_bitcast_fusion.yours_ref, s32[1,128]{1,0:T(1,128)S(1)} %get-tuple-element.67.names_ref), custom_call_target="tpu_custom_call" | custom-call | flops 478150656 | bytes 1867776 | tf_op jit(solution)/shard_map/pallas_call | solution.py:228
  82.5 0.4 collective-permute-done.24
  82.9 3.3 %collective-permute-start.25 = (f32[64,256]{1,0:T(8,128)S(1)}, f32[64,256]{1,0:T(8,128)S(1)}, u32[]{:S(2)}, u32[]{:S(2)}) collective-permute-start(f32[64,256]{1,0:T(8,128)S(1)} %add_add_fusion), channel_id=1, source_target_pairs={{0,1},{1,0},{2,3},{3,2},{4,5},{5,4},{6,7},{7,6},{8,9},{9,8},{10,11... | collective-permute-start | bytes 196616 | tf_op jit(solution)/shard_map/ppermute | solution.py:36
  86.2 0.5 fusion.8
  86.7 0.1 collective-permute-start.21
  86.8 0.3 collective-permute-done.25
  87.1 0.7 maximum_bitcast_fusion
  87.8 0.3 collective-permute-done.21
  88.1 0.7 add_bitcast_fusion
  (48 shorter events, 0.2 us)
Async XLA Ops:
  0.6 11.8 %copy-start = (bf16[1,512,256]{2,1,0:T(8,128)(2,1)S(1)}, bf16[1,512,256]{2,1,0:T(8,128)(2,1)}, u32[]{:S(2)}) copy-start(bf16[1,512,256]{2,1,0:T(8,128)(2,1)} %param.9) | copy-start | bytes 786436
  0.6 14.5 %collective-permute-start = (bf16[608,256]{1,0:T(8,128)(2,1)}, bf16[608,256]{1,0:T(8,128)(2,1)S(1)}, u32[]{:S(2)}, u32[]{:S(2)}) collective-permute-start(bf16[608,256]{1,0:T(8,128)(2,1)} %bitcast.47), channel_id=1, source_target_pairs={{0,2},{1,9},{2,0},{3,11},{4,6},{5,13},{6,4},{7,15},{8,10},{9,1},{1... | collective-permute-start | bytes 933896 | tf_op jit(solution)/shard_map/ppermute | solution.py:36
  2.8 12.4 %collective-permute-start.1 = (bf16[608,256]{1,0:T(8,128)(2,1)}, bf16[608,256]{1,0:T(8,128)(2,1)S(1)}, u32[]{:S(2)}, u32[]{:S(2)}) collective-permute-start(bf16[608,256]{1,0:T(8,128)(2,1)} %bitcast.48), channel_id=1, source_target_pairs={{0,6},{1,25},{2,4},{3,27},{4,2},{5,29},{6,0},{7,31},{8,14},{9,17},... | collective-permute-start | bytes 933896 | tf_op jit(solution)/shard_map/ppermute | solution.py:36
  4.6 10.6 %collective-permute-start.2 = (bf16[608,256]{1,0:T(8,128)(2,1)}, bf16[608,256]{1,0:T(8,128)(2,1)S(1)}, u32[]{:S(2)}, u32[]{:S(2)}) collective-permute-start(bf16[608,256]{1,0:T(8,128)(2,1)} %bitcast.49), channel_id=1, source_target_pairs={{0,4},{1,17},{2,6},{3,19},{4,0},{5,21},{6,2},{7,23},{8,12},{9,25},... | collective-permute-start | bytes 933896 | tf_op jit(solution)/shard_map/ppermute | solution.py:36
  7.6 0.7 copy-start.3
  13.3 4.5 %copy-start.1 = (bf16[1,608,256]{2,1,0:T(8,128)(2,1)S(1)}, bf16[1,608,256]{2,1,0:T(8,128)(2,1)}, u32[]{:S(2)}) copy-start(bf16[1,608,256]{2,1,0:T(8,128)(2,1)} %param.8) | copy-start | bytes 933892
  15.2 5.3 %collective-permute-start.6 = (bf16[2,608,256]{2,1,0:T(8,128)(2,1)S(1)}, bf16[2,608,256]{2,1,0:T(8,128)(2,1)S(1)}, u32[]{:S(2)}, u32[]{:S(2)}) collective-permute-start(bf16[2,608,256]{2,1,0:T(8,128)(2,1)S(1)} %pad_maximum_fusion.1.refs_2_), channel_id=1, source_target_pairs={{0,1},{1,0},{2,3},{3,2},{4,5},{5,4},{6,7},{7,6},{8,9},{9,8},{10,11... | collective-permute-start | bytes 1867784 | tf_op jit(solution)/shard_map/ppermute | solution.py:36
  17.9 2.6 %collective-permute-start.5 = (bf16[2,608,256]{2,1,0:T(8,128)(2,1)S(1)}, bf16[2,608,256]{2,1,0:T(8,128)(2,1)S(1)}, u32[]{:S(2)}, u32[]{:S(2)}) collective-permute-start(bf16[2,608,256]{2,1,0:T(8,128)(2,1)S(1)} %pad_maximum_fusion.refs_0_), channel_id=1, source_target_pairs={{0,1},{1,0},{2,3},{3,2},{4,5},{5,4},{6,7},{7,6},{8,9},{9,8},{10,11... | collective-permute-start | bytes 1867784 | tf_op jit(solution)/shard_map/ppermute | solution.py:36
  18.0 9.6 %collective-permute-start.4 = (bf16[2,608,256]{2,1,0:T(8,128)(2,1)S(1)}, bf16[2,608,256]{2,1,0:T(8,128)(2,1)}, u32[]{:S(2)}, u32[]{:S(2)}) collective-permute-start(bf16[2,608,256]{2,1,0:T(8,128)(2,1)S(1)} %pad_maximum_fusion.1.refs_2_), channel_id=1, source_target_pairs={{0,8},{1,3},{2,10},{3,1},{4,12},{5,7},{6,14},{7,5},{8,0},{9,11},{1... | collective-permute-start | bytes 1867784 | tf_op jit(solution)/shard_map/ppermute | solution.py:36
  18.3 10.7 %collective-permute-start.3 = (bf16[2,608,256]{2,1,0:T(8,128)(2,1)S(1)}, bf16[2,608,256]{2,1,0:T(8,128)(2,1)}, u32[]{:S(2)}, u32[]{:S(2)}) collective-permute-start(bf16[2,608,256]{2,1,0:T(8,128)(2,1)S(1)} %pad_maximum_fusion.refs_0_), channel_id=1, source_target_pairs={{0,24},{1,7},{2,26},{3,5},{4,28},{5,3},{6,30},{7,1},{8,16},{9,15},... | collective-permute-start | bytes 1867784 | tf_op jit(solution)/shard_map/ppermute | solution.py:36
  29.0 5.2 %collective-permute-start.11 = (bf16[2,608,256]{2,1,0:T(8,128)(2,1)}, bf16[2,608,256]{2,1,0:T(8,128)(2,1)S(1)}, u32[]{:S(2)}, u32[]{:S(2)}) collective-permute-start(bf16[2,608,256]{2,1,0:T(8,128)(2,1)} %collective-permute-done.3.refs_0_), channel_id=1, source_target_pairs={{0,1},{1,0},{2,3},{3,2},{4,5},{5,4},{6,7},{7,6},{8,9},{9,8},{10,11... | collective-permute-start | bytes 1867784 | tf_op jit(solution)/shard_map/ppermute | solution.py:36
  31.5 3.8 %collective-permute-start.12 = (bf16[2,608,256]{2,1,0:T(8,128)(2,1)}, bf16[2,608,256]{2,1,0:T(8,128)(2,1)S(1)}, u32[]{:S(2)}, u32[]{:S(2)}) collective-permute-start(bf16[2,608,256]{2,1,0:T(8,128)(2,1)} %collective-permute-done.4.refs_2_), channel_id=1, source_target_pairs={{0,1},{1,0},{2,3},{3,2},{4,5},{5,4},{6,7},{7,6},{8,9},{9,8},{10,11... | collective-permute-start | bytes 1867784 | tf_op jit(solution)/shard_map/ppermute | solution.py:36
  31.5 17.3 %collective-permute-start.10 = (bf16[2,608,256]{2,1,0:T(8,128)(2,1)}, bf16[2,608,256]{2,1,0:T(8,128)(2,1)}, u32[]{:S(2)}, u32[]{:S(2)}) collective-permute-start(bf16[2,608,256]{2,1,0:T(8,128)(2,1)} %collective-permute-done.4.refs_2_), channel_id=1, source_target_pairs={{0,24},{1,7},{2,26},{3,5},{4,28},{5,3},{6,30},{7,1},{8,16},{9,15},... | collective-permute-start | bytes 1867784 | tf_op jit(solution)/shard_map/ppermute | solution.py:36
  33.9 14.9 %collective-permute-start.7 = (bf16[2,608,256]{2,1,0:T(8,128)(2,1)S(1)}, bf16[2,608,256]{2,1,0:T(8,128)(2,1)}, u32[]{:S(2)}, u32[]{:S(2)}) collective-permute-start(bf16[2,608,256]{2,1,0:T(8,128)(2,1)S(1)} %pad_maximum_fusion.refs_0_), channel_id=1, source_target_pairs={{0,8},{1,3},{2,10},{3,1},{4,12},{5,7},{6,14},{7,5},{8,0},{9,11},{1... | collective-permute-start | bytes 1867784 | tf_op jit(solution)/shard_map/ppermute | solution.py:36
  33.9 15.2 %collective-permute-start.8 = (bf16[2,608,256]{2,1,0:T(8,128)(2,1)S(1)}, bf16[2,608,256]{2,1,0:T(8,128)(2,1)}, u32[]{:S(2)}, u32[]{:S(2)}) collective-permute-start(bf16[2,608,256]{2,1,0:T(8,128)(2,1)S(1)} %pad_maximum_fusion.1.refs_2_), channel_id=1, source_target_pairs={{0,24},{1,7},{2,26},{3,5},{4,28},{5,3},{6,30},{7,1},{8,16},{9,15},... | collective-permute-start | bytes 1867784 | tf_op jit(solution)/shard_map/ppermute | solution.py:36
  34.2 15.8 %collective-permute-start.9 = (bf16[2,608,256]{2,1,0:T(8,128)(2,1)}, bf16[2,608,256]{2,1,0:T(8,128)(2,1)}, u32[]{:S(2)}, u32[]{:S(2)}) collective-permute-start(bf16[2,608,256]{2,1,0:T(8,128)(2,1)} %collective-permute-done.3.refs_0_), channel_id=1, source_target_pairs={{0,8},{1,3},{2,10},{3,1},{4,12},{5,7},{6,14},{7,5},{8,0},{9,11},{1... | collective-permute-start | bytes 1867784 | tf_op jit(solution)/shard_map/ppermute | solution.py:36
  41.7 25.0 %all-to-all-start = ((bf16[32,64,256]{2,1,0:T(8,128)(2,1)}), bf16[32,64,256]{2,1,0:T(8,128)(2,1)}, u32[]{:S(2)}, u32[]{:S(2)}) async-start(bf16[32,64,256]{2,1,0:T(8,128)(2,1)} %bitcast.58), calls=%async_computation | async-start | bytes 2097152 | tf_op jit(solution)/shard_map/all_to_all | solution.py:293
  50.0 3.3 %collective-permute-start.15 = (bf16[2,608,256]{2,1,0:T(8,128)(2,1)}, bf16[2,608,256]{2,1,0:T(8,128)(2,1)S(1)}, u32[]{:S(2)}, u32[]{:S(2)}) collective-permute-start(bf16[2,608,256]{2,1,0:T(8,128)(2,1)} %collective-permute-done.7.refs_0_), channel_id=1, source_target_pairs={{0,1},{1,0},{2,3},{3,2},{4,5},{5,4},{6,7},{7,6},{8,9},{9,8},{10,11... | collective-permute-start | bytes 1867784 | tf_op jit(solution)/shard_map/ppermute | solution.py:36
  51.1 2.8 %collective-permute-start.16 = (bf16[2,608,256]{2,1,0:T(8,128)(2,1)}, bf16[2,608,256]{2,1,0:T(8,128)(2,1)S(1)}, u32[]{:S(2)}, u32[]{:S(2)}) collective-permute-start(bf16[2,608,256]{2,1,0:T(8,128)(2,1)} %collective-permute-done.8.refs_2_), channel_id=1, source_target_pairs={{0,1},{1,0},{2,3},{3,2},{4,5},{5,4},{6,7},{7,6},{8,9},{9,8},{10,11... | collective-permute-start | bytes 1867784 | tf_op jit(solution)/shard_map/ppermute | solution.py:36
  51.2 9.2 %collective-permute-start.13 = (bf16[2,608,256]{2,1,0:T(8,128)(2,1)}, bf16[2,608,256]{2,1,0:T(8,128)(2,1)S(1)}, u32[]{:S(2)}, u32[]{:S(2)}) collective-permute-start(bf16[2,608,256]{2,1,0:T(8,128)(2,1)} %collective-permute-done.9.refs_0_), channel_id=1, source_target_pairs={{0,1},{1,0},{2,3},{3,2},{4,5},{5,4},{6,7},{7,6},{8,9},{9,8},{10,11... | collective-permute-start | bytes 1867784 | tf_op jit(solution)/shard_map/ppermute | solution.py:36
  51.7 8.7 %collective-permute-start.14 = (bf16[2,608,256]{2,1,0:T(8,128)(2,1)}, bf16[2,608,256]{2,1,0:T(8,128)(2,1)S(1)}, u32[]{:S(2)}, u32[]{:S(2)}) collective-permute-start(bf16[2,608,256]{2,1,0:T(8,128)(2,1)} %collective-permute-done.10.refs_2_), channel_id=1, source_target_pairs={{0,1},{1,0},{2,3},{3,2},{4,5},{5,4},{6,7},{7,6},{8,9},{9,8},{10,11... | collective-permute-start | bytes 1867784 | tf_op jit(solution)/shard_map/ppermute | solution.py:36
  60.3 6.5 %copy-start.4 = (f32[128,256]{1,0:T(8,128)S(1)}, f32[128,256]{1,0:T(8,128)}, u32[]{:S(2)}) copy-start(f32[128,256]{1,0:T(8,128)} %fusion.15) | copy-start | bytes 393220
  60.3 11.9 %copy-start.5 = (s32[1,16384,1]{1,2,0:T(1,128)S(1)}, s32[1,16384,1]{1,2,0:T(1,128)}, u32[]{:S(2)}) copy-start(s32[1,16384,1]{1,2,0:T(1,128)} %param.10) | copy-start | bytes 196612
  66.8 5.6 %copy-start.6 = (s32[1,16384]{1,0:T(1,128)S(1)}, s32[1,16384]{1,0:T(1,128)}, u32[]{:S(2)}) copy-start(s32[1,16384]{1,0:T(1,128)} %param.11) | copy-start | bytes 196612
  67.2 1.4 %collective-permute-start.17 = (f32[64,256]{1,0:T(8,128)S(1)}, f32[64,256]{1,0:T(8,128)S(1)}, u32[]{:S(2)}, u32[]{:S(2)}) collective-permute-start(f32[64,256]{1,0:T(8,128)S(1)} %slice_select_fusion), channel_id=1, source_target_pairs={{0,1},{1,0},{2,3},{3,2},{4,5},{5,4},{6,7},{7,6},{8,9},{9,8},{10,11... | collective-permute-start | bytes 196616 | tf_op jit(solution)/shard_map/ppermute | solution.py:36
  68.6 6.9 %collective-permute-start.18 = (f32[64,256]{1,0:T(8,128)S(1)}, f32[64,256]{1,0:T(8,128)S(1)}, u32[]{:S(2)}, u32[]{:S(2)}) collective-permute-start(f32[64,256]{1,0:T(8,128)S(1)} %select_add_fusion), channel_id=1, source_target_pairs={{0,2},{1,3},{2,0},{3,1},{4,6},{5,7},{6,4},{7,5},{8,10},{9,11},{10,... | collective-permute-start | bytes 196616 | tf_op jit(solution)/shard_map/ppermute | solution.py:36
  68.9 6.6 %collective-permute-start.19 = (f32[64,256]{1,0:T(8,128)S(1)}, f32[64,256]{1,0:T(8,128)S(1)}, u32[]{:S(2)}, u32[]{:S(2)}) collective-permute-start(f32[64,256]{1,0:T(8,128)S(1)} %select_add_fusion), channel_id=1, source_target_pairs={{0,6},{1,7},{2,4},{3,5},{4,2},{5,3},{6,0},{7,1},{8,14},{9,15},{10,... | collective-permute-start | bytes 196616 | tf_op jit(solution)/shard_map/ppermute | solution.py:36
  71.2 4.6 %collective-permute-start.20 = (f32[64,256]{1,0:T(8,128)S(1)}, f32[64,256]{1,0:T(8,128)S(1)}, u32[]{:S(2)}, u32[]{:S(2)}) collective-permute-start(f32[64,256]{1,0:T(8,128)S(1)} %select_add_fusion), channel_id=1, source_target_pairs={{0,4},{1,5},{2,6},{3,7},{4,0},{5,1},{6,2},{7,3},{8,12},{9,13},{10,... | collective-permute-start | bytes 196616 | tf_op jit(solution)/shard_map/ppermute | solution.py:36
  75.5 4.4 %copy-start.2 = (bf16[1,608,256]{2,1,0:T(8,128)(2,1)S(1)}, bf16[1,608,256]{2,1,0:T(8,128)(2,1)}, u32[]{:S(2)}) copy-start(bf16[1,608,256]{2,1,0:T(8,128)(2,1)} %param.8) | copy-start | bytes 933892
  75.8 6.7 %collective-permute-start.22 = (f32[64,256]{1,0:T(8,128)S(1)}, f32[64,256]{1,0:T(8,128)S(1)}, u32[]{:S(2)}, u32[]{:S(2)}) collective-permute-start(f32[64,256]{1,0:T(8,128)S(1)} %add_add_fusion.1), channel_id=1, source_target_pairs={{0,8},{1,9},{2,10},{3,11},{4,12},{5,13},{6,14},{7,15},{8,0},{9,1},... | collective-permute-start | bytes 196616 | tf_op jit(solution)/shard_map/ppermute | solution.py:36
  75.9 6.6 %collective-permute-start.23 = (f32[64,256]{1,0:T(8,128)S(1)}, f32[64,256]{1,0:T(8,128)S(1)}, u32[]{:S(2)}, u32[]{:S(2)}) collective-permute-start(f32[64,256]{1,0:T(8,128)S(1)} %add_add_fusion.1), channel_id=1, source_target_pairs={{0,24},{1,25},{2,26},{3,27},{4,28},{5,29},{6,30},{7,31},{8,16},{9,... | collective-permute-start | bytes 196616 | tf_op jit(solution)/shard_map/ppermute | solution.py:36
  77.8 5.2 %collective-permute-start.24 = (f32[64,256]{1,0:T(8,128)S(1)}, f32[64,256]{1,0:T(8,128)S(1)}, u32[]{:S(2)}, u32[]{:S(2)}) collective-permute-start(f32[64,256]{1,0:T(8,128)S(1)} %add_add_fusion.1), channel_id=1, source_target_pairs={{0,16},{1,17},{2,18},{3,19},{4,20},{5,21},{6,22},{7,23},{8,24},{9,... | collective-permute-start | bytes 196616 | tf_op jit(solution)/shard_map/ppermute | solution.py:36
  82.9 4.2 %collective-permute-start.25 = (f32[64,256]{1,0:T(8,128)S(1)}, f32[64,256]{1,0:T(8,128)S(1)}, u32[]{:S(2)}, u32[]{:S(2)}) collective-permute-start(f32[64,256]{1,0:T(8,128)S(1)} %add_add_fusion), channel_id=1, source_target_pairs={{0,1},{1,0},{2,3},{3,2},{4,5},{5,4},{6,7},{7,6},{8,9},{9,8},{10,11... | collective-permute-start | bytes 196616 | tf_op jit(solution)/shard_map/ppermute | solution.py:36
  86.7 1.4 %collective-permute-start.21 = (f32[128,256]{1,0:T(8,128)S(1)}, f32[128,256]{1,0:T(8,128)S(1)}, u32[]{:S(2)}, u32[]{:S(2)}) collective-permute-start(f32[128,256]{1,0:T(8,128)S(1)} %fusion.8), channel_id=1, source_target_pairs={{0,1},{1,0},{2,3},{3,2},{4,5},{5,4},{6,7},{7,6},{8,9},{9,8},{10,11... | collective-permute-start | bytes 393224 | tf_op jit(solution)/shard_map/ppermute | solution.py:36

commit v4 on v3

--- a/solution.py
+++ b/solution.py
@@ -272,7 +272,7 @@
     root_hits = (root_ids[:, None] == my_targets[None, :]).astype(BF)
     root_arrivals = jnp.dot(root_hits, child_rows[0], preferred_element_type=F32)
 
-    turned, keep, outgoing, root_arrivals = lax.optimization_barrier((turned, keep, outgoing, root_arrivals))
+    turned, keep, outgoing = lax.optimization_barrier((turned, keep, outgoing))
     lines = [jnp.stack(turned[:2]), jnp.stack(turned[2:])]
     far_a = shifted(lines[0], second(2))
     near_b = shifted(lines[1], second(1))
@@ -283,7 +283,7 @@
     parts = both(lines[0], 0, 0) + both(lines[1], 0, 2)
     total = products(front, myself, keep, parts)
     yours = parts[1][0][0]
-    far_a, near_b, lines, total = lax.optimization_barrier((far_a, near_b, lines, total))
+    far_a, near_b, lines, total, root_arrivals = lax.optimization_barrier((far_a, near_b, lines, total, root_arrivals))
     opposite = [shifted(far_a, second(1)), shifted(near_b, second(2))]
     near_a = shifted(lines[0], second(1))
     far_b = shifted(lines[1], second(2))

time: 89.4 us -> 87.7 us (0.981)
  waiting for transfers between devices: 6.24 us -> 4.81 us
    ppermute x26, waiting for transfers between devices: 6.24 us -> 4.8 us  [shifted(): lax.ppermute(x, 'hss', [(i, move(i)) for i in range(lax.axis_size('hss'))])]
  transfers between devices with their start and end apart: 27 -> 27, of which waited for: 10 -> 9; matrix products, arithmetic and copies ran while one was open for 15% -> 15% of each run, Pallas kernels for 34% -> 35%
where the time goes in v4:
time: 87.7 us; the launch traced here: 87.2 us
  starting transfers between devices  35.5 us (40%)
  Pallas kernels  30.6 us (35%)
  other arithmetic  7.58 us (9%)
  matrix products  6.17 us (7%)
  waiting for transfers between devices  4.81 us (5%)
  local copies, waits for them, and re-layouts  1.57 us (2%)
  between operations  1 us (1%)
    ppermute x26, starting transfers between devices, shifted(): lax.ppermute(x, 'hss', [(i, move(i)) for i in range(lax.axis_size('hss'))])  27.9 us
    pallas_call x4, Pallas kernels, products(): pl.pallas_call(functools.partial(product_kernel, units, plain, masked, st...  25.4 us
    all_to_all x1, starting transfers between devices, body(): lax.all_to_all(outgoing.reshape(leaf_total, CAP, SAMPLES), 'hss', split_a...  7.56 us
    ppermute x26, waiting for transfers between devices, shifted(): lax.ppermute(x, 'hss', [(i, move(i)) for i in range(lax.axis_size('hss'))])  4.8 us
    pallas_call x1, Pallas kernels, fates(): pl.pallas_call(fate_kernel, in_specs=[pl.BlockSpec(memory_space=pltpu.SME...  2.65 us
    pallas_call x1, Pallas kernels, pair_terms(): pl.pallas_call(pair_kernel, grid_spec=pltpu.PrefetchScalarGridSpec(num_sc...  2.55 us
    broadcast_in_dim x3, other arithmetic, body(): return (parent[None], pair[None], root[None])  2.12 us
    dot_general x1, matrix products, body(): full = full + jnp.dot(selector, incoming, preferred_element_type=F32)  2.11 us
  transfers between devices with their start and end apart: 27, of which 9 were waited for; matrix products, arithmetic and copies ran while one was open for 15% of the time, Pallas kernels for 35%

profile of v4, /device:TPU:1, one launch (start us, length us, event | category | flops | bytes accessed | tf_op | source)
XLA Modules:
  0.0 87.2 jit_solution(17982140349981152601)
XLA Ops:
  0.6 0.0 copy-start
  0.6 2.1 %collective-permute-start = (bf16[608,256]{1,0:T(8,128)(2,1)}, bf16[608,256]{1,0:T(8,128)(2,1)S(1)}, u32[]{:S(2)}, u32[]{:S(2)}) collective-permute-start(bf16[608,256]{1,0:T(8,128)(2,1)} %bitcast.47), channel_id=1, source_target_pairs={{0,2},{1,9},{2,0},{3,11},{4,6},{5,13},{6,4},{7,15},{8,10},{9,1},{1... | collective-permute-start | bytes 933896 | tf_op jit(solution)/shard_map/ppermute | solution.py:36
  2.8 1.8 %collective-permute-start.1 = (bf16[608,256]{1,0:T(8,128)(2,1)}, bf16[608,256]{1,0:T(8,128)(2,1)S(1)}, u32[]{:S(2)}, u32[]{:S(2)}) collective-permute-start(bf16[608,256]{1,0:T(8,128)(2,1)} %bitcast.48), channel_id=1, source_target_pairs={{0,6},{1,25},{2,4},{3,27},{4,2},{5,29},{6,0},{7,31},{8,14},{9,17},... | collective-permute-start | bytes 933896 | tf_op jit(solution)/shard_map/ppermute | solution.py:36
  4.6 0.6 collective-permute-start.2
  5.2 0.7 bitcast_add_fusion
  5.9 0.2 convert_reduce_fusion
  6.1 0.8 add_add_fusion.2
  6.9 0.7 copy.15
  7.6 0.7 copy-done.3
  8.3 2.6 %shard_map.94 = (s32[32,128]{1,0:T(8,128)S(1)}, f32[32,768]{1,0:T(8,128)S(1)}) custom-call(s32[1]{0:T(128)} %bitcast.me_ref, s32[31,128]{1,0:T(8,128)S(1)} %bitcast.52, s32[32,128]{1,0:T(8,128)S(1)} %bitcast.51), custom_call_target="tpu_custom_call" | custom-call | flops 33554432 | bytes 131072 | tf_op jit(solution)/shard_map/pallas_call | solution.py:96
  11.0 1.8 %fusion.2 = bf16[2048,256]{1,0:T(8,128)(2,1)} fusion(s32[512]{0:T(512)S(1)} %multiply_add_fusion, bf16[1,512,256]{2,1,0:T(8,128)(2,1)S(1)} %copy-done), kind=kOutput, calls=%fused_computation.6 | convolution fusion | flops 538443776 | bytes 1312768 | tf_op jit(solution)/shard_map/dot_general | solution.py:267
  12.9 0.7 collective-permute-done.1
  13.6 0.1 pad_maximum_fusion.1.refs_2_
  13.6 2.7 %collective-permute-start.6 = (bf16[2,608,256]{2,1,0:T(8,128)(2,1)S(1)}, bf16[2,608,256]{2,1,0:T(8,128)(2,1)S(1)}, u32[]{:S(2)}, u32[]{:S(2)}) collective-permute-start(bf16[2,608,256]{2,1,0:T(8,128)(2,1)S(1)} %pad_maximum_fusion.1.refs_2_), channel_id=1, source_target_pairs={{0,1},{1,0},{2,3},{3,2},{4,5},{5,4},{6,7},{7,6},{8,9},{9,8},{10,11... | collective-permute-start | bytes 1867784 | tf_op jit(solution)/shard_map/ppermute | solution.py:36
  16.3 0.1 pad_maximum_fusion.refs_0_
  16.4 1.7 %collective-permute-start.5 = (bf16[2,608,256]{2,1,0:T(8,128)(2,1)S(1)}, bf16[2,608,256]{2,1,0:T(8,128)(2,1)S(1)}, u32[]{:S(2)}, u32[]{:S(2)}) collective-permute-start(bf16[2,608,256]{2,1,0:T(8,128)(2,1)S(1)} %pad_maximum_fusion.refs_0_), channel_id=1, source_target_pairs={{0,1},{1,0},{2,3},{3,2},{4,5},{5,4},{6,7},{7,6},{8,9},{9,8},{10,11... | collective-permute-start | bytes 1867784 | tf_op jit(solution)/shard_map/ppermute | solution.py:36
  18.0 1.9 %collective-permute-start.3 = (bf16[2,608,256]{2,1,0:T(8,128)(2,1)S(1)}, bf16[2,608,256]{2,1,0:T(8,128)(2,1)}, u32[]{:S(2)}, u32[]{:S(2)}) collective-permute-start(bf16[2,608,256]{2,1,0:T(8,128)(2,1)S(1)} %pad_maximum_fusion.refs_0_), channel_id=1, source_target_pairs={{0,24},{1,7},{2,26},{3,5},{4,28},{5,3},{6,30},{7,1},{8,16},{9,15},... | collective-permute-start | bytes 1867784 | tf_op jit(solution)/shard_map/ppermute | solution.py:36
  19.9 1.4 %select_reduce_fusion.1 = s32[128]{0:T(128)S(1)} fusion(s32[32,128]{1,0:T(8,128)S(1)} %add_add_fusion.2, s32[128]{0:T(128)S(1)} %iota_add_fusion, s32[32,128]{1,0:T(8,128)S(1)} %get-tuple-element.38), kind=kLoop, calls=%fused_computation.8 | loop fusion | flops 1572736 | bytes 33792 | tf_op jit(solution)/shard_map/reduce_sum | solution.py:269
  21.3 0.9 %fusion.15 = f32[128,256]{1,0:T(8,128)} fusion(bf16[1,512,256]{2,1,0:T(8,128)(2,1)S(1)} %copy-done, s32[512]{0:T(512)S(1)} %get-tuple-element.63, s32[128]{0:T(128)S(1)} %broadcast_add_fusion.4), kind=kOutput, calls=%fused_computation.29 | convolution fusion | flops 33619968 | bytes 395776 | tf_op jit(solution)/shard_map/dot_general | solution.py:273
  22.2 6.2 %shard_map.95.refs_4_ = f32[1216,256]{1,0:T(8,128)S(1)} custom-call(s32[1]{0:T(128)} %bitcast.me_ref, bf16[608,19456]{1,0:T(8,128)(2,1)} %bitcast.53, f32[32,768]{1,0:T(8,128)S(1)} %get-tuple-element.33.keep_ref, bf16[2,608,256]{2,1,0:T(8,128)(2,1)S(1)} %pad_maximum_fusion.refs_0_, bf16[2,608,256]{2,1,0:T(8,128)(2,1)S(1)} %collective-permute-done.5.refs_1_, ...), custom_call_target="tpu_custom_call" | custom-call | flops 956301312 | bytes 1867776 | tf_op jit(solution)/shard_map/pallas_call | solution.py:179
  28.5 0.2 collective-permute-done.3.refs_0_
  28.7 0.9 %collective-permute-start.11 = (bf16[2,608,256]{2,1,0:T(8,128)(2,1)}, bf16[2,608,256]{2,1,0:T(8,128)(2,1)S(1)}, u32[]{:S(2)}, u32[]{:S(2)}) collective-permute-start(bf16[2,608,256]{2,1,0:T(8,128)(2,1)} %collective-permute-done.3.refs_0_), channel_id=1, source_target_pairs={{0,1},{1,0},{2,3},{3,2},{4,5},{5,4},{6,7},{7,6},{8,9},{9,8},{10,11... | collective-permute-start | bytes 1867784 | tf_op jit(solution)/shard_map/ppermute | solution.py:36
  29.7 1.9 %collective-permute-start.10 = (bf16[2,608,256]{2,1,0:T(8,128)(2,1)}, bf16[2,608,256]{2,1,0:T(8,128)(2,1)}, u32[]{:S(2)}, u32[]{:S(2)}) collective-permute-start(bf16[2,608,256]{2,1,0:T(8,128)(2,1)} %collective-permute-done.4.refs_2_), channel_id=1, source_target_pairs={{0,24},{1,7},{2,26},{3,5},{4,28},{5,3},{6,30},{7,1},{8,16},{9,15},... | collective-permute-start | bytes 1867784 | tf_op jit(solution)/shard_map/ppermute | solution.py:36
  31.6 0.8 collective-permute-start.8
  32.4 0.9 collective-permute-start.9
  33.2 6.4 %shard_map.96.refs_4_ = f32[1216,256]{1,0:T(8,128)S(1)} custom-call(s32[1]{0:T(128)} %bitcast.me_ref, bf16[608,19456]{1,0:T(8,128)(2,1)} %bitcast.54, f32[32,768]{1,0:T(8,128)S(1)} %get-tuple-element.33.keep_ref, bf16[2,608,256]{2,1,0:T(8,128)(2,1)} %collective-permute-done.3.refs_0_, ...), custom_call_target="tpu_custom_call", output_to_operand_aliasing={{}: (7, {})} | custom-call | flops 956301312 | bytes 1867776 | tf_op jit(solution)/shard_map/pallas_call | solution.py:179
  39.6 7.6 %all-to-all-start = ((bf16[32,64,256]{2,1,0:T(8,128)(2,1)}), bf16[32,64,256]{2,1,0:T(8,128)(2,1)}, u32[]{:S(2)}, u32[]{:S(2)}) async-start(bf16[32,64,256]{2,1,0:T(8,128)(2,1)} %bitcast.58), calls=%async_computation | async-start | bytes 2097152 | tf_op jit(solution)/shard_map/all_to_all | solution.py:293
  47.2 0.0 collective-permute-done.8.refs_2_
  47.2 0.5 collective-permute-done.9.refs_0_
  47.7 1.6 %collective-permute-start.15 = (bf16[2,608,256]{2,1,0:T(8,128)(2,1)}, bf16[2,608,256]{2,1,0:T(8,128)(2,1)S(1)}, u32[]{:S(2)}, u32[]{:S(2)}) collective-permute-start(bf16[2,608,256]{2,1,0:T(8,128)(2,1)} %collective-permute-done.7.refs_0_), channel_id=1, source_target_pairs={{0,1},{1,0},{2,3},{3,2},{4,5},{5,4},{6,7},{7,6},{8,9},{9,8},{10,11... | collective-permute-start | bytes 1867784 | tf_op jit(solution)/shard_map/ppermute | solution.py:36
  49.3 0.5 collective-permute-start.13
  49.8 0.1 collective-permute-start.14
  49.9 0.8 fusion.34
  50.7 0.7 fusion.36
  51.3 0.1 select_reduce_fusion.2
  51.4 0.6 collective-permute-done.16.refs_3_
  52.1 6.4 %shard_map.97.refs_4_ = f32[1216,256]{1,0:T(8,128)S(1)} custom-call(s32[1]{0:T(128)} %bitcast.me_ref, bf16[608,19456]{1,0:T(8,128)(2,1)} %bitcast.55, f32[32,768]{1,0:T(8,128)S(1)} %get-tuple-element.33.keep_ref, bf16[2,608,256]{2,1,0:T(8,128)(2,1)} %collective-permute-done.7.refs_0_, ...), custom_call_target="tpu_custom_call", output_to_operand_aliasing={{}: (7, {})} | custom-call | flops 956301312 | bytes 1867776 | tf_op jit(solution)/shard_map/pallas_call | solution.py:179
  58.4 0.0 copy-start.4
  58.5 6.4 %shard_map.98 = f32[1216,256]{1,0:T(8,128)S(1)} custom-call(s32[1]{0:T(128)} %bitcast.me_ref, bf16[608,19456]{1,0:T(8,128)(2,1)} %bitcast.56, f32[32,768]{1,0:T(8,128)S(1)} %get-tuple-element.33.keep_ref, bf16[2,608,256]{2,1,0:T(8,128)(2,1)} %collective-permute-done.9.refs_0_, ...), custom_call_target="tpu_custom_call", output_to_operand_aliasing={{}: (7, {})} | custom-call | flops 956301312 | bytes 1867776 | tf_op jit(solution)/shard_map/pallas_call | solution.py:179
  64.9 0.4 fusion.12
  65.4 0.5 collective-permute-start.17
  65.9 0.9 %collective-permute-done.17 = f32[64,256]{1,0:T(8,128)S(1)} collective-permute-done((f32[64,256]{1,0:T(8,128)S(1)}, f32[64,256]{1,0:T(8,128)S(1)}, u32[]{:S(2)}, u32[]{:S(2)}) %collective-permute-start.17) | collective-permute-done | bytes 65568 | tf_op jit(solution)/shard_map/ppermute | solution.py:36
  66.8 1.0 %collective-permute-start.18 = (f32[64,256]{1,0:T(8,128)S(1)}, f32[64,256]{1,0:T(8,128)S(1)}, u32[]{:S(2)}, u32[]{:S(2)}) collective-permute-start(f32[64,256]{1,0:T(8,128)S(1)} %select_add_fusion), channel_id=1, source_target_pairs={{0,2},{1,3},{2,0},{3,1},{4,6},{5,7},{6,4},{7,5},{8,10},{9,11},{10,... | collective-permute-start | bytes 196616 | tf_op jit(solution)/shard_map/ppermute | solution.py:36
  67.8 1.9 %collective-permute-start.19 = (f32[64,256]{1,0:T(8,128)S(1)}, f32[64,256]{1,0:T(8,128)S(1)}, u32[]{:S(2)}, u32[]{:S(2)}) collective-permute-start(f32[64,256]{1,0:T(8,128)S(1)} %select_add_fusion), channel_id=1, source_target_pairs={{0,6},{1,7},{2,4},{3,5},{4,2},{5,3},{6,0},{7,1},{8,14},{9,15},{10,... | collective-permute-start | bytes 196616 | tf_op jit(solution)/shard_map/ppermute | solution.py:36
  69.7 0.4 collective-permute-start.20
  70.1 0.1 fusion.23
  70.3 0.3 fusion.6
  70.5 0.6 select_reduce_fusion
  71.2 0.1 sub.45
  71.3 2.1 %fusion = f32[608,256]{1,0:T(8,128)S(1)} fusion(bf16[2048,256]{1,0:T(8,128)(2,1)} %bitcast.14, s32[2048]{0:T(1024)S(1)} %sub.45), kind=kOutput, calls=%fused_computation.1 | convolution fusion | flops 638779392 | bytes 1679360 | tf_op jit(solution)/shard_map/dot_general | solution.py:326
  73.4 0.9 %collective-permute-done.20 = f32[64,256]{1,0:T(8,128)S(1)} collective-permute-done((f32[64,256]{1,0:T(8,128)S(1)}, f32[64,256]{1,0:T(8,128)S(1)}, u32[]{:S(2)}, u32[]{:S(2)}) %collective-permute-start.20) | collective-permute-done | bytes 65568 | tf_op jit(solution)/shard_map/ppermute | solution.py:36
  74.3 0.1 collective-permute-start.22
  74.4 1.7 %collective-permute-start.23 = (f32[64,256]{1,0:T(8,128)S(1)}, f32[64,256]{1,0:T(8,128)S(1)}, u32[]{:S(2)}, u32[]{:S(2)}) collective-permute-start(f32[64,256]{1,0:T(8,128)S(1)} %add_add_fusion.1), channel_id=1, source_target_pairs={{0,24},{1,25},{2,26},{3,27},{4,28},{5,29},{6,30},{7,31},{8,16},{9,... | collective-permute-start | bytes 196616 | tf_op jit(solution)/shard_map/ppermute | solution.py:36
  76.1 1.5 %collective-permute-start.24 = (f32[64,256]{1,0:T(8,128)S(1)}, f32[64,256]{1,0:T(8,128)S(1)}, u32[]{:S(2)}, u32[]{:S(2)}) collective-permute-start(f32[64,256]{1,0:T(8,128)S(1)} %add_add_fusion.1), channel_id=1, source_target_pairs={{0,16},{1,17},{2,18},{3,19},{4,20},{5,21},{6,22},{7,23},{8,24},{9,... | collective-permute-start | bytes 196616 | tf_op jit(solution)/shard_map/ppermute | solution.py:36
  77.7 0.8 convert_bitcast_fusion
  78.5 2.5 %shard_map.99 = f32[608,256]{1,0:T(8,128)S(1)} custom-call(s32[1]{0:T(128)} %bitcast.me_ref, bf16[608,19456]{1,0:T(8,128)(2,1)} %bitcast.57, bf16[608,256]{1,0:T(8,128)(2,1)S(1)} %bitcast.50, bf16[608,256]{1,0:T(8,128)(2,1)S(1)} %slice_bitcast_fusion.yours_ref, s32[1,128]{1,0:T(1,128)S(1)} %get-tuple-element.67.names_ref), custom_call_target="tpu_custom_call" | custom-call | flops 478150656 | bytes 1867776 | tf_op jit(solution)/shard_map/pallas_call | solution.py:228
  81.0 0.3 collective-permute-done.24
  81.3 3.3 %collective-permute-start.25 = (f32[64,256]{1,0:T(8,128)S(1)}, f32[64,256]{1,0:T(8,128)S(1)}, u32[]{:S(2)}, u32[]{:S(2)}) collective-permute-start(f32[64,256]{1,0:T(8,128)S(1)} %add_add_fusion), channel_id=1, source_target_pairs={{0,1},{1,0},{2,3},{3,2},{4,5},{5,4},{6,7},{7,6},{8,9},{9,8},{10,11... | collective-permute-start | bytes 196616 | tf_op jit(solution)/shard_map/ppermute | solution.py:36
  84.6 0.5 fusion.8
  85.1 0.1 collective-permute-start.21
  85.2 0.3 collective-permute-done.25
  85.5 0.7 maximum_bitcast_fusion
  86.2 0.3 collective-permute-done.21
  86.5 0.7 add_bitcast_fusion
  (48 shorter events, 0.2 us)
Async XLA Ops:
  0.6 10.4 %copy-start = (bf16[1,512,256]{2,1,0:T(8,128)(2,1)S(1)}, bf16[1,512,256]{2,1,0:T(8,128)(2,1)}, u32[]{:S(2)}) copy-start(bf16[1,512,256]{2,1,0:T(8,128)(2,1)} %param.9) | copy-start | bytes 786436
  0.6 12.2 %collective-permute-start = (bf16[608,256]{1,0:T(8,128)(2,1)}, bf16[608,256]{1,0:T(8,128)(2,1)S(1)}, u32[]{:S(2)}, u32[]{:S(2)}) collective-permute-start(bf16[608,256]{1,0:T(8,128)(2,1)} %bitcast.47), channel_id=1, source_target_pairs={{0,2},{1,9},{2,0},{3,11},{4,6},{5,13},{6,4},{7,15},{8,10},{9,1},{1... | collective-permute-start | bytes 933896 | tf_op jit(solution)/shard_map/ppermute | solution.py:36
  2.8 10.8 %collective-permute-start.1 = (bf16[608,256]{1,0:T(8,128)(2,1)}, bf16[608,256]{1,0:T(8,128)(2,1)S(1)}, u32[]{:S(2)}, u32[]{:S(2)}) collective-permute-start(bf16[608,256]{1,0:T(8,128)(2,1)} %bitcast.48), channel_id=1, source_target_pairs={{0,6},{1,25},{2,4},{3,27},{4,2},{5,29},{6,0},{7,31},{8,14},{9,17},... | collective-permute-start | bytes 933896 | tf_op jit(solution)/shard_map/ppermute | solution.py:36
  4.6 9.0 %collective-permute-start.2 = (bf16[608,256]{1,0:T(8,128)(2,1)}, bf16[608,256]{1,0:T(8,128)(2,1)S(1)}, u32[]{:S(2)}, u32[]{:S(2)}) collective-permute-start(bf16[608,256]{1,0:T(8,128)(2,1)} %bitcast.49), channel_id=1, source_target_pairs={{0,4},{1,17},{2,6},{3,19},{4,0},{5,21},{6,2},{7,23},{8,12},{9,25},... | collective-permute-start | bytes 933896 | tf_op jit(solution)/shard_map/ppermute | solution.py:36
  7.6 0.7 copy-start.3
  11.0 5.3 %copy-start.1 = (bf16[1,608,256]{2,1,0:T(8,128)(2,1)S(1)}, bf16[1,608,256]{2,1,0:T(8,128)(2,1)}, u32[]{:S(2)}) copy-start(bf16[1,608,256]{2,1,0:T(8,128)(2,1)} %param.8) | copy-start | bytes 933892
  13.6 8.6 %collective-permute-start.6 = (bf16[2,608,256]{2,1,0:T(8,128)(2,1)S(1)}, bf16[2,608,256]{2,1,0:T(8,128)(2,1)S(1)}, u32[]{:S(2)}, u32[]{:S(2)}) collective-permute-start(bf16[2,608,256]{2,1,0:T(8,128)(2,1)S(1)} %pad_maximum_fusion.1.refs_2_), channel_id=1, source_target_pairs={{0,1},{1,0},{2,3},{3,2},{4,5},{5,4},{6,7},{7,6},{8,9},{9,8},{10,11... | collective-permute-start | bytes 1867784 | tf_op jit(solution)/shard_map/ppermute | solution.py:36
  16.3 12.2 %collective-permute-start.4 = (bf16[2,608,256]{2,1,0:T(8,128)(2,1)S(1)}, bf16[2,608,256]{2,1,0:T(8,128)(2,1)}, u32[]{:S(2)}, u32[]{:S(2)}) collective-permute-start(bf16[2,608,256]{2,1,0:T(8,128)(2,1)S(1)} %pad_maximum_fusion.1.refs_2_), channel_id=1, source_target_pairs={{0,8},{1,3},{2,10},{3,1},{4,12},{5,7},{6,14},{7,5},{8,0},{9,11},{1... | collective-permute-start | bytes 1867784 | tf_op jit(solution)/shard_map/ppermute | solution.py:36
  16.4 5.9 %collective-permute-start.5 = (bf16[2,608,256]{2,1,0:T(8,128)(2,1)S(1)}, bf16[2,608,256]{2,1,0:T(8,128)(2,1)S(1)}, u32[]{:S(2)}, u32[]{:S(2)}) collective-permute-start(bf16[2,608,256]{2,1,0:T(8,128)(2,1)S(1)} %pad_maximum_fusion.refs_0_), channel_id=1, source_target_pairs={{0,1},{1,0},{2,3},{3,2},{4,5},{5,4},{6,7},{7,6},{8,9},{9,8},{10,11... | collective-permute-start | bytes 1867784 | tf_op jit(solution)/shard_map/ppermute | solution.py:36
  18.0 10.7 %collective-permute-start.3 = (bf16[2,608,256]{2,1,0:T(8,128)(2,1)S(1)}, bf16[2,608,256]{2,1,0:T(8,128)(2,1)}, u32[]{:S(2)}, u32[]{:S(2)}) collective-permute-start(bf16[2,608,256]{2,1,0:T(8,128)(2,1)S(1)} %pad_maximum_fusion.refs_0_), channel_id=1, source_target_pairs={{0,24},{1,7},{2,26},{3,5},{4,28},{5,3},{6,30},{7,1},{8,16},{9,15},... | collective-permute-start | bytes 1867784 | tf_op jit(solution)/shard_map/ppermute | solution.py:36
  28.7 3.6 %collective-permute-start.11 = (bf16[2,608,256]{2,1,0:T(8,128)(2,1)}, bf16[2,608,256]{2,1,0:T(8,128)(2,1)S(1)}, u32[]{:S(2)}, u32[]{:S(2)}) collective-permute-start(bf16[2,608,256]{2,1,0:T(8,128)(2,1)} %collective-permute-done.3.refs_0_), channel_id=1, source_target_pairs={{0,1},{1,0},{2,3},{3,2},{4,5},{5,4},{6,7},{7,6},{8,9},{9,8},{10,11... | collective-permute-start | bytes 1867784 | tf_op jit(solution)/shard_map/ppermute | solution.py:36
  29.7 3.5 %collective-permute-start.12 = (bf16[2,608,256]{2,1,0:T(8,128)(2,1)}, bf16[2,608,256]{2,1,0:T(8,128)(2,1)S(1)}, u32[]{:S(2)}, u32[]{:S(2)}) collective-permute-start(bf16[2,608,256]{2,1,0:T(8,128)(2,1)} %collective-permute-done.4.refs_2_), channel_id=1, source_target_pairs={{0,1},{1,0},{2,3},{3,2},{4,5},{5,4},{6,7},{7,6},{8,9},{9,8},{10,11... | collective-permute-start | bytes 1867784 | tf_op jit(solution)/shard_map/ppermute | solution.py:36
  29.7 17.5 %collective-permute-start.10 = (bf16[2,608,256]{2,1,0:T(8,128)(2,1)}, bf16[2,608,256]{2,1,0:T(8,128)(2,1)}, u32[]{:S(2)}, u32[]{:S(2)}) collective-permute-start(bf16[2,608,256]{2,1,0:T(8,128)(2,1)} %collective-permute-done.4.refs_2_), channel_id=1, source_target_pairs={{0,24},{1,7},{2,26},{3,5},{4,28},{5,3},{6,30},{7,1},{8,16},{9,15},... | collective-permute-start | bytes 1867784 | tf_op jit(solution)/shard_map/ppermute | solution.py:36
  31.6 15.6 %collective-permute-start.7 = (bf16[2,608,256]{2,1,0:T(8,128)(2,1)S(1)}, bf16[2,608,256]{2,1,0:T(8,128)(2,1)}, u32[]{:S(2)}, u32[]{:S(2)}) collective-permute-start(bf16[2,608,256]{2,1,0:T(8,128)(2,1)S(1)} %pad_maximum_fusion.refs_0_), channel_id=1, source_target_pairs={{0,8},{1,3},{2,10},{3,1},{4,12},{5,7},{6,14},{7,5},{8,0},{9,11},{1... | collective-permute-start | bytes 1867784 | tf_op jit(solution)/shard_map/ppermute | solution.py:36
  31.6 15.7 %collective-permute-start.8 = (bf16[2,608,256]{2,1,0:T(8,128)(2,1)S(1)}, bf16[2,608,256]{2,1,0:T(8,128)(2,1)}, u32[]{:S(2)}, u32[]{:S(2)}) collective-permute-start(bf16[2,608,256]{2,1,0:T(8,128)(2,1)S(1)} %pad_maximum_fusion.1.refs_2_), channel_id=1, source_target_pairs={{0,24},{1,7},{2,26},{3,5},{4,28},{5,3},{6,30},{7,1},{8,16},{9,15},... | collective-permute-start | bytes 1867784 | tf_op jit(solution)/shard_map/ppermute | solution.py:36
  32.4 15.4 %collective-permute-start.9 = (bf16[2,608,256]{2,1,0:T(8,128)(2,1)}, bf16[2,608,256]{2,1,0:T(8,128)(2,1)}, u32[]{:S(2)}, u32[]{:S(2)}) collective-permute-start(bf16[2,608,256]{2,1,0:T(8,128)(2,1)} %collective-permute-done.3.refs_0_), channel_id=1, source_target_pairs={{0,8},{1,3},{2,10},{3,1},{4,12},{5,7},{6,14},{7,5},{8,0},{9,11},{1... | collective-permute-start | bytes 1867784 | tf_op jit(solution)/shard_map/ppermute | solution.py:36
  39.6 25.3 %all-to-all-start = ((bf16[32,64,256]{2,1,0:T(8,128)(2,1)}), bf16[32,64,256]{2,1,0:T(8,128)(2,1)}, u32[]{:S(2)}, u32[]{:S(2)}) async-start(bf16[32,64,256]{2,1,0:T(8,128)(2,1)} %bitcast.58), calls=%async_computation | async-start | bytes 2097152 | tf_op jit(solution)/shard_map/all_to_all | solution.py:293
  47.7 3.7 %collective-permute-start.15 = (bf16[2,608,256]{2,1,0:T(8,128)(2,1)}, bf16[2,608,256]{2,1,0:T(8,128)(2,1)S(1)}, u32[]{:S(2)}, u32[]{:S(2)}) collective-permute-start(bf16[2,608,256]{2,1,0:T(8,128)(2,1)} %collective-permute-done.7.refs_0_), channel_id=1, source_target_pairs={{0,1},{1,0},{2,3},{3,2},{4,5},{5,4},{6,7},{7,6},{8,9},{9,8},{10,11... | collective-permute-start | bytes 1867784 | tf_op jit(solution)/shard_map/ppermute | solution.py:36
  49.3 2.8 %collective-permute-start.16 = (bf16[2,608,256]{2,1,0:T(8,128)(2,1)}, bf16[2,608,256]{2,1,0:T(8,128)(2,1)S(1)}, u32[]{:S(2)}, u32[]{:S(2)}) collective-permute-start(bf16[2,608,256]{2,1,0:T(8,128)(2,1)} %collective-permute-done.8.refs_2_), channel_id=1, source_target_pairs={{0,1},{1,0},{2,3},{3,2},{4,5},{5,4},{6,7},{7,6},{8,9},{9,8},{10,11... | collective-permute-start | bytes 1867784 | tf_op jit(solution)/shard_map/ppermute | solution.py:36
  49.3 9.2 %collective-permute-start.13 = (bf16[2,608,256]{2,1,0:T(8,128)(2,1)}, bf16[2,608,256]{2,1,0:T(8,128)(2,1)S(1)}, u32[]{:S(2)}, u32[]{:S(2)}) collective-permute-start(bf16[2,608,256]{2,1,0:T(8,128)(2,1)} %collective-permute-done.9.refs_0_), channel_id=1, source_target_pairs={{0,1},{1,0},{2,3},{3,2},{4,5},{5,4},{6,7},{7,6},{8,9},{9,8},{10,11... | collective-permute-start | bytes 1867784 | tf_op jit(solution)/shard_map/ppermute | solution.py:36
  49.8 8.7 %collective-permute-start.14 = (bf16[2,608,256]{2,1,0:T(8,128)(2,1)}, bf16[2,608,256]{2,1,0:T(8,128)(2,1)S(1)}, u32[]{:S(2)}, u32[]{:S(2)}) collective-permute-start(bf16[2,608,256]{2,1,0:T(8,128)(2,1)} %collective-permute-done.10.refs_2_), channel_id=1, source_target_pairs={{0,1},{1,0},{2,3},{3,2},{4,5},{5,4},{6,7},{7,6},{8,9},{9,8},{10,11... | collective-permute-start | bytes 1867784 | tf_op jit(solution)/shard_map/ppermute | solution.py:36
  58.4 6.5 %copy-start.4 = (f32[128,256]{1,0:T(8,128)S(1)}, f32[128,256]{1,0:T(8,128)}, u32[]{:S(2)}) copy-start(f32[128,256]{1,0:T(8,128)} %fusion.15) | copy-start | bytes 393220
  58.4 11.6 %copy-start.5 = (s32[1,16384,1]{1,2,0:T(1,128)S(1)}, s32[1,16384,1]{1,2,0:T(1,128)}, u32[]{:S(2)}) copy-start(s32[1,16384,1]{1,2,0:T(1,128)} %param.10) | copy-start | bytes 196612
  64.9 5.4 %copy-start.6 = (s32[1,16384]{1,0:T(1,128)S(1)}, s32[1,16384]{1,0:T(1,128)}, u32[]{:S(2)}) copy-start(s32[1,16384]{1,0:T(1,128)} %param.11) | copy-start | bytes 196612
  65.4 1.4 %collective-permute-start.17 = (f32[64,256]{1,0:T(8,128)S(1)}, f32[64,256]{1,0:T(8,128)S(1)}, u32[]{:S(2)}, u32[]{:S(2)}) collective-permute-start(f32[64,256]{1,0:T(8,128)S(1)} %slice_select_fusion), channel_id=1, source_target_pairs={{0,1},{1,0},{2,3},{3,2},{4,5},{5,4},{6,7},{7,6},{8,9},{9,8},{10,11... | collective-permute-start | bytes 196616 | tf_op jit(solution)/shard_map/ppermute | solution.py:36
  66.8 6.6 %collective-permute-start.18 = (f32[64,256]{1,0:T(8,128)S(1)}, f32[64,256]{1,0:T(8,128)S(1)}, u32[]{:S(2)}, u32[]{:S(2)}) collective-permute-start(f32[64,256]{1,0:T(8,128)S(1)} %select_add_fusion), channel_id=1, source_target_pairs={{0,2},{1,3},{2,0},{3,1},{4,6},{5,7},{6,4},{7,5},{8,10},{9,11},{10,... | collective-permute-start | bytes 196616 | tf_op jit(solution)/shard_map/ppermute | solution.py:36
  67.8 5.6 %collective-permute-start.19 = (f32[64,256]{1,0:T(8,128)S(1)}, f32[64,256]{1,0:T(8,128)S(1)}, u32[]{:S(2)}, u32[]{:S(2)}) collective-permute-start(f32[64,256]{1,0:T(8,128)S(1)} %select_add_fusion), channel_id=1, source_target_pairs={{0,6},{1,7},{2,4},{3,5},{4,2},{5,3},{6,0},{7,1},{8,14},{9,15},{10,... | collective-permute-start | bytes 196616 | tf_op jit(solution)/shard_map/ppermute | solution.py:36
  69.7 4.6 %collective-permute-start.20 = (f32[64,256]{1,0:T(8,128)S(1)}, f32[64,256]{1,0:T(8,128)S(1)}, u32[]{:S(2)}, u32[]{:S(2)}) collective-permute-start(f32[64,256]{1,0:T(8,128)S(1)} %select_add_fusion), channel_id=1, source_target_pairs={{0,4},{1,5},{2,6},{3,7},{4,0},{5,1},{6,2},{7,3},{8,12},{9,13},{10,... | collective-permute-start | bytes 196616 | tf_op jit(solution)/shard_map/ppermute | solution.py:36
  73.4 5.1 %copy-start.2 = (bf16[1,608,256]{2,1,0:T(8,128)(2,1)S(1)}, bf16[1,608,256]{2,1,0:T(8,128)(2,1)}, u32[]{:S(2)}) copy-start(bf16[1,608,256]{2,1,0:T(8,128)(2,1)} %param.8) | copy-start | bytes 933892
  74.3 6.7 %collective-permute-start.22 = (f32[64,256]{1,0:T(8,128)S(1)}, f32[64,256]{1,0:T(8,128)S(1)}, u32[]{:S(2)}, u32[]{:S(2)}) collective-permute-start(f32[64,256]{1,0:T(8,128)S(1)} %add_add_fusion.1), channel_id=1, source_target_pairs={{0,8},{1,9},{2,10},{3,11},{4,12},{5,13},{6,14},{7,15},{8,0},{9,1},... | collective-permute-start | bytes 196616 | tf_op jit(solution)/shard_map/ppermute | solution.py:36
  74.4 6.6 %collective-permute-start.23 = (f32[64,256]{1,0:T(8,128)S(1)}, f32[64,256]{1,0:T(8,128)S(1)}, u32[]{:S(2)}, u32[]{:S(2)}) collective-permute-start(f32[64,256]{1,0:T(8,128)S(1)} %add_add_fusion.1), channel_id=1, source_target_pairs={{0,24},{1,25},{2,26},{3,27},{4,28},{5,29},{6,30},{7,31},{8,16},{9,... | collective-permute-start | bytes 196616 | tf_op jit(solution)/shard_map/ppermute | solution.py:36
  76.1 5.2 %collective-permute-start.24 = (f32[64,256]{1,0:T(8,128)S(1)}, f32[64,256]{1,0:T(8,128)S(1)}, u32[]{:S(2)}, u32[]{:S(2)}) collective-permute-start(f32[64,256]{1,0:T(8,128)S(1)} %add_add_fusion.1), channel_id=1, source_target_pairs={{0,16},{1,17},{2,18},{3,19},{4,20},{5,21},{6,22},{7,23},{8,24},{9,... | collective-permute-start | bytes 196616 | tf_op jit(solution)/shard_map/ppermute | solution.py:36
  81.3 4.2 %collective-permute-start.25 = (f32[64,256]{1,0:T(8,128)S(1)}, f32[64,256]{1,0:T(8,128)S(1)}, u32[]{:S(2)}, u32[]{:S(2)}) collective-permute-start(f32[64,256]{1,0:T(8,128)S(1)} %add_add_fusion), channel_id=1, source_target_pairs={{0,1},{1,0},{2,3},{3,2},{4,5},{5,4},{6,7},{7,6},{8,9},{9,8},{10,11... | collective-permute-start | bytes 196616 | tf_op jit(solution)/shard_map/ppermute | solution.py:36
  85.1 1.4 %collective-permute-start.21 = (f32[128,256]{1,0:T(8,128)S(1)}, f32[128,256]{1,0:T(8,128)S(1)}, u32[]{:S(2)}, u32[]{:S(2)}) collective-permute-start(f32[128,256]{1,0:T(8,128)S(1)} %fusion.8), channel_id=1, source_target_pairs={{0,1},{1,0},{2,3},{3,2},{4,5},{5,4},{6,7},{7,6},{8,9},{9,8},{10,11... | collective-permute-start | bytes 393224 | tf_op jit(solution)/shard_map/ppermute | solution.py:36
